TPU v7x, 32 devices: a whole 2x2x4 slice. The times are simulated.
32 devices in a mesh: dom: 16 (over z, x, core), lag: 2 (over y).
Axes of the slice: x: 2, y: 2, z: 4, core: 2. Of those that a mesh axis runs over, the one named last changes fastest.
Arguments:
- delayed_crowd_history: bfloat16 [2, 64, 512, 128], P('lag', None, 'dom'), may hold values from -6 to 6
- predicted_crowd_array: bfloat16 [64, 512, 128], P('lag', 'dom'), may hold values from -40 to 40
- probe_target_spot: int32 [256, 256], P('dom'), may hold values from 0 to 255
- alive_probe_places: int32 [256], P('dom'), may hold values from 64 to 256, as said below
- probed_heat_levels: float32 [256, 256], P('dom'), may hold values from -6 to 6
- probe_reciprocal_spread: float32 [256, 256], P('dom'), may hold values from 0.1 to 1.6
- decay_extent_squares: int32 [256], P('dom'), may hold values from 16 to 32
Outputs:
- smoothed: bfloat16 [2, 64, 512, 128], P('lag', None, 'dom')
Inputs may be any that keep to these rules, and one draw needn't show every extreme that they name: `alive_probe_places`: live observations of a patch occupy its first slots.
All inputs are finite; a program needn't handle non-finite values.
Results may differ from a plain program's by a relative error of at most 0.0062.
Values may be sent and summed in bfloat16 or wider, within the bound.
No kernel may reach another device: no remote copies, remote signals or barrier semaphores. Data moves between devices by JAX's collectives and lax.ppermute only.
A program may use at most 64 MiB of HBM per device.

v0:
```python
import functools

import jax
import jax.numpy as jnp
from jax import lax
from jax.experimental import pallas as pl
from jax.experimental.pallas import tpu as pltpu
from jax.sharding import PartitionSpec as P

PATCH = 16
NS_STEPS = 4
RADIUS = 32
FAR = RADIUS - PATCH // 2
NEAR = FAR - PATCH
MIDDLE = (PATCH - 1) / 2

NT = (((1,), (1,)), ((), ()))
NN = (((1,), (0,)), ((), ()))
f32 = jnp.float32
bf16 = jnp.bfloat16


def mm(a, b, dims=NN):
    return lax.dot_general(a, b, dims, preferred_element_type=f32)


def split(x):
    high = x.astype(bf16)
    return high, (x - high.astype(f32)).astype(bf16)


def fields_kernel(cols, table_ref, part_ref, field_ref, sum_ref):
    sum_ref[...] = jnp.sum(part_ref[...].astype(f32), axis=0)
    patches, slots = table_ref.shape[1:]
    patch_cols = cols // PATCH
    patch_rows = patches // patch_cols
    spot = table_ref[2].astype(jnp.int32)
    row_in = spot // PATCH
    col_in = spot % PATCH
    iota_row = lax.broadcasted_iota(jnp.int32, (PATCH, slots), 0)
    iota_col = lax.broadcasted_iota(jnp.int32, (cols, slots), 0)
    for a in range(patch_rows):
        total = jnp.zeros((4 * PATCH, cols), f32)
        for b in range(patch_cols):
            p = a * patch_cols + b
            prec = table_ref[0, p : p + 1, :]
            level = table_ref[1, p : p + 1, :]
            prec_high = prec.astype(bf16).astype(f32)
            level_high = level.astype(bf16).astype(f32)
            on_row = row_in[p : p + 1, :] == iota_row
            pieces = [
                jnp.where(on_row, piece, 0.0).astype(bf16)
                for piece in (prec_high, prec - prec_high, level_high, level - level_high)
            ]
            on_col = jnp.where(col_in[p : p + 1, :] + b * PATCH == iota_col, 1.0, 0.0).astype(bf16)
            total = total + mm(jnp.concatenate(pieces, 0), on_col, NT)
        rows = slice(a * PATCH, (a + 1) * PATCH)
        field_ref[0, rows, :] = total[:PATCH] + total[PATCH : 2 * PATCH]
        field_ref[1, rows, :] = total[2 * PATCH : 3 * PATCH] + total[3 * PATCH :]


def state_kernel(after_ref, hist_ref, lag_ref, mean_ref, flat_ref):
    members, tile_rows, cols = hist_ref.shape
    state = hist_ref[...].astype(f32)
    mean = jnp.sum(state, axis=0) / members
    mean_ref[...] = mean
    flat_ref[...] = (state - mean[None]).reshape(members * tile_rows, cols)
    for r in range(tile_rows):
        lag_ref[r] = flat_ref[pl.ds(r, members, stride=tile_rows), :].astype(bf16)


def half_of_lags():
    return lax.axis_index("lag") // (lax.axis_size("lag") // 2)


def ring(tiles, shares, turn):
    half = shares // 2
    pairs = []
    for t in range(tiles):
        for l in range(shares):
            target = t + (1 if (l // half) ^ turn else -1)
            if 0 <= target < tiles:
                pairs.append((t * shares + l, target * shares + l))
            else:
                pairs.append((t * shares + l, t * shares + (l + half) % shares))
    return pairs


def taper_plan(centre_row, inverse_square):
    q_row = lax.broadcasted_iota(jnp.int32, inverse_square.shape, 0)
    col = lax.broadcasted_iota(jnp.int32, inverse_square.shape, 1)
    col_square = jnp.square(col.astype(f32) - (q_row.astype(f32) * PATCH + MIDDLE))
    return centre_row, col_square, inverse_square


def accumulate(total, plan, anomalies, weight, innovation, first_row):
    centre_row, col_square, inverse_square = plan
    patches, cols = col_square.shape
    lefts = []
    for i, anomaly in enumerate(anomalies):
        members = anomaly.shape[0]
        offset = (first_row + i).astype(f32) - centre_row
        taper = jnp.square(jnp.maximum(0.0, 1.0 - (offset * offset + col_square) * inverse_square))
        scale = taper * weight[i : i + 1]
        blocks = anomaly.reshape(members // PATCH, PATCH, cols)
        left = [
            (blocks * jnp.broadcast_to(scale[q : q + 1], (PATCH, cols)).astype(bf16)[None]).reshape(members, cols)
            for q in range(patches)
        ]
        tail = taper * innovation[i : i + 1]
        left.append(jnp.concatenate([tail, jnp.zeros((PATCH - patches, cols), f32)], 0).astype(bf16))
        lefts.append(jnp.concatenate(left, 0))
    return total + mm(jnp.concatenate(lefts, 1), jnp.concatenate(anomalies, 1), NT)


STEP = 8


def paired(totals, members, patch_cols):
    pairs = patch_cols // 2
    grams, sides = [], []
    for total in totals:
        for pair in range(pairs):
            at = 2 * pair * members
            grams.append(jnp.concatenate([total[at : at + members], total[at + members : at + 2 * members]], 1))
        for pair in range(pairs):
            at = patch_cols * members + 2 * pair
            sides.append(jnp.concatenate([total[at : at + 1], total[at + 1 : at + 2]], 1))
    return jnp.concatenate(grams, 0), jnp.concatenate(sides, 0)


def message_of(grams, sides):
    return jnp.concatenate([grams.astype(bf16), *split(sides)], 0)


def read_message(ref, side_count):
    at = ref.shape[0] - 2 * side_count
    high, low = ref[at : at + side_count, :].astype(f32), ref[at + side_count :, :].astype(f32)
    return jnp.concatenate([ref[:at, :].astype(f32), high + low], 0)


def arrived(ref, turn, side_count):
    tile = lax.axis_index("dom")
    there = jnp.where(half_of_lags() ^ turn == 1, tile > 0, tile < lax.axis_size("dom") - 1)
    return jnp.where(there, read_message(ref, side_count), 0.0)


def outward(turn, rows_ref, held_ref, inverse_ref, message_ref, total_ref):
    tile_rows, members, cols = rows_ref.shape
    patch_cols = cols // PATCH
    down = half_of_lags() ^ turn
    near = pl.multiple_of(down * (tile_rows - NEAR), 8)
    middle = jnp.where(down == 0, MIDDLE - PATCH, MIDDLE + tile_rows)
    plans = [
        taper_plan(middle, inverse_ref[1 - down]),
        taper_plan(middle + jnp.where(down == 0, -PATCH, PATCH).astype(f32), inverse_ref[down]),
    ]
    anomalies = [rows_ref[near + i] for i in range(NEAR)]
    fields = [held_ref[k, pl.ds(near, NEAR), :] for k in range(2)]
    blank = jnp.zeros(total_ref.shape[1:], f32)
    totals = [accumulate(blank, plan, anomalies, *fields, near) for plan in plans]
    for start in range(NEAR, FAR, STEP):
        anomalies = [rows_ref[start + i] for i in range(STEP)]
        fields = [held_ref[k, start : start + STEP, :] for k in range(2)]
        totals[0] = accumulate(totals[0], plans[0], anomalies, *fields, jnp.int32(start))
    total_ref[1 - down] = totals[0]
    total_ref[down] = totals[1]
    message_ref[...] = message_of(*paired([total_ref[0], total_ref[1]], members, patch_cols))


def first_kernel(shares, *refs):
    parts, refs = refs[:shares], refs[shares:]
    sum_ref, field_ref, inverse_ref, rows_ref, held_ref, message_ref, flat_ref, total_ref = refs
    share_members, tile_rows, cols = parts[0].shape
    members = share_members * shares
    lag = lax.axis_index("lag")
    states = [part[...].astype(f32) for part in parts]
    mean = functools.reduce(jnp.add, [jnp.sum(state, axis=0) for state in states[1:]], sum_ref[...]) / members
    for k, state in enumerate(states):
        at = pl.multiple_of(lax.rem(lag + k, shares) * (share_members * tile_rows), 8)
        flat_ref[pl.ds(at, share_members * tile_rows), :] = (state - mean[None]).reshape(-1, cols)
    weight = field_ref[0]
    held_ref[0] = weight
    held_ref[1] = field_ref[1] - mean * weight
    for r in range(tile_rows):
        rows_ref[r] = flat_ref[pl.ds(r, members, stride=tile_rows), :].astype(bf16)
    outward(0, rows_ref, held_ref, inverse_ref, message_ref, total_ref)


def second_kernel(rows_ref, held_ref, inverse_ref, message_ref, total_ref):
    outward(1, rows_ref, held_ref, inverse_ref, message_ref, total_ref)


def own_kernel(after_ref, rows_ref, held_ref, inverse_ref, first_ref, out_ref):
    tile_rows, members, cols = rows_ref.shape
    patch_cols = cols // PATCH
    plans = [taper_plan(MIDDLE + a * PATCH, inverse_ref[a]) for a in range(tile_rows // PATCH)]
    totals = [jnp.zeros((patch_cols * members + PATCH, members), f32) for _ in plans]
    for start in range(0, tile_rows, STEP):
        anomalies = [rows_ref[start + i] for i in range(STEP)]
        fields = [held_ref[k, start : start + STEP, :] for k in range(2)]
        totals = [accumulate(total, plan, anomalies, *fields, jnp.int32(start)) for total, plan in zip(totals, plans)]
    sums = jnp.concatenate(paired(totals, members, patch_cols), 0)
    out_ref[...] = sums + arrived(first_ref, 0, patch_cols)


def finish_kernel(total_ref, second_ref, lag_ref, mean_ref, out_ref, flat_ref):
    tile_rows, members, cols = lag_ref.shape
    degree = members - 1.0
    pair_count = total_ref.shape[0] // members
    grams_end = pair_count * members
    wide = 2 * cols
    row = lax.broadcasted_iota(jnp.int32, (members, wide), 0)
    lane = lax.broadcasted_iota(jnp.int32, (members, wide), 1)
    identity = jnp.where(row == lane % members, 1.0, 0.0)
    left_mask = jnp.where(lane[:, :cols] < members, 1.0, 0.0).astype(bf16)
    right_mask = jnp.where(lane[:, :cols] < members, 0.0, 1.0).astype(bf16)
    nothing = jnp.zeros((2 * members, cols), bf16)

    def blocks(y):
        upper, lower = (jnp.concatenate([half * left_mask, half * right_mask], 0) for half in (y[:, :cols], y[:, cols:]))
        return jnp.concatenate(
            [jnp.concatenate([upper, nothing], 1), jnp.concatenate([nothing, lower], 1)], 0
        )

    def right(y):
        high, low = split(y)
        return blocks(high), blocks(low)

    def product(lefts, factor):
        high, low = factor
        rows = lefts[0][0].shape[0]
        first = mm(jnp.concatenate([part for pair in lefts for part in pair], 0), high)
        second = mm(jnp.concatenate([pair[0] for pair in lefts], 0), low)
        return [
            first[2 * k * rows : (2 * k + 1) * rows]
            + (first[(2 * k + 1) * rows : (2 * k + 2) * rows] + second[k * rows : (k + 1) * rows])
            for k in range(len(lefts))
        ]

    total = total_ref[...] + arrived(second_ref, 1, pair_count)
    grams = [total[p * members : (p + 1) * members] for p in range(pair_count)]
    squares = jnp.concatenate([jnp.sum(gram * gram, axis=0, keepdims=True) for gram in grams], 0)
    at_left = lax.broadcasted_iota(jnp.int32, squares.shape, 1) < members
    norm_left = jnp.sum(jnp.where(at_left, squares, 0.0), axis=1, keepdims=True)
    norm_right = jnp.sum(jnp.where(at_left, 0.0, squares), axis=1, keepdims=True)
    bounds = degree + jnp.sqrt(jnp.where(at_left, norm_left, norm_right))
    quads = range(pair_count // 2)

    def beside(parts, q):
        return jnp.concatenate([parts[2 * q], parts[2 * q + 1]], 1)

    def rows_of(table):
        return [table[p : p + 1] for p in range(pair_count)]

    bound = [beside(rows_of(bounds), q) for q in quads]
    sides = [beside(rows_of(total[grams_end:]), q) for q in quads]
    iterates = [(beside(grams, q) + degree * identity) / bound[q] for q in quads]
    corrections = [1.5 * identity - 0.5 * iterates[q] for q in quads]
    factors = [right(corrections[q]) for q in quads]
    iterates = [product([split(iterates[q])], factors[q])[0] for q in quads]
    roots = corrections
    for step in range(1, NS_STEPS):
        halves = [split(roots[q]) for q in quads]
        corrections = [1.5 * identity - 0.5 * product([halves[q]], right(iterates[q]))[0] for q in quads]
        factors = [right(corrections[q]) for q in quads]
        if step < NS_STEPS - 1:
            both = [product([split(iterates[q]), halves[q]], factors[q]) for q in quads]
            iterates = [pair[0] for pair in both]
            roots = [pair[1] for pair in both]
        else:
            roots = [product([halves[q]], factors[q])[0] for q in quads]
    mixings = []
    for q in quads:
        factor = right(roots[q])
        side = jnp.broadcast_to(sides[q], (PATCH, wide))
        inner = product([split(side)], factor)[0]
        weights = product([split(inner)], factor)[0][:1] / bound[q]
        mixing = (jnp.sqrt(degree / bound[q]) * roots[q] + weights).astype(bf16)
        mixings += [mixing[:, :cols], mixing[:, cols:]]

    patch = lax.broadcasted_iota(jnp.int32, (members, cols), 1) // PATCH
    even = jnp.where(patch % 2 == 0, 1.0, 0.0).astype(bf16)
    odd = jnp.where(patch % 2 == 1, 1.0, 0.0).astype(bf16)
    per_row = cols // (2 * PATCH)
    for a in range(tile_rows // PATCH):
        mixing = jnp.concatenate(mixings[a * per_row : (a + 1) * per_row], 0)
        for r in range(a * PATCH, (a + 1) * PATCH, 2):
            state = jnp.concatenate(
                [jnp.concatenate([lag_ref[i] * even, lag_ref[i] * odd], 0) for i in (r, r + 1)], 1
            )
            spread_out = mm(mixing, state)
            for i in (0, 1):
                part = spread_out[:, i * cols : (i + 1) * cols]
                chosen = part[:members]
                for pair in range(1, per_row):
                    chosen = jnp.where(patch // 2 == pair, part[pair * members : (pair + 1) * members], chosen)
                flat_ref[pl.ds(r + i, members, stride=tile_rows), :] = chosen + mean_ref[r + i : r + i + 1, :]
    out_ref[...] = flat_ref[...].reshape(1, members, tile_rows, cols).astype(bf16)


def shards(history, forecast, spot, alive, levels, precision, radius):
    shares = lax.axis_size("lag")
    tiles = lax.axis_size("dom")
    share_members, tile_rows, cols = forecast.shape
    members = share_members * shares
    patch_cols = cols // PATCH
    def call(kernel, name, in_specs, out_shape, scratch=()):
        return pl.pallas_call(
            kernel,
            in_specs=in_specs,
            out_specs=jax.tree.map(lambda _: vmem, out_shape),
            out_shape=out_shape,
            scratch_shapes=scratch,
            compiler_params=pltpu.CompilerParams(vmem_limit_bytes=32 * 2**20),
            name=name,
        )

    shape = jax.ShapeDtypeStruct
    vmem = pl.BlockSpec(memory_space=pltpu.VMEM)
    parts = [forecast]
    for k in range(1, shares):
        parts.append(lax.ppermute(forecast, "lag", [((i + k) % shares, i) for i in range(shares)]))
    live = lax.broadcasted_iota(jnp.int32, spot.shape, 1) < alive[:, None]
    weights = jnp.where(live, precision, 0.0)
    kind = lax.broadcasted_iota(jnp.int32, (3, *spot.shape), 0)
    tables = jnp.where(kind == 0, weights[None], jnp.where(kind == 1, (weights * levels)[None], spot.astype(f32)[None]))
    inverse = jnp.broadcast_to(
        (1.0 / jnp.square(radius.astype(f32))).reshape(-1, patch_cols, 1), (tile_rows // PATCH, patch_cols, cols)
    )
    sent, tables = lax.optimization_barrier((inverse, tables))
    rings = [ring(tiles, shares, turn) for turn in range(2)]
    axes = ("dom", "lag")
    next_inverses = [lax.ppermute(sent, axes, [(t, s) for s, t in pairs]) for pairs in rings]
    fields, own_sum = call(
        functools.partial(fields_kernel, cols),
        "fields",
        [vmem, vmem],
        [shape((2, tile_rows, cols), f32), shape((tile_rows, cols), f32)],
    )(tables, forecast)
    pair_rows = patch_cols * members
    message_shape = shape((pair_rows + 2 * patch_cols, 2 * members), bf16)
    total_scratch = pltpu.VMEM((2, patch_cols * members + PATCH, members), f32)
    rows, held, message = call(
        functools.partial(first_kernel, shares),
        "first_gram",
        [vmem] * (shares + 3),
        [shape((tile_rows, members, cols), bf16), shape((2, tile_rows, cols), f32), message_shape],
        [pltpu.VMEM((members * tile_rows, cols), f32), total_scratch],
    )(*parts, own_sum, fields, next_inverses[0])
    first = lax.ppermute(message, axes, rings[0])
    message = call(second_kernel, "second_gram", [vmem] * 3, message_shape, [total_scratch])(rows, held, next_inverses[1])
    second = lax.ppermute(message, axes, rings[1])
    lag_rows, lag_mean = call(
        state_kernel,
        "state",
        [vmem, vmem],
        [shape((tile_rows, members, cols), bf16), shape((tile_rows, cols), f32)],
        [pltpu.VMEM((members * tile_rows, cols), f32)],
    )(held, history[0])
    own_shape = shape((pair_rows + patch_cols, 2 * members), f32)
    own = call(own_kernel, "own_gram", [vmem] * 5, own_shape)(lag_mean, rows, held, inverse, first)
    return call(
        finish_kernel,
        "finish",
        [vmem] * 4,
        shape((1, members, tile_rows, cols), bf16),
        [pltpu.VMEM((members * tile_rows, cols), f32)],
    )(own, second, lag_rows, lag_mean)


def solution(mesh):
    in_specs = (
        P("lag", None, "dom", None),
        P("lag", "dom", None),
        P("dom", None),
        P("dom"),
        P("dom", None),
        P("dom", None),
        P("dom"),
    )
    out_specs = P("lag", None, "dom", None)
    return jax.shard_map(shards, mesh=mesh, in_specs=in_specs, out_specs=out_specs, check_vma=False)
```

profile of v0, /device:TPU:0, one launch (start us, length us, event | category | flops | bytes accessed | tf_op | source)
XLA Modules:
  0.0 23.9 jit_solution(16756141195834247686)
XLA Ops:
  0.0 0.0 copy-start.4
  0.0 3.0 %collective-permute-start = (bf16[32,32,128]{2,1,0:T(8,128)(2,1)}, bf16[32,32,128]{2,1,0:T(8,128)(2,1)S(1)}, u32[]{:S(2)}, u32[]{:S(2)}) collective-permute-start(bf16[32,32,128]{2,1,0:T(8,128)(2,1)} %refs_0_.1), channel_id=1, source_target_pairs={{1,0},{0,1},{3,2},{2,3},{5,4},{4,5},{7,6},{6,7},{9,8},{8,9},{11,10... | collective-permute-start | bytes 786440 | tf_op jit(solution)/shard_map/ppermute | solution.py:323
  3.0 0.7 %multiply_divide_fusion = f32[16]{0:T(128)S(1)} fusion(s32[16]{0:T(128)} %param.13), kind=kLoop, calls=%fused_computation.5 | loop fusion | flops 48 | bytes 128 | tf_op jit(solution)/shard_map/div | solution.py:329
  3.6 0.0 copy-done.4
  3.6 0.0 copy-start.3
  3.6 0.8 %fusion.1 = (f32[16,256]{1,0:T(8,128)S(1)}, f32[16,256]{1,0:T(8,128)S(1)}) fusion(f32[16,256]{1,0:T(8,128)} %param.11, f32[16,256]{1,0:T(8,128)} %param.12, s32[16]{0:T(128)S(1)} %copy-done.4), kind=kLoop, calls=%fused_computation.6 | loop fusion | flops 12288 | bytes 65600 | tf_op jit(solution)/shard_map/mul | solution.py:327
  4.5 0.1 broadcast_in_dim.39
  4.5 0.0 copy-done.3
  4.6 0.1 select_select_fusion.table_ref
  4.6 0.1 broadcast_in_dim.40.inverse_ref
  4.7 0.0 collective-permute-start.1
  4.7 2.0 %collective-permute-start.3 = (f32[2,8,128]{2,1,0:T(8,128)S(1)}, f32[2,8,128]{2,1,0:T(8,128)S(1)}, u32[]{:S(2)}, u32[]{:S(2)}) collective-permute-start(f32[2,8,128]{2,1,0:T(8,128)S(1)} %broadcast_in_dim.40.inverse_ref), channel_id=1, source_target_pairs={{2,0},{0,1},{4,2},{1,3},{6,4},{3,5},{8,6},{5,7},{10,8},{7,9},{12,1... | collective-permute-start | bytes 24584 | tf_op jit(solution)/shard_map/ppermute | solution.py:334
  6.7 0.0 copy-start
  6.7 0.9 %copy-done = bf16[32,32,128]{2,1,0:T(8,128)(2,1)S(1)} copy-done((bf16[32,32,128]{2,1,0:T(8,128)(2,1)S(1)}, bf16[32,32,128]{2,1,0:T(8,128)(2,1)}, u32[]{:S(2)}) %copy-start) | copy-done | bytes 262168
  7.7 0.0 copy-start.1
  7.7 0.5 %fields.1 = (f32[2,32,128]{2,1,0:T(8,128)S(1)}, f32[32,128]{1,0:T(8,128)S(1)}) custom-call(f32[3,16,256]{2,1,0:T(8,128)S(1)} %select_select_fusion.table_ref, bf16[32,32,128]{2,1,0:T(8,128)(2,1)S(1)} %copy-done), custom_call_target="tpu_custom_call" | custom-call | tf_op jit(solution)/shard_map/fields/pallas_call | solution.py:335
  8.2 1.4 %collective-permute-done.1.refs_4_ = f32[2,8,128]{2,1,0:T(8,128)S(1)} collective-permute-done((f32[2,8,128]{2,1,0:T(8,128)S(1)}, f32[2,8,128]{2,1,0:T(8,128)S(1)}, u32[]{:S(2)}, u32[]{:S(2)}) %collective-permute-start.1) | collective-permute-done | bytes 8224 | tf_op jit(solution)/shard_map/ppermute | solution.py:334
  9.6 0.0 collective-permute-done.refs_1_
  9.6 0.0 copy-done.1
  9.6 0.0 copy-start.2
  9.6 1.8 %first_gram.1 = (bf16[32,64,128]{2,1,0:T(8,128)(2,1)S(1)}, f32[2,32,128]{2,1,0:T(8,128)S(1)}, bf16[528,128]{1,0:T(8,128)(2,1)S(1)}) custom-call(bf16[32,32,128]{2,1,0:T(8,128)(2,1)S(1)} %copy-done.1, bf16[32,32,128]{2,1,0:T(8,128)(2,1)S(1)} %collective-permute-done.refs_1_, f32[32,128]{1,0:T(8,128)S(1)} %get-tuple-element.15.refs_2_, ...), custom_call_target="tpu_custom_call" | custom-call | tf_op jit(solution)/shard_map/first_gram/pallas_call | solution.py:344
  11.4 1.7 %collective-permute-start.2 = (bf16[528,128]{1,0:T(8,128)(2,1)S(1)}, bf16[528,128]{1,0:T(8,128)(2,1)S(1)}, u32[]{:S(2)}, u32[]{:S(2)}) collective-permute-start(bf16[528,128]{1,0:T(8,128)(2,1)S(1)} %get-tuple-element.21), channel_id=1, source_target_pairs={{0,1},{1,3},{2,0},{3,5},{4,2},{5,7},{6,4},{7,9},{8,6},{9,11},{10,8... | collective-permute-start | bytes 405512 | tf_op jit(solution)/shard_map/ppermute | solution.py:351
  13.1 0.0 collective-permute-done.3.inverse_ref
  13.1 1.4 %second_gram.1 = bf16[528,128]{1,0:T(8,128)(2,1)S(1)} custom-call(bf16[32,64,128]{2,1,0:T(8,128)(2,1)S(1)} %get-tuple-element.20.rows_ref, f32[2,32,128]{2,1,0:T(8,128)S(1)} %get-tuple-element.18.after_ref.held_ref, f32[2,8,128]{2,1,0:T(8,128)S(1)} %collective-permute-done.3.inverse_ref), custom_call_target="tpu_custom_call" | custom-call | tf_op jit(solution)/shard_map/second_gram/pallas_call | solution.py:352
  14.5 0.1 collective-permute-start.4
  14.6 0.0 copy-done.2
  14.6 0.7 %state.1 = (bf16[32,64,128]{2,1,0:T(8,128)(2,1)S(1)}, f32[32,128]{1,0:T(8,128)S(1)}) custom-call(f32[2,32,128]{2,1,0:T(8,128)S(1)} %get-tuple-element.18.after_ref.held_ref, bf16[64,32,128]{2,1,0:T(8,128)(2,1)S(1)} %bitcast.1), custom_call_target="tpu_custom_call" | custom-call | tf_op jit(solution)/shard_map/state/pallas_call | solution.py:354
  15.3 0.3 %collective-permute-done.2.first_ref = bf16[528,128]{1,0:T(8,128)(2,1)S(1)} collective-permute-done((bf16[528,128]{1,0:T(8,128)(2,1)S(1)}, bf16[528,128]{1,0:T(8,128)(2,1)S(1)}, u32[]{:S(2)}, u32[]{:S(2)}) %collective-permute-start.2) | collective-permute-done | bytes 135200 | tf_op jit(solution)/shard_map/ppermute | solution.py:351
  15.7 2.5 %own_gram.1.total_ref = f32[520,128]{1,0:T(8,128)S(1)} custom-call(f32[32,128]{1,0:T(8,128)S(1)} %get-tuple-element.19.after_ref.mean_ref, bf16[32,64,128]{2,1,0:T(8,128)(2,1)S(1)} %get-tuple-element.20.rows_ref, f32[2,32,128]{2,1,0:T(8,128)S(1)} %get-tuple-element.18.after_ref.held_ref, f32[2,8,128]{2,1,0:T(8,128)S(1)} %broadcast_in_dim.40.inverse_ref, ...), custom_call_target="tpu_custom_call" | custom-call | tf_op jit(solution)/shard_map/own_gram/pallas_call | solution.py:362
  18.2 1.4 %collective-permute-done.4.second_ref = bf16[528,128]{1,0:T(8,128)(2,1)S(1)} collective-permute-done((bf16[528,128]{1,0:T(8,128)(2,1)S(1)}, bf16[528,128]{1,0:T(8,128)(2,1)S(1)}, u32[]{:S(2)}, u32[]{:S(2)}) %collective-permute-start.4) | collective-permute-done | bytes 135200 | tf_op jit(solution)/shard_map/ppermute | solution.py:353
  19.6 4.3 %finish.1 = bf16[1,64,32,128]{3,2,1,0:T(8,128)(2,1)} custom-call(f32[520,128]{1,0:T(8,128)S(1)} %own_gram.1.total_ref, bf16[528,128]{1,0:T(8,128)(2,1)S(1)} %collective-permute-done.4.second_ref, bf16[32,64,128]{2,1,0:T(8,128)(2,1)S(1)} %get-tuple-element.22.lag_ref, f32[32,128]{1,0:T(8,128)S(1)} %get-tuple-element.19.after_ref.mean_ref), custom_call_target="tpu_custom_call" | custom-call | tf_op jit(solution)/shard_map/finish/pallas_call | solution.py:363
  (2 shorter events, 0.0 us)
Async XLA Ops:
  0.0 3.6 %copy-start.4 = (s32[16]{0:T(128)S(1)}, s32[16]{0:T(128)}, u32[]{:S(2)}) copy-start(s32[16]{0:T(128)} %param.10) | copy-start | bytes 196
  0.0 9.6 %collective-permute-start = (bf16[32,32,128]{2,1,0:T(8,128)(2,1)}, bf16[32,32,128]{2,1,0:T(8,128)(2,1)S(1)}, u32[]{:S(2)}, u32[]{:S(2)}) collective-permute-start(bf16[32,32,128]{2,1,0:T(8,128)(2,1)} %refs_0_.1), channel_id=1, source_target_pairs={{1,0},{0,1},{3,2},{2,3},{5,4},{4,5},{7,6},{6,7},{9,8},{8,9},{11,10... | collective-permute-start | bytes 786440 | tf_op jit(solution)/shard_map/ppermute | solution.py:323
  3.6 0.9 %copy-start.3 = (s32[16,256]{1,0:T(8,128)S(1)}, s32[16,256]{1,0:T(8,128)}, u32[]{:S(2)}) copy-start(s32[16,256]{1,0:T(8,128)} %param.9) | copy-start | bytes 49156
  4.7 4.9 %collective-permute-start.1 = (f32[2,8,128]{2,1,0:T(8,128)S(1)}, f32[2,8,128]{2,1,0:T(8,128)S(1)}, u32[]{:S(2)}, u32[]{:S(2)}) collective-permute-start(f32[2,8,128]{2,1,0:T(8,128)S(1)} %broadcast_in_dim.40.inverse_ref), channel_id=1, source_target_pairs={{1,0},{3,1},{0,2},{5,3},{2,4},{7,5},{4,6},{9,7},{6,8},{11,9},{8,10... | collective-permute-start | bytes 24584 | tf_op jit(solution)/shard_map/ppermute | solution.py:334
  4.7 8.4 %collective-permute-start.3 = (f32[2,8,128]{2,1,0:T(8,128)S(1)}, f32[2,8,128]{2,1,0:T(8,128)S(1)}, u32[]{:S(2)}, u32[]{:S(2)}) collective-permute-start(f32[2,8,128]{2,1,0:T(8,128)S(1)} %broadcast_in_dim.40.inverse_ref), channel_id=1, source_target_pairs={{2,0},{0,1},{4,2},{1,3},{6,4},{3,5},{8,6},{5,7},{10,8},{7,9},{12,1... | collective-permute-start | bytes 24584 | tf_op jit(solution)/shard_map/ppermute | solution.py:334
  6.7 0.9 %copy-start = (bf16[32,32,128]{2,1,0:T(8,128)(2,1)S(1)}, bf16[32,32,128]{2,1,0:T(8,128)(2,1)}, u32[]{:S(2)}) copy-start(bf16[32,32,128]{2,1,0:T(8,128)(2,1)} %refs_0_.1) | copy-start | bytes 786436
  7.7 1.9 %copy-start.1 = (bf16[32,32,128]{2,1,0:T(8,128)(2,1)S(1)}, bf16[32,32,128]{2,1,0:T(8,128)(2,1)}, u32[]{:S(2)}) copy-start(bf16[32,32,128]{2,1,0:T(8,128)(2,1)} %refs_0_.1) | copy-start | bytes 786436
  9.6 5.0 %copy-start.2 = (bf16[1,64,32,128]{3,2,1,0:T(8,128)(2,1)S(1)}, bf16[1,64,32,128]{3,2,1,0:T(8,128)(2,1)}, u32[]{:S(2)}) copy-start(bf16[1,64,32,128]{3,2,1,0:T(8,128)(2,1)} %param.7) | copy-start | bytes 1572868
  11.4 4.3 %collective-permute-start.2 = (bf16[528,128]{1,0:T(8,128)(2,1)S(1)}, bf16[528,128]{1,0:T(8,128)(2,1)S(1)}, u32[]{:S(2)}, u32[]{:S(2)}) collective-permute-start(bf16[528,128]{1,0:T(8,128)(2,1)S(1)} %get-tuple-element.21), channel_id=1, source_target_pairs={{0,1},{1,3},{2,0},{3,5},{4,2},{5,7},{6,4},{7,9},{8,6},{9,11},{10,8... | collective-permute-start | bytes 405512 | tf_op jit(solution)/shard_map/ppermute | solution.py:351
  14.5 5.1 %collective-permute-start.4 = (bf16[528,128]{1,0:T(8,128)(2,1)S(1)}, bf16[528,128]{1,0:T(8,128)(2,1)S(1)}, u32[]{:S(2)}, u32[]{:S(2)}) collective-permute-start(bf16[528,128]{1,0:T(8,128)(2,1)S(1)} %second_gram.1), channel_id=1, source_target_pairs={{0,2},{1,0},{2,4},{3,1},{4,6},{5,3},{6,8},{7,5},{8,10},{9,7},{10,1... | collective-permute-start | bytes 405512 | tf_op jit(solution)/shard_map/ppermute | solution.py:353
where the time goes:
time: 24.1 us; the launch traced here: 23.9 us
  Pallas kernels  11.2 us (46%)
  starting transfers between devices  6.79 us (28%)
  waiting for transfers between devices  3.2 us (13%)
  other arithmetic  1.57 us (7%)
  local copies, waits for them, and re-layouts  1.12 us (5%)
    pallas_call x1, Pallas kernels, shards(): call(finish_kernel, 'finish', [vmem] * 4, shape((1, members, tile_rows, c...  4.31 us
    ppermute x1, starting transfers between devices, shards(): lax.ppermute(forecast, 'lag', [((i + k) % shares, i) for i in range(share...  2.97 us
    pallas_call x1, Pallas kernels, shards(): call(own_kernel, 'own_gram', [vmem] * 5, own_shape)  2.46 us
    ppermute x2, starting transfers between devices, shards(): lax.ppermute(sent, axes, [(t, s) for s, t in pairs])  2.02 us
    pallas_call x1, Pallas kernels, shards(): call(functools.partial(first_kernel, shares), 'first_gram', [vmem] * (sha...  1.81 us
    ppermute x1, starting transfers between devices, shards(): first = lax.ppermute(message, axes, rings[0])  1.74 us
    ppermute x1, waiting for transfers between devices, shards(): second = lax.ppermute(message, axes, rings[1])  1.45 us
    ppermute x2, waiting for transfers between devices, shards(): lax.ppermute(sent, axes, [(t, s) for s, t in pairs])  1.4 us
  transfers between devices with their start and end apart: 5, of which 3 were waited for; matrix products, arithmetic and copies ran while one was open for 7% of the time, Pallas kernels for 29%

commit v1 on v0

--- a/solution.py
+++ b/solution.py
@@ -209,92 +209,79 @@
     degree = members - 1.0
     pair_count = total_ref.shape[0] // members
     grams_end = pair_count * members
-    wide = 2 * cols
-    row = lax.broadcasted_iota(jnp.int32, (members, wide), 0)
-    lane = lax.broadcasted_iota(jnp.int32, (members, wide), 1)
+    row = lax.broadcasted_iota(jnp.int32, (members, cols), 0)
+    lane = lax.broadcasted_iota(jnp.int32, (members, cols), 1)
     identity = jnp.where(row == lane % members, 1.0, 0.0)
-    left_mask = jnp.where(lane[:, :cols] < members, 1.0, 0.0).astype(bf16)
-    right_mask = jnp.where(lane[:, :cols] < members, 0.0, 1.0).astype(bf16)
-    nothing = jnp.zeros((2 * members, cols), bf16)
-
-    def blocks(y):
-        upper, lower = (jnp.concatenate([half * left_mask, half * right_mask], 0) for half in (y[:, :cols], y[:, cols:]))
+    left_mask = jnp.where(lane < members, 1.0, 0.0).astype(bf16)
+    right_mask = jnp.where(lane < members, 0.0, 1.0).astype(bf16)
+
+    def right(y):
+        halves = split(y)
         return jnp.concatenate(
-            [jnp.concatenate([upper, nothing], 1), jnp.concatenate([nothing, lower], 1)], 0
+            [jnp.concatenate([half * mask for half in halves], 1) for mask in (left_mask, right_mask)], 0
         )
 
-    def right(y):
-        high, low = split(y)
-        return blocks(high), blocks(low)
-
     def product(lefts, factor):
-        high, low = factor
-        rows = lefts[0][0].shape[0]
-        first = mm(jnp.concatenate([part for pair in lefts for part in pair], 0), high)
-        second = mm(jnp.concatenate([pair[0] for pair in lefts], 0), low)
-        return [
-            first[2 * k * rows : (2 * k + 1) * rows]
-            + (first[(2 * k + 1) * rows : (2 * k + 2) * rows] + second[k * rows : (k + 1) * rows])
-            for k in range(len(lefts))
-        ]
+        both = mm(jnp.concatenate([half for halves in lefts for half in halves], 0), factor)
+        results, at = [], 0
+        for high, low in lefts:
+            rows = high.shape[0]
+            upper, lower = both[at : at + rows], both[at + rows : at + 2 * rows]
+            results.append(upper[:, :cols] + (upper[:, cols:] + lower[:, :cols]))
+            at += 2 * rows
+        return results
 
     total = total_ref[...] + arrived(second_ref, 1, pair_count)
-    grams = [total[p * members : (p + 1) * members] for p in range(pair_count)]
+    pairs = range(pair_count)
+    grams = [total[p * members : (p + 1) * members] for p in pairs]
     squares = jnp.concatenate([jnp.sum(gram * gram, axis=0, keepdims=True) for gram in grams], 0)
     at_left = lax.broadcasted_iota(jnp.int32, squares.shape, 1) < members
     norm_left = jnp.sum(jnp.where(at_left, squares, 0.0), axis=1, keepdims=True)
     norm_right = jnp.sum(jnp.where(at_left, 0.0, squares), axis=1, keepdims=True)
     bounds = degree + jnp.sqrt(jnp.where(at_left, norm_left, norm_right))
-    quads = range(pair_count // 2)
-
-    def beside(parts, q):
-        return jnp.concatenate([parts[2 * q], parts[2 * q + 1]], 1)
-
-    def rows_of(table):
-        return [table[p : p + 1] for p in range(pair_count)]
-
-    bound = [beside(rows_of(bounds), q) for q in quads]
-    sides = [beside(rows_of(total[grams_end:]), q) for q in quads]
-    iterates = [(beside(grams, q) + degree * identity) / bound[q] for q in quads]
-    corrections = [1.5 * identity - 0.5 * iterates[q] for q in quads]
-    factors = [right(corrections[q]) for q in quads]
-    iterates = [product([split(iterates[q])], factors[q])[0] for q in quads]
-    roots = corrections
-    for step in range(1, NS_STEPS):
-        halves = [split(roots[q]) for q in quads]
-        corrections = [1.5 * identity - 0.5 * product([halves[q]], right(iterates[q]))[0] for q in quads]
-        factors = [right(corrections[q]) for q in quads]
-        if step < NS_STEPS - 1:
-            both = [product([split(iterates[q]), halves[q]], factors[q]) for q in quads]
-            iterates = [pair[0] for pair in both]
-            roots = [pair[1] for pair in both]
-        else:
-            roots = [product([halves[q]], factors[q])[0] for q in quads]
+    inverses = 1.0 / bounds
+    spreads = jnp.sqrt(degree * inverses)
+    sides = [jnp.broadcast_to(total[grams_end + p : grams_end + p + 1], (PATCH, cols)) for p in pairs]
+    iterates = [(grams[p] + degree * identity) * inverses[p : p + 1] for p in pairs]
+    roots = [None for _ in pairs]
+    for step in range(NS_STEPS):
+        for p in pairs:
+            iterate = split(iterates[p])
+            root = None if step == 0 else split(roots[p])
+            ahead = iterates[p] if step == 0 else product([root], right(iterates[p]))[0]
+            correction = 1.5 * identity - 0.5 * ahead
+            lefts = [split(sides[p])]
+            if step > 0:
+                lefts.append(root)
+            if step < NS_STEPS - 1:
+                lefts.append(iterate)
+            results = product(lefts, right(correction))
+            sides[p] = results[0]
+            roots[p] = correction if step == 0 else results[1]
+            if step < NS_STEPS - 1:
+                iterates[p] = results[-1]
     mixings = []
-    for q in quads:
-        factor = right(roots[q])
-        side = jnp.broadcast_to(sides[q], (PATCH, wide))
-        inner = product([split(side)], factor)[0]
-        weights = product([split(inner)], factor)[0][:1] / bound[q]
-        mixing = (jnp.sqrt(degree / bound[q]) * roots[q] + weights).astype(bf16)
-        mixings += [mixing[:, :cols], mixing[:, cols:]]
+    for p in pairs:
+        weights = product([split(sides[p])], right(roots[p]))[0][:1] * inverses[p : p + 1]
+        mixings.append((spreads[p : p + 1] * roots[p] + weights).astype(bf16))
 
     patch = lax.broadcasted_iota(jnp.int32, (members, cols), 1) // PATCH
-    even = jnp.where(patch % 2 == 0, 1.0, 0.0).astype(bf16)
-    odd = jnp.where(patch % 2 == 1, 1.0, 0.0).astype(bf16)
-    per_row = cols // (2 * PATCH)
+    masks = [jnp.where(patch % 4 == k, 1.0, 0.0).astype(bf16) for k in range(4)]
+    quads = cols // (4 * PATCH)
     for a in range(tile_rows // PATCH):
-        mixing = jnp.concatenate(mixings[a * per_row : (a + 1) * per_row], 0)
+        mixing = jnp.concatenate(
+            [jnp.concatenate(mixings[2 * q : 2 * q + 2], 1) for q in range(a * quads, (a + 1) * quads)], 0
+        )
         for r in range(a * PATCH, (a + 1) * PATCH, 2):
             state = jnp.concatenate(
-                [jnp.concatenate([lag_ref[i] * even, lag_ref[i] * odd], 0) for i in (r, r + 1)], 1
+                [jnp.concatenate([lag_ref[i] * mask for mask in masks], 0) for i in (r, r + 1)], 1
             )
             spread_out = mm(mixing, state)
             for i in (0, 1):
                 part = spread_out[:, i * cols : (i + 1) * cols]
                 chosen = part[:members]
-                for pair in range(1, per_row):
-                    chosen = jnp.where(patch // 2 == pair, part[pair * members : (pair + 1) * members], chosen)
+                for q in range(1, quads):
+                    chosen = jnp.where(patch // 4 == q, part[q * members : (q + 1) * members], chosen)
                 flat_ref[pl.ds(r + i, members, stride=tile_rows), :] = chosen + mean_ref[r + i : r + i + 1, :]
     out_ref[...] = flat_ref[...].reshape(1, members, tile_rows, cols).astype(bf16)
 

time: 24.1 us -> 25 us (1.037)
  Pallas kernels: 11.2 us -> 12 us
    pallas_call x1, Pallas kernels: 4.31 us -> 5.18 us  [shards(): call(finish_kernel, 'finish', [vmem] * 4, shape((1, members, tile_rows, c...]
  transfers between devices with their start and end apart: 5 -> 5, of which waited for: 3 -> 3; matrix products, arithmetic and copies ran while one was open for 7% -> 7% of each run, Pallas kernels for 29% -> 28%
where the time goes in v1:
time: 25 us; the launch traced here: 24.8 us
  Pallas kernels  12 us (48%)
  starting transfers between devices  6.79 us (27%)
  waiting for transfers between devices  3.2 us (13%)
  other arithmetic  1.57 us (6%)
  local copies, waits for them, and re-layouts  1.12 us (4%)
    pallas_call x1, Pallas kernels, shards(): call(finish_kernel, 'finish', [vmem] * 4, shape((1, members, tile_rows, c...  5.18 us
    ppermute x1, starting transfers between devices, shards(): lax.ppermute(forecast, 'lag', [((i + k) % shares, i) for i in range(share...  2.97 us
    pallas_call x1, Pallas kernels, shards(): call(own_kernel, 'own_gram', [vmem] * 5, own_shape)  2.46 us
    ppermute x2, starting transfers between devices, shards(): lax.ppermute(sent, axes, [(t, s) for s, t in pairs])  2.02 us
    pallas_call x1, Pallas kernels, shards(): call(functools.partial(first_kernel, shares), 'first_gram', [vmem] * (sha...  1.81 us
    ppermute x1, starting transfers between devices, shards(): first = lax.ppermute(message, axes, rings[0])  1.74 us
    ppermute x1, waiting for transfers between devices, shards(): second = lax.ppermute(message, axes, rings[1])  1.45 us
    ppermute x2, waiting for transfers between devices, shards(): lax.ppermute(sent, axes, [(t, s) for s, t in pairs])  1.4 us
  transfers between devices with their start and end apart: 5, of which 3 were waited for; matrix products, arithmetic and copies ran while one was open for 7% of the time, Pallas kernels for 28%

profile of v1, /device:TPU:0, one launch (start us, length us, event | category | flops | bytes accessed | tf_op | source)
XLA Modules:
  0.0 24.8 jit_solution(4849566497699346018)
XLA Ops:
  0.0 0.0 copy-start.4
  0.0 3.0 %collective-permute-start = (bf16[32,32,128]{2,1,0:T(8,128)(2,1)}, bf16[32,32,128]{2,1,0:T(8,128)(2,1)S(1)}, u32[]{:S(2)}, u32[]{:S(2)}) collective-permute-start(bf16[32,32,128]{2,1,0:T(8,128)(2,1)} %refs_0_.1), channel_id=1, source_target_pairs={{1,0},{0,1},{3,2},{2,3},{5,4},{4,5},{7,6},{6,7},{9,8},{8,9},{11,10... | collective-permute-start | bytes 786440 | tf_op jit(solution)/shard_map/ppermute | solution.py:310
  3.0 0.7 %multiply_divide_fusion = f32[16]{0:T(128)S(1)} fusion(s32[16]{0:T(128)} %param.13), kind=kLoop, calls=%fused_computation.5 | loop fusion | flops 48 | bytes 128 | tf_op jit(solution)/shard_map/div | solution.py:316
  3.6 0.0 copy-done.4
  3.6 0.0 copy-start.3
  3.6 0.8 %fusion.1 = (f32[16,256]{1,0:T(8,128)S(1)}, f32[16,256]{1,0:T(8,128)S(1)}) fusion(f32[16,256]{1,0:T(8,128)} %param.11, f32[16,256]{1,0:T(8,128)} %param.12, s32[16]{0:T(128)S(1)} %copy-done.4), kind=kLoop, calls=%fused_computation.6 | loop fusion | flops 12288 | bytes 65600 | tf_op jit(solution)/shard_map/mul | solution.py:314
  4.5 0.1 broadcast_in_dim.39
  4.5 0.0 copy-done.3
  4.6 0.1 select_select_fusion.table_ref
  4.6 0.1 broadcast_in_dim.40.inverse_ref
  4.7 0.0 collective-permute-start.1
  4.7 2.0 %collective-permute-start.3 = (f32[2,8,128]{2,1,0:T(8,128)S(1)}, f32[2,8,128]{2,1,0:T(8,128)S(1)}, u32[]{:S(2)}, u32[]{:S(2)}) collective-permute-start(f32[2,8,128]{2,1,0:T(8,128)S(1)} %broadcast_in_dim.40.inverse_ref), channel_id=1, source_target_pairs={{2,0},{0,1},{4,2},{1,3},{6,4},{3,5},{8,6},{5,7},{10,8},{7,9},{12,1... | collective-permute-start | bytes 24584 | tf_op jit(solution)/shard_map/ppermute | solution.py:321
  6.7 0.0 copy-start
  6.7 0.9 %copy-done = bf16[32,32,128]{2,1,0:T(8,128)(2,1)S(1)} copy-done((bf16[32,32,128]{2,1,0:T(8,128)(2,1)S(1)}, bf16[32,32,128]{2,1,0:T(8,128)(2,1)}, u32[]{:S(2)}) %copy-start) | copy-done | bytes 262168
  7.7 0.0 copy-start.1
  7.7 0.5 %fields.1 = (f32[2,32,128]{2,1,0:T(8,128)S(1)}, f32[32,128]{1,0:T(8,128)S(1)}) custom-call(f32[3,16,256]{2,1,0:T(8,128)S(1)} %select_select_fusion.table_ref, bf16[32,32,128]{2,1,0:T(8,128)(2,1)S(1)} %copy-done), custom_call_target="tpu_custom_call" | custom-call | tf_op jit(solution)/shard_map/fields/pallas_call | solution.py:322
  8.2 1.4 %collective-permute-done.1.refs_4_ = f32[2,8,128]{2,1,0:T(8,128)S(1)} collective-permute-done((f32[2,8,128]{2,1,0:T(8,128)S(1)}, f32[2,8,128]{2,1,0:T(8,128)S(1)}, u32[]{:S(2)}, u32[]{:S(2)}) %collective-permute-start.1) | collective-permute-done | bytes 8224 | tf_op jit(solution)/shard_map/ppermute | solution.py:321
  9.6 0.0 collective-permute-done.refs_1_
  9.6 0.0 copy-done.1
  9.6 0.0 copy-start.2
  9.6 1.8 %first_gram.1 = (bf16[32,64,128]{2,1,0:T(8,128)(2,1)S(1)}, f32[2,32,128]{2,1,0:T(8,128)S(1)}, bf16[528,128]{1,0:T(8,128)(2,1)S(1)}) custom-call(bf16[32,32,128]{2,1,0:T(8,128)(2,1)S(1)} %copy-done.1, bf16[32,32,128]{2,1,0:T(8,128)(2,1)S(1)} %collective-permute-done.refs_1_, f32[32,128]{1,0:T(8,128)S(1)} %get-tuple-element.15.refs_2_, ...), custom_call_target="tpu_custom_call" | custom-call | tf_op jit(solution)/shard_map/first_gram/pallas_call | solution.py:331
  11.4 1.7 %collective-permute-start.2 = (bf16[528,128]{1,0:T(8,128)(2,1)S(1)}, bf16[528,128]{1,0:T(8,128)(2,1)S(1)}, u32[]{:S(2)}, u32[]{:S(2)}) collective-permute-start(bf16[528,128]{1,0:T(8,128)(2,1)S(1)} %get-tuple-element.21), channel_id=1, source_target_pairs={{0,1},{1,3},{2,0},{3,5},{4,2},{5,7},{6,4},{7,9},{8,6},{9,11},{10,8... | collective-permute-start | bytes 405512 | tf_op jit(solution)/shard_map/ppermute | solution.py:338
  13.1 0.0 collective-permute-done.3.inverse_ref
  13.1 1.4 %second_gram.1 = bf16[528,128]{1,0:T(8,128)(2,1)S(1)} custom-call(bf16[32,64,128]{2,1,0:T(8,128)(2,1)S(1)} %get-tuple-element.20.rows_ref, f32[2,32,128]{2,1,0:T(8,128)S(1)} %get-tuple-element.18.after_ref.held_ref, f32[2,8,128]{2,1,0:T(8,128)S(1)} %collective-permute-done.3.inverse_ref), custom_call_target="tpu_custom_call" | custom-call | tf_op jit(solution)/shard_map/second_gram/pallas_call | solution.py:339
  14.5 0.1 collective-permute-start.4
  14.6 0.0 copy-done.2
  14.6 0.7 %state.1 = (bf16[32,64,128]{2,1,0:T(8,128)(2,1)S(1)}, f32[32,128]{1,0:T(8,128)S(1)}) custom-call(f32[2,32,128]{2,1,0:T(8,128)S(1)} %get-tuple-element.18.after_ref.held_ref, bf16[64,32,128]{2,1,0:T(8,128)(2,1)S(1)} %bitcast.1), custom_call_target="tpu_custom_call" | custom-call | tf_op jit(solution)/shard_map/state/pallas_call | solution.py:341
  15.3 0.3 %collective-permute-done.2.first_ref = bf16[528,128]{1,0:T(8,128)(2,1)S(1)} collective-permute-done((bf16[528,128]{1,0:T(8,128)(2,1)S(1)}, bf16[528,128]{1,0:T(8,128)(2,1)S(1)}, u32[]{:S(2)}, u32[]{:S(2)}) %collective-permute-start.2) | collective-permute-done | bytes 135200 | tf_op jit(solution)/shard_map/ppermute | solution.py:338
  15.7 2.5 %own_gram.1.total_ref = f32[520,128]{1,0:T(8,128)S(1)} custom-call(f32[32,128]{1,0:T(8,128)S(1)} %get-tuple-element.19.after_ref.mean_ref, bf16[32,64,128]{2,1,0:T(8,128)(2,1)S(1)} %get-tuple-element.20.rows_ref, f32[2,32,128]{2,1,0:T(8,128)S(1)} %get-tuple-element.18.after_ref.held_ref, f32[2,8,128]{2,1,0:T(8,128)S(1)} %broadcast_in_dim.40.inverse_ref, ...), custom_call_target="tpu_custom_call" | custom-call | tf_op jit(solution)/shard_map/own_gram/pallas_call | solution.py:349
  18.2 1.4 %collective-permute-done.4.second_ref = bf16[528,128]{1,0:T(8,128)(2,1)S(1)} collective-permute-done((bf16[528,128]{1,0:T(8,128)(2,1)S(1)}, bf16[528,128]{1,0:T(8,128)(2,1)S(1)}, u32[]{:S(2)}, u32[]{:S(2)}) %collective-permute-start.4) | collective-permute-done | bytes 135200 | tf_op jit(solution)/shard_map/ppermute | solution.py:340
  19.6 5.2 %finish.1 = bf16[1,64,32,128]{3,2,1,0:T(8,128)(2,1)} custom-call(f32[520,128]{1,0:T(8,128)S(1)} %own_gram.1.total_ref, bf16[528,128]{1,0:T(8,128)(2,1)S(1)} %collective-permute-done.4.second_ref, bf16[32,64,128]{2,1,0:T(8,128)(2,1)S(1)} %get-tuple-element.22.lag_ref, f32[32,128]{1,0:T(8,128)S(1)} %get-tuple-element.19.after_ref.mean_ref), custom_call_target="tpu_custom_call" | custom-call | tf_op jit(solution)/shard_map/finish/pallas_call | solution.py:350
  (2 shorter events, 0.0 us)
Async XLA Ops:
  0.0 3.6 %copy-start.4 = (s32[16]{0:T(128)S(1)}, s32[16]{0:T(128)}, u32[]{:S(2)}) copy-start(s32[16]{0:T(128)} %param.10) | copy-start | bytes 196
  0.0 9.6 %collective-permute-start = (bf16[32,32,128]{2,1,0:T(8,128)(2,1)}, bf16[32,32,128]{2,1,0:T(8,128)(2,1)S(1)}, u32[]{:S(2)}, u32[]{:S(2)}) collective-permute-start(bf16[32,32,128]{2,1,0:T(8,128)(2,1)} %refs_0_.1), channel_id=1, source_target_pairs={{1,0},{0,1},{3,2},{2,3},{5,4},{4,5},{7,6},{6,7},{9,8},{8,9},{11,10... | collective-permute-start | bytes 786440 | tf_op jit(solution)/shard_map/ppermute | solution.py:310
  3.6 0.9 %copy-start.3 = (s32[16,256]{1,0:T(8,128)S(1)}, s32[16,256]{1,0:T(8,128)}, u32[]{:S(2)}) copy-start(s32[16,256]{1,0:T(8,128)} %param.9) | copy-start | bytes 49156
  4.7 4.9 %collective-permute-start.1 = (f32[2,8,128]{2,1,0:T(8,128)S(1)}, f32[2,8,128]{2,1,0:T(8,128)S(1)}, u32[]{:S(2)}, u32[]{:S(2)}) collective-permute-start(f32[2,8,128]{2,1,0:T(8,128)S(1)} %broadcast_in_dim.40.inverse_ref), channel_id=1, source_target_pairs={{1,0},{3,1},{0,2},{5,3},{2,4},{7,5},{4,6},{9,7},{6,8},{11,9},{8,10... | collective-permute-start | bytes 24584 | tf_op jit(solution)/shard_map/ppermute | solution.py:321
  4.7 8.4 %collective-permute-start.3 = (f32[2,8,128]{2,1,0:T(8,128)S(1)}, f32[2,8,128]{2,1,0:T(8,128)S(1)}, u32[]{:S(2)}, u32[]{:S(2)}) collective-permute-start(f32[2,8,128]{2,1,0:T(8,128)S(1)} %broadcast_in_dim.40.inverse_ref), channel_id=1, source_target_pairs={{2,0},{0,1},{4,2},{1,3},{6,4},{3,5},{8,6},{5,7},{10,8},{7,9},{12,1... | collective-permute-start | bytes 24584 | tf_op jit(solution)/shard_map/ppermute | solution.py:321
  6.7 0.9 %copy-start = (bf16[32,32,128]{2,1,0:T(8,128)(2,1)S(1)}, bf16[32,32,128]{2,1,0:T(8,128)(2,1)}, u32[]{:S(2)}) copy-start(bf16[32,32,128]{2,1,0:T(8,128)(2,1)} %refs_0_.1) | copy-start | bytes 786436
  7.7 1.9 %copy-start.1 = (bf16[32,32,128]{2,1,0:T(8,128)(2,1)S(1)}, bf16[32,32,128]{2,1,0:T(8,128)(2,1)}, u32[]{:S(2)}) copy-start(bf16[32,32,128]{2,1,0:T(8,128)(2,1)} %refs_0_.1) | copy-start | bytes 786436
  9.6 5.0 %copy-start.2 = (bf16[1,64,32,128]{3,2,1,0:T(8,128)(2,1)S(1)}, bf16[1,64,32,128]{3,2,1,0:T(8,128)(2,1)}, u32[]{:S(2)}) copy-start(bf16[1,64,32,128]{3,2,1,0:T(8,128)(2,1)} %param.7) | copy-start | bytes 1572868
  11.4 4.3 %collective-permute-start.2 = (bf16[528,128]{1,0:T(8,128)(2,1)S(1)}, bf16[528,128]{1,0:T(8,128)(2,1)S(1)}, u32[]{:S(2)}, u32[]{:S(2)}) collective-permute-start(bf16[528,128]{1,0:T(8,128)(2,1)S(1)} %get-tuple-element.21), channel_id=1, source_target_pairs={{0,1},{1,3},{2,0},{3,5},{4,2},{5,7},{6,4},{7,9},{8,6},{9,11},{10,8... | collective-permute-start | bytes 405512 | tf_op jit(solution)/shard_map/ppermute | solution.py:338
  14.5 5.1 %collective-permute-start.4 = (bf16[528,128]{1,0:T(8,128)(2,1)S(1)}, bf16[528,128]{1,0:T(8,128)(2,1)S(1)}, u32[]{:S(2)}, u32[]{:S(2)}) collective-permute-start(bf16[528,128]{1,0:T(8,128)(2,1)S(1)} %second_gram.1), channel_id=1, source_target_pairs={{0,2},{1,0},{2,4},{3,1},{4,6},{5,3},{6,8},{7,5},{8,10},{9,7},{10,1... | collective-permute-start | bytes 405512 | tf_op jit(solution)/shard_map/ppermute | solution.py:340

commit v2 on v1

--- a/solution.py
+++ b/solution.py
@@ -245,25 +245,26 @@
     iterates = [(grams[p] + degree * identity) * inverses[p : p + 1] for p in pairs]
     roots = [None for _ in pairs]
     for step in range(NS_STEPS):
-        for p in pairs:
-            iterate = split(iterates[p])
-            root = None if step == 0 else split(roots[p])
-            ahead = iterates[p] if step == 0 else product([root], right(iterates[p]))[0]
-            correction = 1.5 * identity - 0.5 * ahead
-            lefts = [split(sides[p])]
-            if step > 0:
-                lefts.append(root)
-            if step < NS_STEPS - 1:
-                lefts.append(iterate)
-            results = product(lefts, right(correction))
-            sides[p] = results[0]
-            roots[p] = correction if step == 0 else results[1]
-            if step < NS_STEPS - 1:
-                iterates[p] = results[-1]
-    mixings = []
-    for p in pairs:
-        weights = product([split(sides[p])], right(roots[p]))[0][:1] * inverses[p : p + 1]
-        mixings.append((spreads[p : p + 1] * roots[p] + weights).astype(bf16))
+        last = step == NS_STEPS - 1
+        iterate_halves = [split(iterates[p]) for p in pairs]
+        if step == 0:
+            ahead = iterates
+        else:
+            root_halves = [split(roots[p]) for p in pairs]
+            factors = [right(iterates[p]) for p in pairs]
+            ahead = [product([root_halves[p]], factors[p])[0] for p in pairs]
+        corrections = [1.5 * identity - 0.5 * ahead[p] for p in pairs]
+        factors = [right(corrections[p]) for p in pairs]
+        lefts = [
+            [split(sides[p])] + ([] if step == 0 else [root_halves[p]]) + ([] if last else [iterate_halves[p]]) for p in pairs
+        ]
+        results = [product(lefts[p], factors[p]) for p in pairs]
+        sides = [results[p][0] for p in pairs]
+        roots = corrections if step == 0 else [results[p][1] for p in pairs]
+        iterates = [results[p][-1] for p in pairs]
+    factors = [right(roots[p]) for p in pairs]
+    weights = [product([split(sides[p])], factors[p])[0][:1] * inverses[p : p + 1] for p in pairs]
+    mixings = [(spreads[p : p + 1] * roots[p] + weights[p]).astype(bf16) for p in pairs]
 
     patch = lax.broadcasted_iota(jnp.int32, (members, cols), 1) // PATCH
     masks = [jnp.where(patch % 4 == k, 1.0, 0.0).astype(bf16) for k in range(4)]

time: 25 us -> 23.6 us (0.944)
  Pallas kernels: 12 us -> 10.6 us
    pallas_call x1, Pallas kernels: 5.18 us -> 3.78 us  [shards(): call(finish_kernel, 'finish', [vmem] * 4, shape((1, members, tile_rows, c...]
  transfers between devices with their start and end apart: 5 -> 5, of which waited for: 3 -> 3; matrix products, arithmetic and copies ran while one was open for 7% -> 7% of each run, Pallas kernels for 28% -> 29%
where the time goes in v2:
time: 23.6 us; the launch traced here: 23.4 us
  Pallas kernels  10.6 us (45%)
  starting transfers between devices  6.79 us (29%)
  waiting for transfers between devices  3.2 us (14%)
  other arithmetic  1.57 us (7%)
  local copies, waits for them, and re-layouts  1.12 us (5%)
    pallas_call x1, Pallas kernels, shards(): call(finish_kernel, 'finish', [vmem] * 4, shape((1, members, tile_rows, c...  3.78 us
    ppermute x1, starting transfers between devices, shards(): lax.ppermute(forecast, 'lag', [((i + k) % shares, i) for i in range(share...  2.97 us
    pallas_call x1, Pallas kernels, shards(): call(own_kernel, 'own_gram', [vmem] * 5, own_shape)  2.46 us
    ppermute x2, starting transfers between devices, shards(): lax.ppermute(sent, axes, [(t, s) for s, t in pairs])  2.02 us
    pallas_call x1, Pallas kernels, shards(): call(functools.partial(first_kernel, shares), 'first_gram', [vmem] * (sha...  1.81 us
    ppermute x1, starting transfers between devices, shards(): first = lax.ppermute(message, axes, rings[0])  1.74 us
    ppermute x1, waiting for transfers between devices, shards(): second = lax.ppermute(message, axes, rings[1])  1.45 us
    ppermute x2, waiting for transfers between devices, shards(): lax.ppermute(sent, axes, [(t, s) for s, t in pairs])  1.4 us
  transfers between devices with their start and end apart: 5, of which 3 were waited for; matrix products, arithmetic and copies ran while one was open for 7% of the time, Pallas kernels for 29%

profile of v2, /device:TPU:0, one launch (start us, length us, event | category | flops | bytes accessed | tf_op | source)
XLA Modules:
  0.0 23.4 jit_solution(7070589784371391565)
XLA Ops:
  0.0 0.0 copy-start.4
  0.0 3.0 %collective-permute-start = (bf16[32,32,128]{2,1,0:T(8,128)(2,1)}, bf16[32,32,128]{2,1,0:T(8,128)(2,1)S(1)}, u32[]{:S(2)}, u32[]{:S(2)}) collective-permute-start(bf16[32,32,128]{2,1,0:T(8,128)(2,1)} %refs_0_.1), channel_id=1, source_target_pairs={{1,0},{0,1},{3,2},{2,3},{5,4},{4,5},{7,6},{6,7},{9,8},{8,9},{11,10... | collective-permute-start | bytes 786440 | tf_op jit(solution)/shard_map/ppermute | solution.py:311
  3.0 0.7 %multiply_divide_fusion = f32[16]{0:T(128)S(1)} fusion(s32[16]{0:T(128)} %param.13), kind=kLoop, calls=%fused_computation.5 | loop fusion | flops 48 | bytes 128 | tf_op jit(solution)/shard_map/div | solution.py:317
  3.6 0.0 copy-done.4
  3.6 0.0 copy-start.3
  3.6 0.8 %fusion.1 = (f32[16,256]{1,0:T(8,128)S(1)}, f32[16,256]{1,0:T(8,128)S(1)}) fusion(f32[16,256]{1,0:T(8,128)} %param.11, f32[16,256]{1,0:T(8,128)} %param.12, s32[16]{0:T(128)S(1)} %copy-done.4), kind=kLoop, calls=%fused_computation.6 | loop fusion | flops 12288 | bytes 65600 | tf_op jit(solution)/shard_map/mul | solution.py:315
  4.5 0.1 broadcast_in_dim.39
  4.5 0.0 copy-done.3
  4.6 0.1 select_select_fusion.table_ref
  4.6 0.1 broadcast_in_dim.40.inverse_ref
  4.7 0.0 collective-permute-start.1
  4.7 2.0 %collective-permute-start.3 = (f32[2,8,128]{2,1,0:T(8,128)S(1)}, f32[2,8,128]{2,1,0:T(8,128)S(1)}, u32[]{:S(2)}, u32[]{:S(2)}) collective-permute-start(f32[2,8,128]{2,1,0:T(8,128)S(1)} %broadcast_in_dim.40.inverse_ref), channel_id=1, source_target_pairs={{2,0},{0,1},{4,2},{1,3},{6,4},{3,5},{8,6},{5,7},{10,8},{7,9},{12,1... | collective-permute-start | bytes 24584 | tf_op jit(solution)/shard_map/ppermute | solution.py:322
  6.7 0.0 copy-start
  6.7 0.9 %copy-done = bf16[32,32,128]{2,1,0:T(8,128)(2,1)S(1)} copy-done((bf16[32,32,128]{2,1,0:T(8,128)(2,1)S(1)}, bf16[32,32,128]{2,1,0:T(8,128)(2,1)}, u32[]{:S(2)}) %copy-start) | copy-done | bytes 262168
  7.7 0.0 copy-start.1
  7.7 0.5 %fields.1 = (f32[2,32,128]{2,1,0:T(8,128)S(1)}, f32[32,128]{1,0:T(8,128)S(1)}) custom-call(f32[3,16,256]{2,1,0:T(8,128)S(1)} %select_select_fusion.table_ref, bf16[32,32,128]{2,1,0:T(8,128)(2,1)S(1)} %copy-done), custom_call_target="tpu_custom_call" | custom-call | tf_op jit(solution)/shard_map/fields/pallas_call | solution.py:323
  8.2 1.4 %collective-permute-done.1.refs_4_ = f32[2,8,128]{2,1,0:T(8,128)S(1)} collective-permute-done((f32[2,8,128]{2,1,0:T(8,128)S(1)}, f32[2,8,128]{2,1,0:T(8,128)S(1)}, u32[]{:S(2)}, u32[]{:S(2)}) %collective-permute-start.1) | collective-permute-done | bytes 8224 | tf_op jit(solution)/shard_map/ppermute | solution.py:322
  9.6 0.0 collective-permute-done.refs_1_
  9.6 0.0 copy-done.1
  9.6 0.0 copy-start.2
  9.6 1.8 %first_gram.1 = (bf16[32,64,128]{2,1,0:T(8,128)(2,1)S(1)}, f32[2,32,128]{2,1,0:T(8,128)S(1)}, bf16[528,128]{1,0:T(8,128)(2,1)S(1)}) custom-call(bf16[32,32,128]{2,1,0:T(8,128)(2,1)S(1)} %copy-done.1, bf16[32,32,128]{2,1,0:T(8,128)(2,1)S(1)} %collective-permute-done.refs_1_, f32[32,128]{1,0:T(8,128)S(1)} %get-tuple-element.15.refs_2_, ...), custom_call_target="tpu_custom_call" | custom-call | tf_op jit(solution)/shard_map/first_gram/pallas_call | solution.py:332
  11.4 1.7 %collective-permute-start.2 = (bf16[528,128]{1,0:T(8,128)(2,1)S(1)}, bf16[528,128]{1,0:T(8,128)(2,1)S(1)}, u32[]{:S(2)}, u32[]{:S(2)}) collective-permute-start(bf16[528,128]{1,0:T(8,128)(2,1)S(1)} %get-tuple-element.21), channel_id=1, source_target_pairs={{0,1},{1,3},{2,0},{3,5},{4,2},{5,7},{6,4},{7,9},{8,6},{9,11},{10,8... | collective-permute-start | bytes 405512 | tf_op jit(solution)/shard_map/ppermute | solution.py:339
  13.1 0.0 collective-permute-done.3.inverse_ref
  13.1 1.4 %second_gram.1 = bf16[528,128]{1,0:T(8,128)(2,1)S(1)} custom-call(bf16[32,64,128]{2,1,0:T(8,128)(2,1)S(1)} %get-tuple-element.20.rows_ref, f32[2,32,128]{2,1,0:T(8,128)S(1)} %get-tuple-element.18.after_ref.held_ref, f32[2,8,128]{2,1,0:T(8,128)S(1)} %collective-permute-done.3.inverse_ref), custom_call_target="tpu_custom_call" | custom-call | tf_op jit(solution)/shard_map/second_gram/pallas_call | solution.py:340
  14.5 0.1 collective-permute-start.4
  14.6 0.0 copy-done.2
  14.6 0.7 %state.1 = (bf16[32,64,128]{2,1,0:T(8,128)(2,1)S(1)}, f32[32,128]{1,0:T(8,128)S(1)}) custom-call(f32[2,32,128]{2,1,0:T(8,128)S(1)} %get-tuple-element.18.after_ref.held_ref, bf16[64,32,128]{2,1,0:T(8,128)(2,1)S(1)} %bitcast.1), custom_call_target="tpu_custom_call" | custom-call | tf_op jit(solution)/shard_map/state/pallas_call | solution.py:342
  15.3 0.3 %collective-permute-done.2.first_ref = bf16[528,128]{1,0:T(8,128)(2,1)S(1)} collective-permute-done((bf16[528,128]{1,0:T(8,128)(2,1)S(1)}, bf16[528,128]{1,0:T(8,128)(2,1)S(1)}, u32[]{:S(2)}, u32[]{:S(2)}) %collective-permute-start.2) | collective-permute-done | bytes 135200 | tf_op jit(solution)/shard_map/ppermute | solution.py:339
  15.7 2.5 %own_gram.1.total_ref = f32[520,128]{1,0:T(8,128)S(1)} custom-call(f32[32,128]{1,0:T(8,128)S(1)} %get-tuple-element.19.after_ref.mean_ref, bf16[32,64,128]{2,1,0:T(8,128)(2,1)S(1)} %get-tuple-element.20.rows_ref, f32[2,32,128]{2,1,0:T(8,128)S(1)} %get-tuple-element.18.after_ref.held_ref, f32[2,8,128]{2,1,0:T(8,128)S(1)} %broadcast_in_dim.40.inverse_ref, ...), custom_call_target="tpu_custom_call" | custom-call | tf_op jit(solution)/shard_map/own_gram/pallas_call | solution.py:350
  18.2 1.4 %collective-permute-done.4.second_ref = bf16[528,128]{1,0:T(8,128)(2,1)S(1)} collective-permute-done((bf16[528,128]{1,0:T(8,128)(2,1)S(1)}, bf16[528,128]{1,0:T(8,128)(2,1)S(1)}, u32[]{:S(2)}, u32[]{:S(2)}) %collective-permute-start.4) | collective-permute-done | bytes 135200 | tf_op jit(solution)/shard_map/ppermute | solution.py:341
  19.6 3.8 %finish.1 = bf16[1,64,32,128]{3,2,1,0:T(8,128)(2,1)} custom-call(f32[520,128]{1,0:T(8,128)S(1)} %own_gram.1.total_ref, bf16[528,128]{1,0:T(8,128)(2,1)S(1)} %collective-permute-done.4.second_ref, bf16[32,64,128]{2,1,0:T(8,128)(2,1)S(1)} %get-tuple-element.22.lag_ref, f32[32,128]{1,0:T(8,128)S(1)} %get-tuple-element.19.after_ref.mean_ref), custom_call_target="tpu_custom_call" | custom-call | tf_op jit(solution)/shard_map/finish/pallas_call | solution.py:351
  (2 shorter events, 0.0 us)
Async XLA Ops:
  0.0 3.6 %copy-start.4 = (s32[16]{0:T(128)S(1)}, s32[16]{0:T(128)}, u32[]{:S(2)}) copy-start(s32[16]{0:T(128)} %param.10) | copy-start | bytes 196
  0.0 9.6 %collective-permute-start = (bf16[32,32,128]{2,1,0:T(8,128)(2,1)}, bf16[32,32,128]{2,1,0:T(8,128)(2,1)S(1)}, u32[]{:S(2)}, u32[]{:S(2)}) collective-permute-start(bf16[32,32,128]{2,1,0:T(8,128)(2,1)} %refs_0_.1), channel_id=1, source_target_pairs={{1,0},{0,1},{3,2},{2,3},{5,4},{4,5},{7,6},{6,7},{9,8},{8,9},{11,10... | collective-permute-start | bytes 786440 | tf_op jit(solution)/shard_map/ppermute | solution.py:311
  3.6 0.9 %copy-start.3 = (s32[16,256]{1,0:T(8,128)S(1)}, s32[16,256]{1,0:T(8,128)}, u32[]{:S(2)}) copy-start(s32[16,256]{1,0:T(8,128)} %param.9) | copy-start | bytes 49156
  4.7 4.9 %collective-permute-start.1 = (f32[2,8,128]{2,1,0:T(8,128)S(1)}, f32[2,8,128]{2,1,0:T(8,128)S(1)}, u32[]{:S(2)}, u32[]{:S(2)}) collective-permute-start(f32[2,8,128]{2,1,0:T(8,128)S(1)} %broadcast_in_dim.40.inverse_ref), channel_id=1, source_target_pairs={{1,0},{3,1},{0,2},{5,3},{2,4},{7,5},{4,6},{9,7},{6,8},{11,9},{8,10... | collective-permute-start | bytes 24584 | tf_op jit(solution)/shard_map/ppermute | solution.py:322
  4.7 8.4 %collective-permute-start.3 = (f32[2,8,128]{2,1,0:T(8,128)S(1)}, f32[2,8,128]{2,1,0:T(8,128)S(1)}, u32[]{:S(2)}, u32[]{:S(2)}) collective-permute-start(f32[2,8,128]{2,1,0:T(8,128)S(1)} %broadcast_in_dim.40.inverse_ref), channel_id=1, source_target_pairs={{2,0},{0,1},{4,2},{1,3},{6,4},{3,5},{8,6},{5,7},{10,8},{7,9},{12,1... | collective-permute-start | bytes 24584 | tf_op jit(solution)/shard_map/ppermute | solution.py:322
  6.7 0.9 %copy-start = (bf16[32,32,128]{2,1,0:T(8,128)(2,1)S(1)}, bf16[32,32,128]{2,1,0:T(8,128)(2,1)}, u32[]{:S(2)}) copy-start(bf16[32,32,128]{2,1,0:T(8,128)(2,1)} %refs_0_.1) | copy-start | bytes 786436
  7.7 1.9 %copy-start.1 = (bf16[32,32,128]{2,1,0:T(8,128)(2,1)S(1)}, bf16[32,32,128]{2,1,0:T(8,128)(2,1)}, u32[]{:S(2)}) copy-start(bf16[32,32,128]{2,1,0:T(8,128)(2,1)} %refs_0_.1) | copy-start | bytes 786436
  9.6 5.0 %copy-start.2 = (bf16[1,64,32,128]{3,2,1,0:T(8,128)(2,1)S(1)}, bf16[1,64,32,128]{3,2,1,0:T(8,128)(2,1)}, u32[]{:S(2)}) copy-start(bf16[1,64,32,128]{3,2,1,0:T(8,128)(2,1)} %param.7) | copy-start | bytes 1572868
  11.4 4.3 %collective-permute-start.2 = (bf16[528,128]{1,0:T(8,128)(2,1)S(1)}, bf16[528,128]{1,0:T(8,128)(2,1)S(1)}, u32[]{:S(2)}, u32[]{:S(2)}) collective-permute-start(bf16[528,128]{1,0:T(8,128)(2,1)S(1)} %get-tuple-element.21), channel_id=1, source_target_pairs={{0,1},{1,3},{2,0},{3,5},{4,2},{5,7},{6,4},{7,9},{8,6},{9,11},{10,8... | collective-permute-start | bytes 405512 | tf_op jit(solution)/shard_map/ppermute | solution.py:339
  14.5 5.1 %collective-permute-start.4 = (bf16[528,128]{1,0:T(8,128)(2,1)S(1)}, bf16[528,128]{1,0:T(8,128)(2,1)S(1)}, u32[]{:S(2)}, u32[]{:S(2)}) collective-permute-start(bf16[528,128]{1,0:T(8,128)(2,1)S(1)} %second_gram.1), channel_id=1, source_target_pairs={{0,2},{1,0},{2,4},{3,1},{4,6},{5,3},{6,8},{7,5},{8,10},{9,7},{10,1... | collective-permute-start | bytes 405512 | tf_op jit(solution)/shard_map/ppermute | solution.py:341

commit v3 on v2

--- a/solution.py
+++ b/solution.py
@@ -113,7 +113,7 @@
     return total + mm(jnp.concatenate(lefts, 1), jnp.concatenate(anomalies, 1), NT)
 
 
-STEP = 8
+STEP = 4
 
 
 def paired(totals, members, patch_cols):
@@ -155,10 +155,12 @@
         taper_plan(middle, inverse_ref[1 - down]),
         taper_plan(middle + jnp.where(down == 0, -PATCH, PATCH).astype(f32), inverse_ref[down]),
     ]
-    anomalies = [rows_ref[near + i] for i in range(NEAR)]
-    fields = [held_ref[k, pl.ds(near, NEAR), :] for k in range(2)]
-    blank = jnp.zeros(total_ref.shape[1:], f32)
-    totals = [accumulate(blank, plan, anomalies, *fields, near) for plan in plans]
+    totals = [jnp.zeros(total_ref.shape[1:], f32) for _ in plans]
+    near_fields = [held_ref[k, pl.ds(near, NEAR), :] for k in range(2)]
+    for start in range(0, NEAR, STEP):
+        anomalies = [rows_ref[near + start + i] for i in range(STEP)]
+        fields = [field[start : start + STEP] for field in near_fields]
+        totals = [accumulate(total, plan, anomalies, *fields, near + start) for total, plan in zip(totals, plans)]
     for start in range(NEAR, FAR, STEP):
         anomalies = [rows_ref[start + i] for i in range(STEP)]
         fields = [held_ref[k, start : start + STEP, :] for k in range(2)]
@@ -215,20 +217,31 @@
     left_mask = jnp.where(lane < members, 1.0, 0.0).astype(bf16)
     right_mask = jnp.where(lane < members, 0.0, 1.0).astype(bf16)
 
-    def right(y):
-        halves = split(y)
-        return jnp.concatenate(
-            [jnp.concatenate([half * mask for half in halves], 1) for mask in (left_mask, right_mask)], 0
-        )
-
-    def product(lefts, factor):
-        both = mm(jnp.concatenate([half for halves in lefts for half in halves], 0), factor)
-        results, at = [], 0
-        for high, low in lefts:
-            rows = high.shape[0]
-            upper, lower = both[at : at + rows], both[at + rows : at + 2 * rows]
-            results.append(upper[:, :cols] + (upper[:, cols:] + lower[:, :cols]))
-            at += 2 * rows
+    def splits(parts):
+        highs = [part.astype(bf16) for part in parts]
+        rests = [part - high.astype(f32) for part, high in zip(parts, highs)]
+        return list(zip(highs, [rest.astype(bf16) for rest in rests]))
+
+    def rights(parts):
+        return [
+            jnp.concatenate(
+                [jnp.concatenate([half * mask for half in halves], 1) for mask in (left_mask, right_mask)], 0
+            )
+            for halves in splits(parts)
+        ]
+
+    def products(lefts, factors):
+        stacks = [jnp.concatenate([half for halves in left for half in halves], 0) for left in lefts]
+        boths = [mm(stack, factor) for stack, factor in zip(stacks, factors)]
+        results = []
+        for left, both in zip(lefts, boths):
+            parts, at = [], 0
+            for high, low in left:
+                rows = high.shape[0]
+                upper, lower = both[at : at + rows], both[at + rows : at + 2 * rows]
+                parts.append(upper[:, :cols] + (upper[:, cols:] + lower[:, :cols]))
+                at += 2 * rows
+            results.append(parts)
         return results
 
     total = total_ref[...] + arrived(second_ref, 1, pair_count)
@@ -245,25 +258,22 @@
     iterates = [(grams[p] + degree * identity) * inverses[p : p + 1] for p in pairs]
     roots = [None for _ in pairs]
     for step in range(NS_STEPS):
-        last = step == NS_STEPS - 1
-        iterate_halves = [split(iterates[p]) for p in pairs]
+        lefts = [[halves] for halves in splits(sides)]
         if step == 0:
             ahead = iterates
         else:
-            root_halves = [split(roots[p]) for p in pairs]
-            factors = [right(iterates[p]) for p in pairs]
-            ahead = [product([root_halves[p]], factors[p])[0] for p in pairs]
-        corrections = [1.5 * identity - 0.5 * ahead[p] for p in pairs]
-        factors = [right(corrections[p]) for p in pairs]
-        lefts = [
-            [split(sides[p])] + ([] if step == 0 else [root_halves[p]]) + ([] if last else [iterate_halves[p]]) for p in pairs
-        ]
-        results = [product(lefts[p], factors[p]) for p in pairs]
-        sides = [results[p][0] for p in pairs]
-        roots = corrections if step == 0 else [results[p][1] for p in pairs]
-        iterates = [results[p][-1] for p in pairs]
-    factors = [right(roots[p]) for p in pairs]
-    weights = [product([split(sides[p])], factors[p])[0][:1] * inverses[p : p + 1] for p in pairs]
+            root_halves = splits(roots)
+            lefts = [left + [halves] for left, halves in zip(lefts, root_halves)]
+            ahead = [parts[0] for parts in products([[halves] for halves in root_halves], rights(iterates))]
+        if step < NS_STEPS - 1:
+            lefts = [left + [halves] for left, halves in zip(lefts, splits(iterates))]
+        corrections = [1.5 * identity - 0.5 * product for product in ahead]
+        results = products(lefts, rights(corrections))
+        sides = [parts[0] for parts in results]
+        roots = corrections if step == 0 else [parts[1] for parts in results]
+        iterates = [parts[-1] for parts in results]
+    weights = [parts[0][:1] for parts in products([[halves] for halves in splits(sides)], rights(roots))]
+    weights = [weights[p] * inverses[p : p + 1] for p in pairs]
     mixings = [(spreads[p : p + 1] * roots[p] + weights[p]).astype(bf16) for p in pairs]
 
     patch = lax.broadcasted_iota(jnp.int32, (members, cols), 1) // PATCH

time: 23.6 us -> 23.8 us (level)
  transfers between devices with their start and end apart: 5 -> 5, of which waited for: 3 -> 3; matrix products, arithmetic and copies ran while one was open for 7% -> 7% of each run, Pallas kernels for 29% -> 30%
where the time goes in v3:
time: 23.8 us; the launch traced here: 23.6 us
  Pallas kernels  10.8 us (45%)
  starting transfers between devices  6.77 us (28%)
  waiting for transfers between devices  3.2 us (13%)
  other arithmetic  1.57 us (7%)
  local copies, waits for them, and re-layouts  1.12 us (5%)
    pallas_call x1, Pallas kernels, shards(): call(finish_kernel, 'finish', [vmem] * 4, shape((1, members, tile_rows, c...  3.78 us
    ppermute x1, starting transfers between devices, shards(): lax.ppermute(forecast, 'lag', [((i + k) % shares, i) for i in range(share...  2.97 us
    pallas_call x1, Pallas kernels, shards(): call(own_kernel, 'own_gram', [vmem] * 5, own_shape)  2.45 us
    ppermute x2, starting transfers between devices, shards(): lax.ppermute(sent, axes, [(t, s) for s, t in pairs])  2.02 us
    pallas_call x1, Pallas kernels, shards(): call(functools.partial(first_kernel, shares), 'first_gram', [vmem] * (sha...  2 us
    ppermute x1, starting transfers between devices, shards(): first = lax.ppermute(message, axes, rings[0])  1.72 us
    ppermute x1, waiting for transfers between devices, shards(): second = lax.ppermute(message, axes, rings[1])  1.47 us
    pallas_call x1, Pallas kernels, shards(): call(second_kernel, 'second_gram', [vmem] * 3, message_shape, [total_scra...  1.41 us
  transfers between devices with their start and end apart: 5, of which 3 were waited for; matrix products, arithmetic and copies ran while one was open for 7% of the time, Pallas kernels for 30%

profile of v3, /device:TPU:0, one launch (start us, length us, event | category | flops | bytes accessed | tf_op | source)
XLA Modules:
  0.0 23.6 jit_solution(12579905639481366689)
XLA Ops:
  0.0 0.0 copy-start.4
  0.0 3.0 %collective-permute-start = (bf16[32,32,128]{2,1,0:T(8,128)(2,1)}, bf16[32,32,128]{2,1,0:T(8,128)(2,1)S(1)}, u32[]{:S(2)}, u32[]{:S(2)}) collective-permute-start(bf16[32,32,128]{2,1,0:T(8,128)(2,1)} %refs_0_.1), channel_id=1, source_target_pairs={{1,0},{0,1},{3,2},{2,3},{5,4},{4,5},{7,6},{6,7},{9,8},{8,9},{11,10... | collective-permute-start | bytes 786440 | tf_op jit(solution)/shard_map/ppermute | solution.py:321
  3.0 0.7 %multiply_divide_fusion = f32[16]{0:T(128)S(1)} fusion(s32[16]{0:T(128)} %param.13), kind=kLoop, calls=%fused_computation.5 | loop fusion | flops 48 | bytes 128 | tf_op jit(solution)/shard_map/div | solution.py:327
  3.6 0.0 copy-done.4
  3.6 0.0 copy-start.3
  3.6 0.8 %fusion.1 = (f32[16,256]{1,0:T(8,128)S(1)}, f32[16,256]{1,0:T(8,128)S(1)}) fusion(f32[16,256]{1,0:T(8,128)} %param.11, f32[16,256]{1,0:T(8,128)} %param.12, s32[16]{0:T(128)S(1)} %copy-done.4), kind=kLoop, calls=%fused_computation.6 | loop fusion | flops 12288 | bytes 65600 | tf_op jit(solution)/shard_map/mul | solution.py:325
  4.5 0.1 broadcast_in_dim.39
  4.5 0.0 copy-done.3
  4.6 0.1 select_select_fusion.table_ref
  4.6 0.1 broadcast_in_dim.40.inverse_ref
  4.7 0.0 collective-permute-start.1
  4.7 2.0 %collective-permute-start.3 = (f32[2,8,128]{2,1,0:T(8,128)S(1)}, f32[2,8,128]{2,1,0:T(8,128)S(1)}, u32[]{:S(2)}, u32[]{:S(2)}) collective-permute-start(f32[2,8,128]{2,1,0:T(8,128)S(1)} %broadcast_in_dim.40.inverse_ref), channel_id=1, source_target_pairs={{2,0},{0,1},{4,2},{1,3},{6,4},{3,5},{8,6},{5,7},{10,8},{7,9},{12,1... | collective-permute-start | bytes 24584 | tf_op jit(solution)/shard_map/ppermute | solution.py:332
  6.7 0.0 copy-start
  6.7 0.9 %copy-done = bf16[32,32,128]{2,1,0:T(8,128)(2,1)S(1)} copy-done((bf16[32,32,128]{2,1,0:T(8,128)(2,1)S(1)}, bf16[32,32,128]{2,1,0:T(8,128)(2,1)}, u32[]{:S(2)}) %copy-start) | copy-done | bytes 262168
  7.7 0.0 copy-start.1
  7.7 0.5 %fields.1 = (f32[2,32,128]{2,1,0:T(8,128)S(1)}, f32[32,128]{1,0:T(8,128)S(1)}) custom-call(f32[3,16,256]{2,1,0:T(8,128)S(1)} %select_select_fusion.table_ref, bf16[32,32,128]{2,1,0:T(8,128)(2,1)S(1)} %copy-done), custom_call_target="tpu_custom_call" | custom-call | tf_op jit(solution)/shard_map/fields/pallas_call | solution.py:333
  8.2 1.4 %collective-permute-done.1.refs_4_ = f32[2,8,128]{2,1,0:T(8,128)S(1)} collective-permute-done((f32[2,8,128]{2,1,0:T(8,128)S(1)}, f32[2,8,128]{2,1,0:T(8,128)S(1)}, u32[]{:S(2)}, u32[]{:S(2)}) %collective-permute-start.1) | collective-permute-done | bytes 8224 | tf_op jit(solution)/shard_map/ppermute | solution.py:332
  9.6 0.0 collective-permute-done.refs_1_
  9.6 0.0 copy-done.1
  9.6 0.0 copy-start.2
  9.6 2.0 %first_gram.1 = (bf16[32,64,128]{2,1,0:T(8,128)(2,1)S(1)}, f32[2,32,128]{2,1,0:T(8,128)S(1)}, bf16[528,128]{1,0:T(8,128)(2,1)S(1)}) custom-call(bf16[32,32,128]{2,1,0:T(8,128)(2,1)S(1)} %copy-done.1, bf16[32,32,128]{2,1,0:T(8,128)(2,1)S(1)} %collective-permute-done.refs_1_, f32[32,128]{1,0:T(8,128)S(1)} %get-tuple-element.15.refs_2_, ...), custom_call_target="tpu_custom_call" | custom-call | tf_op jit(solution)/shard_map/first_gram/pallas_call | solution.py:342
  11.6 1.7 %collective-permute-start.2 = (bf16[528,128]{1,0:T(8,128)(2,1)S(1)}, bf16[528,128]{1,0:T(8,128)(2,1)S(1)}, u32[]{:S(2)}, u32[]{:S(2)}) collective-permute-start(bf16[528,128]{1,0:T(8,128)(2,1)S(1)} %get-tuple-element.21), channel_id=1, source_target_pairs={{0,1},{1,3},{2,0},{3,5},{4,2},{5,7},{6,4},{7,9},{8,6},{9,11},{10,8... | collective-permute-start | bytes 405512 | tf_op jit(solution)/shard_map/ppermute | solution.py:349
  13.3 0.0 collective-permute-done.3.inverse_ref
  13.3 1.4 %second_gram.1 = bf16[528,128]{1,0:T(8,128)(2,1)S(1)} custom-call(bf16[32,64,128]{2,1,0:T(8,128)(2,1)S(1)} %get-tuple-element.20.rows_ref, f32[2,32,128]{2,1,0:T(8,128)S(1)} %get-tuple-element.18.after_ref.held_ref, f32[2,8,128]{2,1,0:T(8,128)S(1)} %collective-permute-done.3.inverse_ref), custom_call_target="tpu_custom_call" | custom-call | tf_op jit(solution)/shard_map/second_gram/pallas_call | solution.py:350
  14.7 0.1 collective-permute-start.4
  14.8 0.0 copy-done.2
  14.8 0.7 %state.1 = (bf16[32,64,128]{2,1,0:T(8,128)(2,1)S(1)}, f32[32,128]{1,0:T(8,128)S(1)}) custom-call(f32[2,32,128]{2,1,0:T(8,128)S(1)} %get-tuple-element.18.after_ref.held_ref, bf16[64,32,128]{2,1,0:T(8,128)(2,1)S(1)} %bitcast.1), custom_call_target="tpu_custom_call" | custom-call | tf_op jit(solution)/shard_map/state/pallas_call | solution.py:352
  15.5 0.3 %collective-permute-done.2.first_ref = bf16[528,128]{1,0:T(8,128)(2,1)S(1)} collective-permute-done((bf16[528,128]{1,0:T(8,128)(2,1)S(1)}, bf16[528,128]{1,0:T(8,128)(2,1)S(1)}, u32[]{:S(2)}, u32[]{:S(2)}) %collective-permute-start.2) | collective-permute-done | bytes 135200 | tf_op jit(solution)/shard_map/ppermute | solution.py:349
  15.9 2.5 %own_gram.1.total_ref = f32[520,128]{1,0:T(8,128)S(1)} custom-call(f32[32,128]{1,0:T(8,128)S(1)} %get-tuple-element.19.after_ref.mean_ref, bf16[32,64,128]{2,1,0:T(8,128)(2,1)S(1)} %get-tuple-element.20.rows_ref, f32[2,32,128]{2,1,0:T(8,128)S(1)} %get-tuple-element.18.after_ref.held_ref, f32[2,8,128]{2,1,0:T(8,128)S(1)} %broadcast_in_dim.40.inverse_ref, ...), custom_call_target="tpu_custom_call" | custom-call | tf_op jit(solution)/shard_map/own_gram/pallas_call | solution.py:360
  18.3 1.5 %collective-permute-done.4.second_ref = bf16[528,128]{1,0:T(8,128)(2,1)S(1)} collective-permute-done((bf16[528,128]{1,0:T(8,128)(2,1)S(1)}, bf16[528,128]{1,0:T(8,128)(2,1)S(1)}, u32[]{:S(2)}, u32[]{:S(2)}) %collective-permute-start.4) | collective-permute-done | bytes 135200 | tf_op jit(solution)/shard_map/ppermute | solution.py:351
  19.8 3.8 %finish.1 = bf16[1,64,32,128]{3,2,1,0:T(8,128)(2,1)} custom-call(f32[520,128]{1,0:T(8,128)S(1)} %own_gram.1.total_ref, bf16[528,128]{1,0:T(8,128)(2,1)S(1)} %collective-permute-done.4.second_ref, bf16[32,64,128]{2,1,0:T(8,128)(2,1)S(1)} %get-tuple-element.22.lag_ref, f32[32,128]{1,0:T(8,128)S(1)} %get-tuple-element.19.after_ref.mean_ref), custom_call_target="tpu_custom_call" | custom-call | tf_op jit(solution)/shard_map/finish/pallas_call | solution.py:361
  (2 shorter events, 0.0 us)
Async XLA Ops:
  0.0 3.6 %copy-start.4 = (s32[16]{0:T(128)S(1)}, s32[16]{0:T(128)}, u32[]{:S(2)}) copy-start(s32[16]{0:T(128)} %param.10) | copy-start | bytes 196
  0.0 9.6 %collective-permute-start = (bf16[32,32,128]{2,1,0:T(8,128)(2,1)}, bf16[32,32,128]{2,1,0:T(8,128)(2,1)S(1)}, u32[]{:S(2)}, u32[]{:S(2)}) collective-permute-start(bf16[32,32,128]{2,1,0:T(8,128)(2,1)} %refs_0_.1), channel_id=1, source_target_pairs={{1,0},{0,1},{3,2},{2,3},{5,4},{4,5},{7,6},{6,7},{9,8},{8,9},{11,10... | collective-permute-start | bytes 786440 | tf_op jit(solution)/shard_map/ppermute | solution.py:321
  3.6 0.9 %copy-start.3 = (s32[16,256]{1,0:T(8,128)S(1)}, s32[16,256]{1,0:T(8,128)}, u32[]{:S(2)}) copy-start(s32[16,256]{1,0:T(8,128)} %param.9) | copy-start | bytes 49156
  4.7 4.9 %collective-permute-start.1 = (f32[2,8,128]{2,1,0:T(8,128)S(1)}, f32[2,8,128]{2,1,0:T(8,128)S(1)}, u32[]{:S(2)}, u32[]{:S(2)}) collective-permute-start(f32[2,8,128]{2,1,0:T(8,128)S(1)} %broadcast_in_dim.40.inverse_ref), channel_id=1, source_target_pairs={{1,0},{3,1},{0,2},{5,3},{2,4},{7,5},{4,6},{9,7},{6,8},{11,9},{8,10... | collective-permute-start | bytes 24584 | tf_op jit(solution)/shard_map/ppermute | solution.py:332
  4.7 8.6 %collective-permute-start.3 = (f32[2,8,128]{2,1,0:T(8,128)S(1)}, f32[2,8,128]{2,1,0:T(8,128)S(1)}, u32[]{:S(2)}, u32[]{:S(2)}) collective-permute-start(f32[2,8,128]{2,1,0:T(8,128)S(1)} %broadcast_in_dim.40.inverse_ref), channel_id=1, source_target_pairs={{2,0},{0,1},{4,2},{1,3},{6,4},{3,5},{8,6},{5,7},{10,8},{7,9},{12,1... | collective-permute-start | bytes 24584 | tf_op jit(solution)/shard_map/ppermute | solution.py:332
  6.7 0.9 %copy-start = (bf16[32,32,128]{2,1,0:T(8,128)(2,1)S(1)}, bf16[32,32,128]{2,1,0:T(8,128)(2,1)}, u32[]{:S(2)}) copy-start(bf16[32,32,128]{2,1,0:T(8,128)(2,1)} %refs_0_.1) | copy-start | bytes 786436
  7.7 1.9 %copy-start.1 = (bf16[32,32,128]{2,1,0:T(8,128)(2,1)S(1)}, bf16[32,32,128]{2,1,0:T(8,128)(2,1)}, u32[]{:S(2)}) copy-start(bf16[32,32,128]{2,1,0:T(8,128)(2,1)} %refs_0_.1) | copy-start | bytes 786436
  9.6 5.2 %copy-start.2 = (bf16[1,64,32,128]{3,2,1,0:T(8,128)(2,1)S(1)}, bf16[1,64,32,128]{3,2,1,0:T(8,128)(2,1)}, u32[]{:S(2)}) copy-start(bf16[1,64,32,128]{3,2,1,0:T(8,128)(2,1)} %param.7) | copy-start | bytes 1572868
  11.6 4.3 %collective-permute-start.2 = (bf16[528,128]{1,0:T(8,128)(2,1)S(1)}, bf16[528,128]{1,0:T(8,128)(2,1)S(1)}, u32[]{:S(2)}, u32[]{:S(2)}) collective-permute-start(bf16[528,128]{1,0:T(8,128)(2,1)S(1)} %get-tuple-element.21), channel_id=1, source_target_pairs={{0,1},{1,3},{2,0},{3,5},{4,2},{5,7},{6,4},{7,9},{8,6},{9,11},{10,8... | collective-permute-start | bytes 405512 | tf_op jit(solution)/shard_map/ppermute | solution.py:349
  14.7 5.1 %collective-permute-start.4 = (bf16[528,128]{1,0:T(8,128)(2,1)S(1)}, bf16[528,128]{1,0:T(8,128)(2,1)S(1)}, u32[]{:S(2)}, u32[]{:S(2)}) collective-permute-start(bf16[528,128]{1,0:T(8,128)(2,1)S(1)} %second_gram.1), channel_id=1, source_target_pairs={{0,2},{1,0},{2,4},{3,1},{4,6},{5,3},{6,8},{7,5},{8,10},{9,7},{10,1... | collective-permute-start | bytes 405512 | tf_op jit(solution)/shard_map/ppermute | solution.py:351

commit v4 on v3

--- a/solution.py
+++ b/solution.py
@@ -113,7 +113,7 @@
     return total + mm(jnp.concatenate(lefts, 1), jnp.concatenate(anomalies, 1), NT)
 
 
-STEP = 4
+STEP = 8
 
 
 def paired(totals, members, patch_cols):
@@ -145,63 +145,96 @@
     return jnp.where(there, read_message(ref, side_count), 0.0)
 
 
-def outward(turn, rows_ref, held_ref, inverse_ref, message_ref, total_ref):
-    tile_rows, members, cols = rows_ref.shape
+def outward(down, near_rows, near_fields, far_rows, far_fields, tile_rows, inverse_ref, message_ref, total_ref):
+    members, cols = near_rows[0].shape
     patch_cols = cols // PATCH
-    down = half_of_lags() ^ turn
-    near = pl.multiple_of(down * (tile_rows - NEAR), 8)
     middle = jnp.where(down == 0, MIDDLE - PATCH, MIDDLE + tile_rows)
     plans = [
         taper_plan(middle, inverse_ref[1 - down]),
         taper_plan(middle + jnp.where(down == 0, -PATCH, PATCH).astype(f32), inverse_ref[down]),
     ]
-    totals = [jnp.zeros(total_ref.shape[1:], f32) for _ in plans]
-    near_fields = [held_ref[k, pl.ds(near, NEAR), :] for k in range(2)]
-    for start in range(0, NEAR, STEP):
-        anomalies = [rows_ref[near + start + i] for i in range(STEP)]
-        fields = [field[start : start + STEP] for field in near_fields]
-        totals = [accumulate(total, plan, anomalies, *fields, near + start) for total, plan in zip(totals, plans)]
-    for start in range(NEAR, FAR, STEP):
-        anomalies = [rows_ref[start + i] for i in range(STEP)]
-        fields = [held_ref[k, start : start + STEP, :] for k in range(2)]
-        totals[0] = accumulate(totals[0], plans[0], anomalies, *fields, jnp.int32(start))
+    blank = jnp.zeros(total_ref.shape[1:], f32)
+    near = down * (tile_rows - NEAR)
+    totals = [accumulate(blank, plan, near_rows, *near_fields, near) for plan in plans]
+    for start in range(0, FAR - NEAR, STEP):
+        rows = slice(start, start + STEP)
+        totals[0] = accumulate(
+            totals[0], plans[0], far_rows[rows], *[field[rows] for field in far_fields], jnp.int32(NEAR + start)
+        )
     total_ref[1 - down] = totals[0]
     total_ref[down] = totals[1]
     message_ref[...] = message_of(*paired([total_ref[0], total_ref[1]], members, patch_cols))
 
 
+def centre(first, parts, sum_ref, field_ref, held_ref, rows_ref, flat_ref):
+    count, members, cols = rows_ref.shape
+    tile_rows = parts[0].shape[1]
+    shares = len(parts)
+    share_members = members // shares
+    lag = lax.axis_index("lag")
+    late = tile_rows - count
+    whole = parts[0][...].astype(f32)
+    states = [jnp.where(first == 0, whole[:, :count], whole[:, late:])] + [part[...].astype(f32) for part in parts[1:]]
+    run = pl.ds(pl.multiple_of(first, 8), count)
+    mean = functools.reduce(jnp.add, [jnp.sum(state, axis=0) for state in states[1:]], sum_ref[run, :]) / members
+    for k, state in enumerate(states):
+        at = pl.multiple_of(lax.rem(lag + k, shares) * (share_members * count), 8)
+        flat_ref[pl.ds(at, share_members * count), :] = (state - mean[None]).reshape(-1, cols)
+    weight = field_ref[0, run, :]
+    held_ref[0] = weight
+    held_ref[1] = field_ref[1, run, :] - mean * weight
+    for r in range(count):
+        rows_ref[r] = flat_ref[pl.ds(r, members, stride=count), :].astype(bf16)
+
+
+def far_run(down, rows_ref, held_ref):
+    at = pl.multiple_of((1 - down) * NEAR, 8)
+    rows = [rows_ref[at + i] for i in range(FAR - NEAR)]
+    return rows, [held_ref[k, pl.ds(at, FAR - NEAR), :] for k in range(2)]
+
+
 def first_kernel(shares, *refs):
     parts, refs = refs[:shares], refs[shares:]
     sum_ref, field_ref, inverse_ref, rows_ref, held_ref, message_ref, flat_ref, total_ref = refs
-    share_members, tile_rows, cols = parts[0].shape
-    members = share_members * shares
-    lag = lax.axis_index("lag")
-    states = [part[...].astype(f32) for part in parts]
-    mean = functools.reduce(jnp.add, [jnp.sum(state, axis=0) for state in states[1:]], sum_ref[...]) / members
-    for k, state in enumerate(states):
-        at = pl.multiple_of(lax.rem(lag + k, shares) * (share_members * tile_rows), 8)
-        flat_ref[pl.ds(at, share_members * tile_rows), :] = (state - mean[None]).reshape(-1, cols)
-    weight = field_ref[0]
-    held_ref[0] = weight
-    held_ref[1] = field_ref[1] - mean * weight
-    for r in range(tile_rows):
-        rows_ref[r] = flat_ref[pl.ds(r, members, stride=tile_rows), :].astype(bf16)
-    outward(0, rows_ref, held_ref, inverse_ref, message_ref, total_ref)
-
-
-def second_kernel(rows_ref, held_ref, inverse_ref, message_ref, total_ref):
-    outward(1, rows_ref, held_ref, inverse_ref, message_ref, total_ref)
-
-
-def own_kernel(after_ref, rows_ref, held_ref, inverse_ref, first_ref, out_ref):
-    tile_rows, members, cols = rows_ref.shape
-    patch_cols = cols // PATCH
-    plans = [taper_plan(MIDDLE + a * PATCH, inverse_ref[a]) for a in range(tile_rows // PATCH)]
+    down = half_of_lags()
+    tile_rows = parts[0].shape[1]
+    centre(down * (tile_rows - FAR), parts, sum_ref, field_ref, held_ref, rows_ref, flat_ref)
+    at = pl.multiple_of(down * (FAR - NEAR), 8)
+    near_rows = [rows_ref[at + i] for i in range(NEAR)]
+    near_fields = [held_ref[k, pl.ds(at, NEAR), :] for k in range(2)]
+    outward(
+        down, near_rows, near_fields, *far_run(down, rows_ref, held_ref), tile_rows, inverse_ref, message_ref, total_ref
+    )
+
+
+def second_kernel(shares, *refs):
+    parts, refs = refs[:shares], refs[shares:]
+    sum_ref, field_ref, most_ref, most_held_ref, inverse_ref, rows_ref, held_ref, message_ref, flat_ref, total_ref = refs
+    down = half_of_lags()
+    tile_rows = parts[0].shape[1]
+    centre((1 - down) * (tile_rows - NEAR), parts, sum_ref, field_ref, held_ref, rows_ref, flat_ref)
+    near_rows = [rows_ref[i] for i in range(NEAR)]
+    near_fields = [held_ref[k] for k in range(2)]
+    outward(
+        1 - down, near_rows, near_fields, *far_run(down, most_ref, most_held_ref), tile_rows, inverse_ref, message_ref, total_ref
+    )
+
+
+def own_kernel(after_ref, most_ref, most_held_ref, rest_ref, rest_held_ref, inverse_ref, first_ref, out_ref):
+    members, cols = most_ref.shape[1:]
+    patch_rows, patch_cols = inverse_ref.shape[:2]
+    down = half_of_lags()
+    plans = [taper_plan(MIDDLE + a * PATCH, inverse_ref[a]) for a in range(patch_rows)]
     totals = [jnp.zeros((patch_cols * members + PATCH, members), f32) for _ in plans]
-    for start in range(0, tile_rows, STEP):
-        anomalies = [rows_ref[start + i] for i in range(STEP)]
-        fields = [held_ref[k, start : start + STEP, :] for k in range(2)]
-        totals = [accumulate(total, plan, anomalies, *fields, jnp.int32(start)) for total, plan in zip(totals, plans)]
+    tile_rows = patch_rows * PATCH
+    for first, rows_ref, held_ref in (
+        (down * (tile_rows - FAR), most_ref, most_held_ref),
+        ((1 - down) * (tile_rows - NEAR), rest_ref, rest_held_ref),
+    ):
+        for start in range(0, rows_ref.shape[0], STEP):
+            anomalies = [rows_ref[start + i] for i in range(STEP)]
+            fields = [held_ref[k, start : start + STEP, :] for k in range(2)]
+            totals = [accumulate(total, plan, anomalies, *fields, first + start) for total, plan in zip(totals, plans)]
     sums = jnp.concatenate(paired(totals, members, patch_cols), 0)
     out_ref[...] = sums + arrived(first_ref, 0, patch_cols)
 
@@ -316,9 +349,13 @@
 
     shape = jax.ShapeDtypeStruct
     vmem = pl.BlockSpec(memory_space=pltpu.VMEM)
-    parts = [forecast]
+    lag = lax.axis_index("lag")
+    most_parts, rest_parts = [forecast], [forecast]
     for k in range(1, shares):
-        parts.append(lax.ppermute(forecast, "lag", [((i + k) % shares, i) for i in range(shares)]))
+        half = lax.rem(lag + shares - k, shares) // (shares // 2)
+        pairs = [((i + k) % shares, i) for i in range(shares)]
+        most = lax.dynamic_slice_in_dim(forecast, half * (tile_rows - FAR), FAR, 1)
+        most_parts.append(lax.ppermute(most, "lag", pairs))
     live = lax.broadcasted_iota(jnp.int32, spot.shape, 1) < alive[:, None]
     weights = jnp.where(live, precision, 0.0)
     kind = lax.broadcasted_iota(jnp.int32, (3, *spot.shape), 0)
@@ -336,18 +373,28 @@
         [vmem, vmem],
         [shape((2, tile_rows, cols), f32), shape((tile_rows, cols), f32)],
     )(tables, forecast)
+    fields, later = lax.optimization_barrier((fields, forecast))
+    for k in range(1, shares):
+        half = lax.rem(lag + shares - k, shares) // (shares // 2)
+        rest = lax.dynamic_slice_in_dim(later, (1 - half) * FAR, tile_rows - FAR, 1)
+        rest_parts.append(lax.ppermute(rest, "lag", [((i + k) % shares, i) for i in range(shares)]))
     pair_rows = patch_cols * members
     message_shape = shape((pair_rows + 2 * patch_cols, 2 * members), bf16)
     total_scratch = pltpu.VMEM((2, patch_cols * members + PATCH, members), f32)
-    rows, held, message = call(
-        functools.partial(first_kernel, shares),
-        "first_gram",
-        [vmem] * (shares + 3),
-        [shape((tile_rows, members, cols), bf16), shape((2, tile_rows, cols), f32), message_shape],
-        [pltpu.VMEM((members * tile_rows, cols), f32), total_scratch],
-    )(*parts, own_sum, fields, next_inverses[0])
+    def run_shapes(count):
+        return [shape((count, members, cols), bf16), shape((2, count, cols), f32), message_shape]
+
+    def run_scratch(count):
+        return [pltpu.VMEM((members * count, cols), f32), total_scratch]
+
+    most, most_held, message = call(
+        functools.partial(first_kernel, shares), "first_gram", [vmem] * (shares + 3), run_shapes(FAR), run_scratch(FAR)
+    )(*most_parts, own_sum, fields, next_inverses[0])
     first = lax.ppermute(message, axes, rings[0])
-    message = call(second_kernel, "second_gram", [vmem] * 3, message_shape, [total_scratch])(rows, held, next_inverses[1])
+    left = tile_rows - FAR
+    rest, rest_held, message = call(
+        functools.partial(second_kernel, shares), "second_gram", [vmem] * (shares + 5), run_shapes(left), run_scratch(left)
+    )(*rest_parts, own_sum, fields, most, most_held, next_inverses[1])
     second = lax.ppermute(message, axes, rings[1])
     lag_rows, lag_mean = call(
         state_kernel,
@@ -355,9 +402,11 @@
         [vmem, vmem],
         [shape((tile_rows, members, cols), bf16), shape((tile_rows, cols), f32)],
         [pltpu.VMEM((members * tile_rows, cols), f32)],
-    )(held, history[0])
+    )(most_held, history[0])
     own_shape = shape((pair_rows + patch_cols, 2 * members), f32)
-    own = call(own_kernel, "own_gram", [vmem] * 5, own_shape)(lag_mean, rows, held, inverse, first)
+    own = call(own_kernel, "own_gram", [vmem] * 7, own_shape)(
+        lag_mean, most, most_held, rest, rest_held, inverse, first
+    )
     return call(
         finish_kernel,
         "finish",

time: 23.8 us -> 23.8 us (level)
  other arithmetic: 1.57 us -> 0.16 us
  local copies, waits for them, and re-layouts: 1.12 us -> 2.5 us
  waiting for transfers between devices: 3.2 us -> 4.06 us
  starting transfers between devices: 6.77 us -> 6.05 us
    dynamic_slice x0 -> x2, local copies, waits for them, and re-layouts: none -> 1.05 us  [the longest x1 1.02 us: shards(): most = lax.dynamic_slice_in_dim(forecast, half * (tile_rows - FAR), FAR, 1)]
    ppermute x1, starting transfers between devices: 1.72 us -> 0.8 us  [shards(): first = lax.ppermute(message, axes, rings[0])]
    ppermute x2, waiting for transfers between devices: 1.4 us -> 2.26 us  [shards(): lax.ppermute(sent, axes, [(t, s) for s, t in pairs])]
    mul x1, other arithmetic: 0.83 us -> 0.07 us  [shards(): weights * levels]
    div x1, other arithmetic: 0.66 us -> 0.01 us  [shards(): 1.0 / jnp.square(radius.astype(f32))]
    unnamed x10 -> x14, local copies, waits for them, and re-layouts: 0.96 us -> 1.3 us
    pallas_call x1, Pallas kernels: 2 us -> 1.67 us  [shards(): call(functools.partial(first_kernel, shares), 'first_gram', [vmem] * (sha...]
    ppermute x1 -> x2, starting transfers between devices: 2.97 us -> 3.13 us  [the longest x1 3.03 us: shards(): most_parts.append(lax.ppermute(most, 'lag', pairs))]
  transfers between devices with their start and end apart: 5 -> 6, of which waited for: 3 -> 3; matrix products, arithmetic and copies ran while one was open for 7% -> 2% of each run, Pallas kernels for 30% -> 29%
where the time goes in v4:
time: 23.8 us; the launch traced here: 23.5 us
  Pallas kernels  10.6 us (45%)
  starting transfers between devices  6.05 us (25%)
  waiting for transfers between devices  4.06 us (17%)
  local copies, waits for them, and re-layouts  2.5 us (11%)
    pallas_call x1, Pallas kernels, shards(): call(finish_kernel, 'finish', [vmem] * 4, shape((1, members, tile_rows, c...  3.77 us
    ppermute x1, starting transfers between devices, shards(): most_parts.append(lax.ppermute(most, 'lag', pairs))  3.03 us
    pallas_call x1, Pallas kernels, shards(): call(own_kernel, 'own_gram', [vmem] * 7, own_shape)  2.45 us
    ppermute x2, waiting for transfers between devices, shards(): lax.ppermute(sent, axes, [(t, s) for s, t in pairs])  2.26 us
    ppermute x2, starting transfers between devices, shards(): lax.ppermute(sent, axes, [(t, s) for s, t in pairs])  2.06 us
    pallas_call x1, Pallas kernels, shards(): call(functools.partial(first_kernel, shares), 'first_gram', [vmem] * (sha...  1.67 us
    ppermute x1, waiting for transfers between devices, shards(): second = lax.ppermute(message, axes, rings[1])  1.59 us
    pallas_call x1, Pallas kernels, shards(): call(functools.partial(second_kernel, shares), 'second_gram', [vmem] * (s...  1.52 us
  transfers between devices with their start and end apart: 6, of which 3 were waited for; matrix products, arithmetic and copies ran while one was open for 2% of the time, Pallas kernels for 29%

profile of v4, /device:TPU:0, one launch (start us, length us, event | category | flops | bytes accessed | tf_op | source)
XLA Modules:
  0.0 23.5 jit_solution(12963933866283544343)
XLA Ops:
  0.0 1.0 %constant_dynamic-slice_fusion.1 = bf16[32,24,128]{2,1,0:T(8,128)(2,1)S(1)} fusion(bf16[32,32,128]{2,1,0:T(8,128)(2,1)} %refs_0_.3, s32[]{:T(128)S(6)} %select_n.22), kind=kLoop, calls=%fused_computation.7 | loop fusion | bytes 393220 | tf_op jit(solution)/shard_map/dynamic_slice | solution.py:357
  1.0 3.0 %collective-permute-start = (bf16[32,24,128]{2,1,0:T(8,128)(2,1)S(1)}, bf16[32,24,128]{2,1,0:T(8,128)(2,1)S(1)}, u32[]{:S(2)}, u32[]{:S(2)}) collective-permute-start(bf16[32,24,128]{2,1,0:T(8,128)(2,1)S(1)} %constant_dynamic-slice_fusion.1), channel_id=1, source_target_pairs={{1,0},{0,1},{3,2},{2,3},{5,4},{4,5},{7,6},{6,7},{9,8},{8,9},{11,10... | collective-permute-start | bytes 589832 | tf_op jit(solution)/shard_map/ppermute | solution.py:358
  4.1 0.0 copy-done.2
  4.1 0.0 copy-start.4
  4.1 0.0 copy-done.5
  4.1 0.7 %copy-done.3 = f32[16,256]{1,0:T(8,128)S(1)} copy-done((f32[16,256]{1,0:T(8,128)S(1)}, f32[16,256]{1,0:T(8,128)}, u32[]{:S(2)}) %copy-start.3) | copy-done | bytes 16408
  4.8 0.0 copy-done.4
  4.8 0.1 fusion.1
  4.9 0.1 select_select_fusion.table_ref
  5.0 0.6 %copy-done.6 = s32[16]{0:T(128)S(1)} copy-done((s32[16]{0:T(128)S(1)}, s32[16]{0:T(128)}, u32[]{:S(2)}) %copy-start.6) | copy-done | bytes 88
  5.5 0.1 broadcast_in_dim.39
  5.6 0.1 broadcast_in_dim.40.inverse_ref
  5.7 0.0 copy-done
  5.7 0.5 %fields.1 = (f32[2,32,128]{2,1,0:T(8,128)S(1)}, f32[32,128]{1,0:T(8,128)S(1)}) custom-call(f32[3,16,256]{2,1,0:T(8,128)S(1)} %select_select_fusion.table_ref, bf16[32,32,128]{2,1,0:T(8,128)(2,1)S(1)} %copy-done), custom_call_target="tpu_custom_call" | custom-call | tf_op jit(solution)/shard_map/fields/pallas_call | solution.py:370
  6.2 0.1 collective-permute-start.2
  6.3 0.0 collective-permute-start.1
  6.4 2.0 %collective-permute-start.3 = (f32[2,8,128]{2,1,0:T(8,128)S(1)}, f32[2,8,128]{2,1,0:T(8,128)S(1)}, u32[]{:S(2)}, u32[]{:S(2)}) collective-permute-start(f32[2,8,128]{2,1,0:T(8,128)S(1)} %broadcast_in_dim.40.inverse_ref), channel_id=1, source_target_pairs={{2,0},{0,1},{4,2},{1,3},{6,4},{3,5},{8,6},{5,7},{10,8},{7,9},{12,1... | collective-permute-start | bytes 24584 | tf_op jit(solution)/shard_map/ppermute | solution.py:369
  8.4 2.3 %collective-permute-done.1.refs_4_ = f32[2,8,128]{2,1,0:T(8,128)S(1)} collective-permute-done((f32[2,8,128]{2,1,0:T(8,128)S(1)}, f32[2,8,128]{2,1,0:T(8,128)S(1)}, u32[]{:S(2)}, u32[]{:S(2)}) %collective-permute-start.1) | collective-permute-done | bytes 8224 | tf_op jit(solution)/shard_map/ppermute | solution.py:369
  10.6 0.0 collective-permute-done.refs_1_
  10.7 1.7 %first_gram.1 = (bf16[24,64,128]{2,1,0:T(8,128)(2,1)S(1)}, f32[2,24,128]{2,1,0:T(8,128)S(1)}, bf16[528,128]{1,0:T(8,128)(2,1)S(1)}) custom-call(bf16[32,32,128]{2,1,0:T(8,128)(2,1)S(1)} %copy-done, bf16[32,24,128]{2,1,0:T(8,128)(2,1)S(1)} %collective-permute-done.refs_1_, f32[32,128]{1,0:T(8,128)S(1)} %get-tuple-element.20.refs_2_, ...), custom_call_target="tpu_custom_call" | custom-call | tf_op jit(solution)/shard_map/first_gram/pallas_call | solution.py:390
  12.3 0.0 copy-start.1
  12.3 0.8 %collective-permute-start.4 = (bf16[528,128]{1,0:T(8,128)(2,1)S(1)}, bf16[528,128]{1,0:T(8,128)(2,1)S(1)}, u32[]{:S(2)}, u32[]{:S(2)}) collective-permute-start(bf16[528,128]{1,0:T(8,128)(2,1)S(1)} %get-tuple-element.30), channel_id=1, source_target_pairs={{0,1},{1,3},{2,0},{3,5},{4,2},{5,7},{6,4},{7,9},{8,6},{9,11},{10,8... | collective-permute-start | bytes 405512 | tf_op jit(solution)/shard_map/ppermute | solution.py:393
  13.1 0.0 collective-permute-done.3.refs_6_
  13.1 0.0 collective-permute-done.2.refs_1_
  13.1 1.5 %second_gram.1 = (bf16[8,64,128]{2,1,0:T(8,128)(2,1)S(1)}, f32[2,8,128]{2,1,0:T(8,128)S(1)}, bf16[528,128]{1,0:T(8,128)(2,1)S(1)}) custom-call(bf16[32,32,128]{2,1,0:T(8,128)(2,1)S(1)} %copy-done, bf16[32,8,128]{2,1,0:T(8,128)(2,1)S(1)} %collective-permute-done.2.refs_1_, f32[32,128]{1,0:T(8,128)S(1)} %get-tuple-element.20.refs_2_, ...), custom_call_target="tpu_custom_call" | custom-call | tf_op jit(solution)/shard_map/second_gram/pallas_call | solution.py:395
  14.7 0.1 collective-permute-start.5
  14.7 0.0 copy-done.1
  14.8 0.7 %state.1 = (bf16[32,64,128]{2,1,0:T(8,128)(2,1)S(1)}, f32[32,128]{1,0:T(8,128)S(1)}) custom-call(f32[2,24,128]{2,1,0:T(8,128)S(1)} %get-tuple-element.24.after_ref.refs_5_.most_held_ref, bf16[64,32,128]{2,1,0:T(8,128)(2,1)S(1)} %bitcast.1), custom_call_target="tpu_custom_call" | custom-call | tf_op jit(solution)/shard_map/state/pallas_call | solution.py:399
  15.5 0.2 collective-permute-done.4.first_ref
  15.7 2.5 %own_gram.1.total_ref = f32[520,128]{1,0:T(8,128)S(1)} custom-call(f32[32,128]{1,0:T(8,128)S(1)} %get-tuple-element.25.after_ref.mean_ref, bf16[24,64,128]{2,1,0:T(8,128)(2,1)S(1)} %get-tuple-element.26.refs_4_.most_ref, f32[2,24,128]{2,1,0:T(8,128)S(1)} %get-tuple-element.24.after_ref.refs_5_.most_held_ref, ...), custom_call_target="tpu_custom_call" | custom-call | tf_op jit(solution)/shard_map/own_gram/pallas_call | solution.py:407
  18.2 1.6 %collective-permute-done.5.second_ref = bf16[528,128]{1,0:T(8,128)(2,1)S(1)} collective-permute-done((bf16[528,128]{1,0:T(8,128)(2,1)S(1)}, bf16[528,128]{1,0:T(8,128)(2,1)S(1)}, u32[]{:S(2)}, u32[]{:S(2)}) %collective-permute-start.5) | collective-permute-done | bytes 135200 | tf_op jit(solution)/shard_map/ppermute | solution.py:398
  19.7 3.8 %finish.1 = bf16[1,64,32,128]{3,2,1,0:T(8,128)(2,1)} custom-call(f32[520,128]{1,0:T(8,128)S(1)} %own_gram.1.total_ref, bf16[528,128]{1,0:T(8,128)(2,1)S(1)} %collective-permute-done.5.second_ref, bf16[32,64,128]{2,1,0:T(8,128)(2,1)S(1)} %get-tuple-element.32.lag_ref, f32[32,128]{1,0:T(8,128)S(1)} %get-tuple-element.25.after_ref.mean_ref), custom_call_target="tpu_custom_call" | custom-call | tf_op jit(solution)/shard_map/finish/pallas_call | solution.py:410
  (9 shorter events, 0.1 us)
Async XLA Ops:
  0.0 4.1 %copy-start.2 = (s32[16,256]{1,0:T(8,128)S(1)}, s32[16,256]{1,0:T(8,128)}, u32[]{:S(2)}) copy-start(s32[16,256]{1,0:T(8,128)} %param.9) | copy-start | bytes 49156
  0.0 4.1 %copy-start.5 = (s32[16]{0:T(128)S(1)}, s32[16]{0:T(128)}, u32[]{:S(2)}) copy-start(s32[16]{0:T(128)} %param.10) | copy-start | bytes 196
  0.0 5.7 %copy-start = (bf16[32,32,128]{2,1,0:T(8,128)(2,1)S(1)}, bf16[32,32,128]{2,1,0:T(8,128)(2,1)}, u32[]{:S(2)}) copy-start(bf16[32,32,128]{2,1,0:T(8,128)(2,1)} %refs_0_.3) | copy-start | bytes 786436
  1.0 9.6 %collective-permute-start = (bf16[32,24,128]{2,1,0:T(8,128)(2,1)S(1)}, bf16[32,24,128]{2,1,0:T(8,128)(2,1)S(1)}, u32[]{:S(2)}, u32[]{:S(2)}) collective-permute-start(bf16[32,24,128]{2,1,0:T(8,128)(2,1)S(1)} %constant_dynamic-slice_fusion.1), channel_id=1, source_target_pairs={{1,0},{0,1},{3,2},{2,3},{5,4},{4,5},{7,6},{6,7},{9,8},{8,9},{11,10... | collective-permute-start | bytes 589832 | tf_op jit(solution)/shard_map/ppermute | solution.py:358
  4.1 0.7 %copy-start.3 = (f32[16,256]{1,0:T(8,128)S(1)}, f32[16,256]{1,0:T(8,128)}, u32[]{:S(2)}) copy-start(f32[16,256]{1,0:T(8,128)} %param.11) | copy-start | bytes 49156
  4.1 0.7 %copy-start.4 = (f32[16,256]{1,0:T(8,128)S(1)}, f32[16,256]{1,0:T(8,128)}, u32[]{:S(2)}) copy-start(f32[16,256]{1,0:T(8,128)} %param.12) | copy-start | bytes 49156
  4.9 0.7 %copy-start.6 = (s32[16]{0:T(128)S(1)}, s32[16]{0:T(128)}, u32[]{:S(2)}) copy-start(s32[16]{0:T(128)} %param.13) | copy-start | bytes 196
  6.2 6.9 %collective-permute-start.2 = (bf16[32,8,128]{2,1,0:T(8,128)(2,1)S(1)}, bf16[32,8,128]{2,1,0:T(8,128)(2,1)S(1)}, u32[]{:S(2)}, u32[]{:S(2)}) collective-permute-start(bf16[32,8,128]{2,1,0:T(8,128)(2,1)S(1)} %constant_dynamic-slice_fusion), channel_id=1, source_target_pairs={{1,0},{0,1},{3,2},{2,3},{5,4},{4,5},{7,6},{6,7},{9,8},{8,9},{11,10... | collective-permute-start | bytes 196616 | tf_op jit(solution)/shard_map/ppermute | solution.py:380
  6.3 4.3 %collective-permute-start.1 = (f32[2,8,128]{2,1,0:T(8,128)S(1)}, f32[2,8,128]{2,1,0:T(8,128)S(1)}, u32[]{:S(2)}, u32[]{:S(2)}) collective-permute-start(f32[2,8,128]{2,1,0:T(8,128)S(1)} %broadcast_in_dim.40.inverse_ref), channel_id=1, source_target_pairs={{1,0},{3,1},{0,2},{5,3},{2,4},{7,5},{4,6},{9,7},{6,8},{11,9},{8,10... | collective-permute-start | bytes 24584 | tf_op jit(solution)/shard_map/ppermute | solution.py:369
  6.4 6.8 %collective-permute-start.3 = (f32[2,8,128]{2,1,0:T(8,128)S(1)}, f32[2,8,128]{2,1,0:T(8,128)S(1)}, u32[]{:S(2)}, u32[]{:S(2)}) collective-permute-start(f32[2,8,128]{2,1,0:T(8,128)S(1)} %broadcast_in_dim.40.inverse_ref), channel_id=1, source_target_pairs={{2,0},{0,1},{4,2},{1,3},{6,4},{3,5},{8,6},{5,7},{10,8},{7,9},{12,1... | collective-permute-start | bytes 24584 | tf_op jit(solution)/shard_map/ppermute | solution.py:369
  12.3 2.4 %copy-start.1 = (bf16[1,64,32,128]{3,2,1,0:T(8,128)(2,1)S(1)}, bf16[1,64,32,128]{3,2,1,0:T(8,128)(2,1)}, u32[]{:S(2)}) copy-start(bf16[1,64,32,128]{3,2,1,0:T(8,128)(2,1)} %param.7) | copy-start | bytes 1572868
  12.3 3.4 %collective-permute-start.4 = (bf16[528,128]{1,0:T(8,128)(2,1)S(1)}, bf16[528,128]{1,0:T(8,128)(2,1)S(1)}, u32[]{:S(2)}, u32[]{:S(2)}) collective-permute-start(bf16[528,128]{1,0:T(8,128)(2,1)S(1)} %get-tuple-element.30), channel_id=1, source_target_pairs={{0,1},{1,3},{2,0},{3,5},{4,2},{5,7},{6,4},{7,9},{8,6},{9,11},{10,8... | collective-permute-start | bytes 405512 | tf_op jit(solution)/shard_map/ppermute | solution.py:393
  14.7 5.1 %collective-permute-start.5 = (bf16[528,128]{1,0:T(8,128)(2,1)S(1)}, bf16[528,128]{1,0:T(8,128)(2,1)S(1)}, u32[]{:S(2)}, u32[]{:S(2)}) collective-permute-start(bf16[528,128]{1,0:T(8,128)(2,1)S(1)} %get-tuple-element.31), channel_id=1, source_target_pairs={{0,2},{1,0},{2,4},{3,1},{4,6},{5,3},{6,8},{7,5},{8,10},{9,7},{10,1... | collective-permute-start | bytes 405512 | tf_op jit(solution)/shard_map/ppermute | solution.py:398

commit v5 on v4

--- a/solution.py
+++ b/solution.py
@@ -373,7 +373,7 @@
         [vmem, vmem],
         [shape((2, tile_rows, cols), f32), shape((tile_rows, cols), f32)],
     )(tables, forecast)
-    fields, later = lax.optimization_barrier((fields, forecast))
+    fields, later, next_inverses = lax.optimization_barrier((fields, forecast, next_inverses))
     for k in range(1, shares):
         half = lax.rem(lag + shares - k, shares) // (shares // 2)
         rest = lax.dynamic_slice_in_dim(later, (1 - half) * FAR, tile_rows - FAR, 1)

time: 23.8 us -> 24.4 us (1.025)
  waiting for transfers between devices: 4.06 us -> 4.97 us
  starting transfers between devices: 6.05 us -> 5.75 us
    ppermute x2, starting transfers between devices: 2.06 us -> 0.52 us  [shards(): lax.ppermute(sent, axes, [(t, s) for s, t in pairs])]
    ppermute x1, starting transfers between devices: 0.09 us -> 1.47 us  [shards(): lax.ppermute(rest, 'lag', [((i + k) % shares, i) for i in range(shares)])]
    ppermute x1, waiting for transfers between devices: 0.01 us -> 0.5 us  [shards(): lax.ppermute(rest, 'lag', [((i + k) % shares, i) for i in range(shares)])]
    ppermute x2, waiting for transfers between devices: 2.26 us -> 2.68 us  [shards(): lax.ppermute(sent, axes, [(t, s) for s, t in pairs])]
  transfers between devices with their start and end apart: 6 -> 6, of which waited for: 3 -> 4; matrix products, arithmetic and copies ran while one was open for 2% -> 1% of each run, Pallas kernels for 29% -> 28%
where the time goes in v5:
time: 24.4 us; the launch traced here: 24.1 us
  Pallas kernels  10.6 us (43%)
  starting transfers between devices  5.75 us (24%)
  waiting for transfers between devices  4.97 us (20%)
  local copies, waits for them, and re-layouts  2.48 us (10%)
    pallas_call x1, Pallas kernels, shards(): call(finish_kernel, 'finish', [vmem] * 4, shape((1, members, tile_rows, c...  3.78 us
    ppermute x1, starting transfers between devices, shards(): most_parts.append(lax.ppermute(most, 'lag', pairs))  3.03 us
    ppermute x2, waiting for transfers between devices, shards(): lax.ppermute(sent, axes, [(t, s) for s, t in pairs])  2.68 us
    pallas_call x1, Pallas kernels, shards(): call(own_kernel, 'own_gram', [vmem] * 7, own_shape)  2.45 us
    ppermute x1, waiting for transfers between devices, shards(): second = lax.ppermute(message, axes, rings[1])  1.79 us
    pallas_call x1, Pallas kernels, shards(): call(functools.partial(first_kernel, shares), 'first_gram', [vmem] * (sha...  1.67 us
    pallas_call x1, Pallas kernels, shards(): call(functools.partial(second_kernel, shares), 'second_gram', [vmem] * (s...  1.53 us
    ppermute x1, starting transfers between devices, shards(): lax.ppermute(rest, 'lag', [((i + k) % shares, i) for i in range(shares)])  1.47 us
  transfers between devices with their start and end apart: 6, of which 4 were waited for; matrix products, arithmetic and copies ran while one was open for 1% of the time, Pallas kernels for 28%

profile of v5, /device:TPU:0, one launch (start us, length us, event | category | flops | bytes accessed | tf_op | source)
XLA Modules:
  0.0 24.1 jit_solution(7617562900701089911)
XLA Ops:
  0.0 1.0 %constant_dynamic-slice_fusion.1 = bf16[32,24,128]{2,1,0:T(8,128)(2,1)S(1)} fusion(bf16[32,32,128]{2,1,0:T(8,128)(2,1)} %refs_0_.3, s32[]{:T(128)S(6)} %select_n.22), kind=kLoop, calls=%fused_computation.7 | loop fusion | bytes 393220 | tf_op jit(solution)/shard_map/dynamic_slice | solution.py:357
  1.0 3.0 %collective-permute-start = (bf16[32,24,128]{2,1,0:T(8,128)(2,1)S(1)}, bf16[32,24,128]{2,1,0:T(8,128)(2,1)S(1)}, u32[]{:S(2)}, u32[]{:S(2)}) collective-permute-start(bf16[32,24,128]{2,1,0:T(8,128)(2,1)S(1)} %constant_dynamic-slice_fusion.1), channel_id=1, source_target_pairs={{1,0},{0,1},{3,2},{2,3},{5,4},{4,5},{7,6},{6,7},{9,8},{8,9},{11,10... | collective-permute-start | bytes 589832 | tf_op jit(solution)/shard_map/ppermute | solution.py:358
  4.1 0.0 copy-done.2
  4.1 0.0 copy-start.4
  4.1 0.0 copy-done.5
  4.1 0.7 %copy-done.3 = f32[16,256]{1,0:T(8,128)S(1)} copy-done((f32[16,256]{1,0:T(8,128)S(1)}, f32[16,256]{1,0:T(8,128)}, u32[]{:S(2)}) %copy-start.3) | copy-done | bytes 16408
  4.8 0.0 copy-done.4
  4.8 0.1 fusion.1
  4.9 0.1 select_select_fusion.table_ref
  5.0 0.6 %copy-done.6 = s32[16]{0:T(128)S(1)} copy-done((s32[16]{0:T(128)S(1)}, s32[16]{0:T(128)}, u32[]{:S(2)}) %copy-start.6) | copy-done | bytes 88
  5.5 0.1 broadcast_in_dim.39
  5.6 0.1 broadcast_in_dim.40.inverse_ref
  5.7 0.0 collective-permute-start.2
  5.7 0.5 %collective-permute-start.1 = (f32[2,8,128]{2,1,0:T(8,128)S(1)}, f32[2,8,128]{2,1,0:T(8,128)S(1)}, u32[]{:S(2)}, u32[]{:S(2)}) collective-permute-start(f32[2,8,128]{2,1,0:T(8,128)S(1)} %broadcast_in_dim.40.inverse_ref), channel_id=1, source_target_pairs={{1,0},{3,1},{0,2},{5,3},{2,4},{7,5},{4,6},{9,7},{6,8},{11,9},{8,10... | collective-permute-start | bytes 24584 | tf_op jit(solution)/shard_map/ppermute | solution.py:369
  6.2 0.0 copy-done
  6.2 0.5 %fields.1 = (f32[2,32,128]{2,1,0:T(8,128)S(1)}, f32[32,128]{1,0:T(8,128)S(1)}) custom-call(f32[3,16,256]{2,1,0:T(8,128)S(1)} %select_select_fusion.table_ref, bf16[32,32,128]{2,1,0:T(8,128)(2,1)S(1)} %copy-done), custom_call_target="tpu_custom_call" | custom-call | tf_op jit(solution)/shard_map/fields/pallas_call | solution.py:370
  6.7 1.6 %collective-permute-done.2.refs_6_ = f32[2,8,128]{2,1,0:T(8,128)S(1)} collective-permute-done((f32[2,8,128]{2,1,0:T(8,128)S(1)}, f32[2,8,128]{2,1,0:T(8,128)S(1)}, u32[]{:S(2)}, u32[]{:S(2)}) %collective-permute-start.2) | collective-permute-done | bytes 8224 | tf_op jit(solution)/shard_map/ppermute | solution.py:369
  8.3 1.1 %collective-permute-done.1.refs_4_ = f32[2,8,128]{2,1,0:T(8,128)S(1)} collective-permute-done((f32[2,8,128]{2,1,0:T(8,128)S(1)}, f32[2,8,128]{2,1,0:T(8,128)S(1)}, u32[]{:S(2)}, u32[]{:S(2)}) %collective-permute-start.1) | collective-permute-done | bytes 8224 | tf_op jit(solution)/shard_map/ppermute | solution.py:369
  9.4 1.5 %collective-permute-start.3 = (bf16[32,8,128]{2,1,0:T(8,128)(2,1)S(1)}, bf16[32,8,128]{2,1,0:T(8,128)(2,1)S(1)}, u32[]{:S(2)}, u32[]{:S(2)}) collective-permute-start(bf16[32,8,128]{2,1,0:T(8,128)(2,1)S(1)} %constant_dynamic-slice_fusion), channel_id=1, source_target_pairs={{1,0},{0,1},{3,2},{2,3},{5,4},{4,5},{7,6},{6,7},{9,8},{8,9},{11,10... | collective-permute-start | bytes 196616 | tf_op jit(solution)/shard_map/ppermute | solution.py:380
  10.9 0.0 collective-permute-done.refs_1_
  10.9 1.7 %first_gram.1 = (bf16[24,64,128]{2,1,0:T(8,128)(2,1)S(1)}, f32[2,24,128]{2,1,0:T(8,128)S(1)}, bf16[528,128]{1,0:T(8,128)(2,1)S(1)}) custom-call(bf16[32,32,128]{2,1,0:T(8,128)(2,1)S(1)} %copy-done, bf16[32,24,128]{2,1,0:T(8,128)(2,1)S(1)} %collective-permute-done.refs_1_, f32[32,128]{1,0:T(8,128)S(1)} %get-tuple-element.22.refs_2_, ...), custom_call_target="tpu_custom_call" | custom-call | tf_op jit(solution)/shard_map/first_gram/pallas_call | solution.py:390
  12.6 0.0 copy-start.1
  12.6 0.7 %collective-permute-start.4 = (bf16[528,128]{1,0:T(8,128)(2,1)S(1)}, bf16[528,128]{1,0:T(8,128)(2,1)S(1)}, u32[]{:S(2)}, u32[]{:S(2)}) collective-permute-start(bf16[528,128]{1,0:T(8,128)(2,1)S(1)} %get-tuple-element.34), channel_id=1, source_target_pairs={{0,1},{1,3},{2,0},{3,5},{4,2},{5,7},{6,4},{7,9},{8,6},{9,11},{10,8... | collective-permute-start | bytes 405512 | tf_op jit(solution)/shard_map/ppermute | solution.py:393
  13.2 0.5 %collective-permute-done.3.refs_1_ = bf16[32,8,128]{2,1,0:T(8,128)(2,1)S(1)} collective-permute-done((bf16[32,8,128]{2,1,0:T(8,128)(2,1)S(1)}, bf16[32,8,128]{2,1,0:T(8,128)(2,1)S(1)}, u32[]{:S(2)}, u32[]{:S(2)}) %collective-permute-start.3) | collective-permute-done | bytes 65568 | tf_op jit(solution)/shard_map/ppermute | solution.py:380
  13.7 1.5 %second_gram.1 = (bf16[8,64,128]{2,1,0:T(8,128)(2,1)S(1)}, f32[2,8,128]{2,1,0:T(8,128)S(1)}, bf16[528,128]{1,0:T(8,128)(2,1)S(1)}) custom-call(bf16[32,32,128]{2,1,0:T(8,128)(2,1)S(1)} %copy-done, bf16[32,8,128]{2,1,0:T(8,128)(2,1)S(1)} %collective-permute-done.3.refs_1_, f32[32,128]{1,0:T(8,128)S(1)} %get-tuple-element.22.refs_2_, ...), custom_call_target="tpu_custom_call" | custom-call | tf_op jit(solution)/shard_map/second_gram/pallas_call | solution.py:395
  15.3 0.1 collective-permute-start.5
  15.3 0.0 copy-done.1
  15.3 0.7 %state.1 = (bf16[32,64,128]{2,1,0:T(8,128)(2,1)S(1)}, f32[32,128]{1,0:T(8,128)S(1)}) custom-call(f32[2,24,128]{2,1,0:T(8,128)S(1)} %get-tuple-element.27.after_ref.refs_5_.most_held_ref, bf16[64,32,128]{2,1,0:T(8,128)(2,1)S(1)} %bitcast.1), custom_call_target="tpu_custom_call" | custom-call | tf_op jit(solution)/shard_map/state/pallas_call | solution.py:399
  16.1 0.0 collective-permute-done.4.first_ref
  16.1 2.5 %own_gram.1.total_ref = f32[520,128]{1,0:T(8,128)S(1)} custom-call(f32[32,128]{1,0:T(8,128)S(1)} %get-tuple-element.28.after_ref.mean_ref, bf16[24,64,128]{2,1,0:T(8,128)(2,1)S(1)} %get-tuple-element.29.refs_4_.most_ref, f32[2,24,128]{2,1,0:T(8,128)S(1)} %get-tuple-element.27.after_ref.refs_5_.most_held_ref, ...), custom_call_target="tpu_custom_call" | custom-call | tf_op jit(solution)/shard_map/own_gram/pallas_call | solution.py:407
  18.5 1.8 %collective-permute-done.5.second_ref = bf16[528,128]{1,0:T(8,128)(2,1)S(1)} collective-permute-done((bf16[528,128]{1,0:T(8,128)(2,1)S(1)}, bf16[528,128]{1,0:T(8,128)(2,1)S(1)}, u32[]{:S(2)}, u32[]{:S(2)}) %collective-permute-start.5) | collective-permute-done | bytes 135200 | tf_op jit(solution)/shard_map/ppermute | solution.py:398
  20.3 3.8 %finish.1 = bf16[1,64,32,128]{3,2,1,0:T(8,128)(2,1)} custom-call(f32[520,128]{1,0:T(8,128)S(1)} %own_gram.1.total_ref, bf16[528,128]{1,0:T(8,128)(2,1)S(1)} %collective-permute-done.5.second_ref, bf16[32,64,128]{2,1,0:T(8,128)(2,1)S(1)} %get-tuple-element.36.lag_ref, f32[32,128]{1,0:T(8,128)S(1)} %get-tuple-element.28.after_ref.mean_ref), custom_call_target="tpu_custom_call" | custom-call | tf_op jit(solution)/shard_map/finish/pallas_call | solution.py:410
  (9 shorter events, 0.0 us)
Async XLA Ops:
  0.0 4.1 %copy-start.2 = (s32[16,256]{1,0:T(8,128)S(1)}, s32[16,256]{1,0:T(8,128)}, u32[]{:S(2)}) copy-start(s32[16,256]{1,0:T(8,128)} %param.9) | copy-start | bytes 49156
  0.0 4.1 %copy-start.5 = (s32[16]{0:T(128)S(1)}, s32[16]{0:T(128)}, u32[]{:S(2)}) copy-start(s32[16]{0:T(128)} %param.10) | copy-start | bytes 196
  0.0 6.2 %copy-start = (bf16[32,32,128]{2,1,0:T(8,128)(2,1)S(1)}, bf16[32,32,128]{2,1,0:T(8,128)(2,1)}, u32[]{:S(2)}) copy-start(bf16[32,32,128]{2,1,0:T(8,128)(2,1)} %refs_0_.3) | copy-start | bytes 786436
  1.0 9.8 %collective-permute-start = (bf16[32,24,128]{2,1,0:T(8,128)(2,1)S(1)}, bf16[32,24,128]{2,1,0:T(8,128)(2,1)S(1)}, u32[]{:S(2)}, u32[]{:S(2)}) collective-permute-start(bf16[32,24,128]{2,1,0:T(8,128)(2,1)S(1)} %constant_dynamic-slice_fusion.1), channel_id=1, source_target_pairs={{1,0},{0,1},{3,2},{2,3},{5,4},{4,5},{7,6},{6,7},{9,8},{8,9},{11,10... | collective-permute-start | bytes 589832 | tf_op jit(solution)/shard_map/ppermute | solution.py:358
  4.1 0.7 %copy-start.3 = (f32[16,256]{1,0:T(8,128)S(1)}, f32[16,256]{1,0:T(8,128)}, u32[]{:S(2)}) copy-start(f32[16,256]{1,0:T(8,128)} %param.11) | copy-start | bytes 49156
  4.1 0.7 %copy-start.4 = (f32[16,256]{1,0:T(8,128)S(1)}, f32[16,256]{1,0:T(8,128)}, u32[]{:S(2)}) copy-start(f32[16,256]{1,0:T(8,128)} %param.12) | copy-start | bytes 49156
  4.9 0.7 %copy-start.6 = (s32[16]{0:T(128)S(1)}, s32[16]{0:T(128)}, u32[]{:S(2)}) copy-start(s32[16]{0:T(128)} %param.13) | copy-start | bytes 196
  5.7 2.6 %collective-permute-start.2 = (f32[2,8,128]{2,1,0:T(8,128)S(1)}, f32[2,8,128]{2,1,0:T(8,128)S(1)}, u32[]{:S(2)}, u32[]{:S(2)}) collective-permute-start(f32[2,8,128]{2,1,0:T(8,128)S(1)} %broadcast_in_dim.40.inverse_ref), channel_id=1, source_target_pairs={{2,0},{0,1},{4,2},{1,3},{6,4},{3,5},{8,6},{5,7},{10,8},{7,9},{12,1... | collective-permute-start | bytes 24584 | tf_op jit(solution)/shard_map/ppermute | solution.py:369
  5.7 3.7 %collective-permute-start.1 = (f32[2,8,128]{2,1,0:T(8,128)S(1)}, f32[2,8,128]{2,1,0:T(8,128)S(1)}, u32[]{:S(2)}, u32[]{:S(2)}) collective-permute-start(f32[2,8,128]{2,1,0:T(8,128)S(1)} %broadcast_in_dim.40.inverse_ref), channel_id=1, source_target_pairs={{1,0},{3,1},{0,2},{5,3},{2,4},{7,5},{4,6},{9,7},{6,8},{11,9},{8,10... | collective-permute-start | bytes 24584 | tf_op jit(solution)/shard_map/ppermute | solution.py:369
  9.4 4.3 %collective-permute-start.3 = (bf16[32,8,128]{2,1,0:T(8,128)(2,1)S(1)}, bf16[32,8,128]{2,1,0:T(8,128)(2,1)S(1)}, u32[]{:S(2)}, u32[]{:S(2)}) collective-permute-start(bf16[32,8,128]{2,1,0:T(8,128)(2,1)S(1)} %constant_dynamic-slice_fusion), channel_id=1, source_target_pairs={{1,0},{0,1},{3,2},{2,3},{5,4},{4,5},{7,6},{6,7},{9,8},{8,9},{11,10... | collective-permute-start | bytes 196616 | tf_op jit(solution)/shard_map/ppermute | solution.py:380
  12.6 2.8 %copy-start.1 = (bf16[1,64,32,128]{3,2,1,0:T(8,128)(2,1)S(1)}, bf16[1,64,32,128]{3,2,1,0:T(8,128)(2,1)}, u32[]{:S(2)}) copy-start(bf16[1,64,32,128]{3,2,1,0:T(8,128)(2,1)} %param.7) | copy-start | bytes 1572868
  12.6 3.5 %collective-permute-start.4 = (bf16[528,128]{1,0:T(8,128)(2,1)S(1)}, bf16[528,128]{1,0:T(8,128)(2,1)S(1)}, u32[]{:S(2)}, u32[]{:S(2)}) collective-permute-start(bf16[528,128]{1,0:T(8,128)(2,1)S(1)} %get-tuple-element.34), channel_id=1, source_target_pairs={{0,1},{1,3},{2,0},{3,5},{4,2},{5,7},{6,4},{7,9},{8,6},{9,11},{10,8... | collective-permute-start | bytes 405512 | tf_op jit(solution)/shard_map/ppermute | solution.py:393
  15.3 5.1 %collective-permute-start.5 = (bf16[528,128]{1,0:T(8,128)(2,1)S(1)}, bf16[528,128]{1,0:T(8,128)(2,1)S(1)}, u32[]{:S(2)}, u32[]{:S(2)}) collective-permute-start(bf16[528,128]{1,0:T(8,128)(2,1)S(1)} %get-tuple-element.35), channel_id=1, source_target_pairs={{0,2},{1,0},{2,4},{3,1},{4,6},{5,3},{6,8},{7,5},{8,10},{9,7},{10,1... | collective-permute-start | bytes 405512 | tf_op jit(solution)/shard_map/ppermute | solution.py:398

commit v6 on v3

--- a/solution.py
+++ b/solution.py
@@ -113,11 +113,12 @@
     return total + mm(jnp.concatenate(lefts, 1), jnp.concatenate(anomalies, 1), NT)
 
 
-STEP = 4
-
-
-def paired(totals, members, patch_cols):
+STEP = 8
+
+
+def packed(totals, members, patch_cols):
     pairs = patch_cols // 2
+    half = members // 2
     grams, sides = [], []
     for total in totals:
         for pair in range(pairs):
@@ -126,7 +127,35 @@
         for pair in range(pairs):
             at = patch_cols * members + 2 * pair
             sides.append(jnp.concatenate([total[at : at + 1], total[at + 1 : at + 2]], 1))
-    return jnp.concatenate(grams, 0), jnp.concatenate(sides, 0)
+    lane = lax.broadcasted_iota(jnp.int32, (half, 2 * members), 1)
+    tops = [gram[:half] for gram in grams]
+    ends = [
+        jnp.where(lane % members < half, pltpu.roll(a[half:], 2 * members - half, 1), b[half:])
+        for a, b in zip(grams[::2], grams[1::2])
+    ]
+    return jnp.concatenate(tops + ends, 0), jnp.concatenate(sides, 0)
+
+
+def unpacked(rows, members):
+    half = members // 2
+    wide = 2 * members
+    count = rows.shape[0] * 2 // (3 * half)
+    lane = lax.broadcasted_iota(jnp.int32, (half, wide), 1)
+    tops = [rows[p * half : (p + 1) * half] for p in range(count)]
+    ends = [rows[(count + k) * half : (count + k + 1) * half] for k in range(count // 2)]
+    per_square = wide // half
+    turned = [
+        jnp.transpose(jnp.concatenate(tops[p : p + per_square], 0)) for p in range(0, count, per_square)
+    ]
+    grams = []
+    for p in range(count):
+        square, at = turned[p // per_square], (p % per_square) * half
+        first = pltpu.roll(square[half:members], (wide - at) % wide, 1)
+        second = pltpu.roll(square[members + half :], (members + wide - at) % wide, 1)
+        corner = ends[p // 2] if p % 2 else pltpu.roll(ends[p // 2], half, 1)
+        bottom = jnp.where(lane % members < half, jnp.where(lane < members, first, second), corner)
+        grams.append(jnp.concatenate([tops[p], bottom], 0))
+    return grams
 
 
 def message_of(grams, sides):
@@ -155,19 +184,17 @@
         taper_plan(middle, inverse_ref[1 - down]),
         taper_plan(middle + jnp.where(down == 0, -PATCH, PATCH).astype(f32), inverse_ref[down]),
     ]
-    totals = [jnp.zeros(total_ref.shape[1:], f32) for _ in plans]
-    near_fields = [held_ref[k, pl.ds(near, NEAR), :] for k in range(2)]
-    for start in range(0, NEAR, STEP):
-        anomalies = [rows_ref[near + start + i] for i in range(STEP)]
-        fields = [field[start : start + STEP] for field in near_fields]
-        totals = [accumulate(total, plan, anomalies, *fields, near + start) for total, plan in zip(totals, plans)]
+    anomalies = [rows_ref[near + i] for i in range(NEAR)]
+    fields = [held_ref[k, pl.ds(near, NEAR), :] for k in range(2)]
+    blank = jnp.zeros(total_ref.shape[1:], f32)
+    totals = [accumulate(blank, plan, anomalies, *fields, near) for plan in plans]
     for start in range(NEAR, FAR, STEP):
         anomalies = [rows_ref[start + i] for i in range(STEP)]
         fields = [held_ref[k, start : start + STEP, :] for k in range(2)]
         totals[0] = accumulate(totals[0], plans[0], anomalies, *fields, jnp.int32(start))
     total_ref[1 - down] = totals[0]
     total_ref[down] = totals[1]
-    message_ref[...] = message_of(*paired([total_ref[0], total_ref[1]], members, patch_cols))
+    message_ref[...] = message_of(*packed([total_ref[0], total_ref[1]], members, patch_cols))
 
 
 def first_kernel(shares, *refs):
@@ -202,15 +229,15 @@
         anomalies = [rows_ref[start + i] for i in range(STEP)]
         fields = [held_ref[k, start : start + STEP, :] for k in range(2)]
         totals = [accumulate(total, plan, anomalies, *fields, jnp.int32(start)) for total, plan in zip(totals, plans)]
-    sums = jnp.concatenate(paired(totals, members, patch_cols), 0)
+    sums = jnp.concatenate(packed(totals, members, patch_cols), 0)
     out_ref[...] = sums + arrived(first_ref, 0, patch_cols)
 
 
 def finish_kernel(total_ref, second_ref, lag_ref, mean_ref, out_ref, flat_ref):
     tile_rows, members, cols = lag_ref.shape
     degree = members - 1.0
-    pair_count = total_ref.shape[0] // members
-    grams_end = pair_count * members
+    pair_count = (tile_rows // PATCH) * (cols // PATCH) // 2
+    grams_end = total_ref.shape[0] - pair_count
     row = lax.broadcasted_iota(jnp.int32, (members, cols), 0)
     lane = lax.broadcasted_iota(jnp.int32, (members, cols), 1)
     identity = jnp.where(row == lane % members, 1.0, 0.0)
@@ -246,7 +273,7 @@
 
     total = total_ref[...] + arrived(second_ref, 1, pair_count)
     pairs = range(pair_count)
-    grams = [total[p * members : (p + 1) * members] for p in pairs]
+    grams = unpacked(total[:grams_end], members)
     squares = jnp.concatenate([jnp.sum(gram * gram, axis=0, keepdims=True) for gram in grams], 0)
     at_left = lax.broadcasted_iota(jnp.int32, squares.shape, 1) < members
     norm_left = jnp.sum(jnp.where(at_left, squares, 0.0), axis=1, keepdims=True)
@@ -336,8 +363,8 @@
         [vmem, vmem],
         [shape((2, tile_rows, cols), f32), shape((tile_rows, cols), f32)],
     )(tables, forecast)
-    pair_rows = patch_cols * members
-    message_shape = shape((pair_rows + 2 * patch_cols, 2 * members), bf16)
+    packed_rows = patch_cols * members * 3 // 4
+    message_shape = shape((packed_rows + 2 * patch_cols, 2 * members), bf16)
     total_scratch = pltpu.VMEM((2, patch_cols * members + PATCH, members), f32)
     rows, held, message = call(
         functools.partial(first_kernel, shares),
@@ -356,7 +383,7 @@
         [shape((tile_rows, members, cols), bf16), shape((tile_rows, cols), f32)],
         [pltpu.VMEM((members * tile_rows, cols), f32)],
     )(held, history[0])
-    own_shape = shape((pair_rows + patch_cols, 2 * members), f32)
+    own_shape = shape((packed_rows + patch_cols, 2 * members), f32)
     own = call(own_kernel, "own_gram", [vmem] * 5, own_shape)(lag_mean, rows, held, inverse, first)
     return call(
         finish_kernel,

time: 23.8 us -> 23.5 us (0.987)
  waiting for transfers between devices: 3.2 us -> 2.82 us
    ppermute x1, waiting for transfers between devices: 0.33 us -> 0.01 us  [shards(): first = lax.ppermute(message, axes, rings[0])]
  transfers between devices with their start and end apart: 5 -> 5, of which waited for: 3 -> 2; matrix products, arithmetic and copies ran while one was open for 7% -> 7% of each run, Pallas kernels for 30% -> 30%
where the time goes in v6:
time: 23.5 us; the launch traced here: 23.2 us
  Pallas kernels  10.9 us (46%)
  starting transfers between devices  6.79 us (29%)
  waiting for transfers between devices  2.82 us (12%)
  other arithmetic  1.57 us (7%)
  local copies, waits for them, and re-layouts  1.12 us (5%)
    pallas_call x1, Pallas kernels, shards(): call(finish_kernel, 'finish', [vmem] * 4, shape((1, members, tile_rows, c...  3.96 us
    ppermute x1, starting transfers between devices, shards(): lax.ppermute(forecast, 'lag', [((i + k) % shares, i) for i in range(share...  2.97 us
    pallas_call x1, Pallas kernels, shards(): call(own_kernel, 'own_gram', [vmem] * 5, own_shape)  2.48 us
    ppermute x2, starting transfers between devices, shards(): lax.ppermute(sent, axes, [(t, s) for s, t in pairs])  2.02 us
    pallas_call x1, Pallas kernels, shards(): call(functools.partial(first_kernel, shares), 'first_gram', [vmem] * (sha...  1.79 us
    ppermute x1, starting transfers between devices, shards(): first = lax.ppermute(message, axes, rings[0])  1.74 us
    pallas_call x1, Pallas kernels, shards(): call(second_kernel, 'second_gram', [vmem] * 3, message_shape, [total_scra...  1.44 us
    ppermute x1, waiting for transfers between devices, shards(): second = lax.ppermute(message, axes, rings[1])  1.41 us
  transfers between devices with their start and end apart: 5, of which 2 were waited for; matrix products, arithmetic and copies ran while one was open for 7% of the time, Pallas kernels for 30%

profile of v6, /device:TPU:0, one launch (start us, length us, event | category | flops | bytes accessed | tf_op | source)
XLA Modules:
  0.0 23.2 jit_solution(3144435312489529356)
XLA Ops:
  0.0 0.0 copy-start.4
  0.0 3.0 %collective-permute-start = (bf16[32,32,128]{2,1,0:T(8,128)(2,1)}, bf16[32,32,128]{2,1,0:T(8,128)(2,1)S(1)}, u32[]{:S(2)}, u32[]{:S(2)}) collective-permute-start(bf16[32,32,128]{2,1,0:T(8,128)(2,1)} %refs_0_.1), channel_id=1, source_target_pairs={{1,0},{0,1},{3,2},{2,3},{5,4},{4,5},{7,6},{6,7},{9,8},{8,9},{11,10... | collective-permute-start | bytes 786440 | tf_op jit(solution)/shard_map/ppermute | solution.py:348
  3.0 0.7 %multiply_divide_fusion = f32[16]{0:T(128)S(1)} fusion(s32[16]{0:T(128)} %param.13), kind=kLoop, calls=%fused_computation.5 | loop fusion | flops 48 | bytes 128 | tf_op jit(solution)/shard_map/div | solution.py:354
  3.6 0.0 copy-done.4
  3.6 0.0 copy-start.3
  3.6 0.8 %fusion.1 = (f32[16,256]{1,0:T(8,128)S(1)}, f32[16,256]{1,0:T(8,128)S(1)}) fusion(f32[16,256]{1,0:T(8,128)} %param.11, f32[16,256]{1,0:T(8,128)} %param.12, s32[16]{0:T(128)S(1)} %copy-done.4), kind=kLoop, calls=%fused_computation.6 | loop fusion | flops 12288 | bytes 65600 | tf_op jit(solution)/shard_map/mul | solution.py:352
  4.5 0.1 broadcast_in_dim.39
  4.5 0.0 copy-done.3
  4.6 0.1 select_select_fusion.table_ref
  4.6 0.1 broadcast_in_dim.40.inverse_ref
  4.7 0.0 collective-permute-start.1
  4.7 2.0 %collective-permute-start.3 = (f32[2,8,128]{2,1,0:T(8,128)S(1)}, f32[2,8,128]{2,1,0:T(8,128)S(1)}, u32[]{:S(2)}, u32[]{:S(2)}) collective-permute-start(f32[2,8,128]{2,1,0:T(8,128)S(1)} %broadcast_in_dim.40.inverse_ref), channel_id=1, source_target_pairs={{2,0},{0,1},{4,2},{1,3},{6,4},{3,5},{8,6},{5,7},{10,8},{7,9},{12,1... | collective-permute-start | bytes 24584 | tf_op jit(solution)/shard_map/ppermute | solution.py:359
  6.7 0.0 copy-start
  6.7 0.9 %copy-done = bf16[32,32,128]{2,1,0:T(8,128)(2,1)S(1)} copy-done((bf16[32,32,128]{2,1,0:T(8,128)(2,1)S(1)}, bf16[32,32,128]{2,1,0:T(8,128)(2,1)}, u32[]{:S(2)}) %copy-start) | copy-done | bytes 262168
  7.7 0.0 copy-start.1
  7.7 0.5 %fields.1 = (f32[2,32,128]{2,1,0:T(8,128)S(1)}, f32[32,128]{1,0:T(8,128)S(1)}) custom-call(f32[3,16,256]{2,1,0:T(8,128)S(1)} %select_select_fusion.table_ref, bf16[32,32,128]{2,1,0:T(8,128)(2,1)S(1)} %copy-done), custom_call_target="tpu_custom_call" | custom-call | tf_op jit(solution)/shard_map/fields/pallas_call | solution.py:360
  8.2 1.4 %collective-permute-done.1.refs_4_ = f32[2,8,128]{2,1,0:T(8,128)S(1)} collective-permute-done((f32[2,8,128]{2,1,0:T(8,128)S(1)}, f32[2,8,128]{2,1,0:T(8,128)S(1)}, u32[]{:S(2)}, u32[]{:S(2)}) %collective-permute-start.1) | collective-permute-done | bytes 8224 | tf_op jit(solution)/shard_map/ppermute | solution.py:359
  9.6 0.0 collective-permute-done.refs_1_
  9.6 0.0 copy-done.1
  9.6 0.0 copy-start.2
  9.6 1.8 %first_gram.1 = (bf16[32,64,128]{2,1,0:T(8,128)(2,1)S(1)}, f32[2,32,128]{2,1,0:T(8,128)S(1)}, bf16[400,128]{1,0:T(8,128)(2,1)S(1)}) custom-call(bf16[32,32,128]{2,1,0:T(8,128)(2,1)S(1)} %copy-done.1, bf16[32,32,128]{2,1,0:T(8,128)(2,1)S(1)} %collective-permute-done.refs_1_, f32[32,128]{1,0:T(8,128)S(1)} %get-tuple-element.15.refs_2_, ...), custom_call_target="tpu_custom_call" | custom-call | tf_op jit(solution)/shard_map/first_gram/pallas_call | solution.py:369
  11.4 1.7 %collective-permute-start.2 = (bf16[400,128]{1,0:T(8,128)(2,1)S(1)}, bf16[400,128]{1,0:T(8,128)(2,1)S(1)}, u32[]{:S(2)}, u32[]{:S(2)}) collective-permute-start(bf16[400,128]{1,0:T(8,128)(2,1)S(1)} %get-tuple-element.21), channel_id=1, source_target_pairs={{0,1},{1,3},{2,0},{3,5},{4,2},{5,7},{6,4},{7,9},{8,6},{9,11},{10,8... | collective-permute-start | bytes 307208 | tf_op jit(solution)/shard_map/ppermute | solution.py:376
  13.1 0.0 collective-permute-done.3.inverse_ref
  13.1 1.4 %second_gram.1 = bf16[400,128]{1,0:T(8,128)(2,1)S(1)} custom-call(bf16[32,64,128]{2,1,0:T(8,128)(2,1)S(1)} %get-tuple-element.20.rows_ref, f32[2,32,128]{2,1,0:T(8,128)S(1)} %get-tuple-element.18.after_ref.held_ref, f32[2,8,128]{2,1,0:T(8,128)S(1)} %collective-permute-done.3.inverse_ref), custom_call_target="tpu_custom_call" | custom-call | tf_op jit(solution)/shard_map/second_gram/pallas_call | solution.py:377
  14.6 0.1 collective-permute-start.4
  14.6 0.0 copy-done.2
  14.6 0.7 %state.1 = (bf16[32,64,128]{2,1,0:T(8,128)(2,1)S(1)}, f32[32,128]{1,0:T(8,128)S(1)}) custom-call(f32[2,32,128]{2,1,0:T(8,128)S(1)} %get-tuple-element.18.after_ref.held_ref, bf16[64,32,128]{2,1,0:T(8,128)(2,1)S(1)} %bitcast.1), custom_call_target="tpu_custom_call" | custom-call | tf_op jit(solution)/shard_map/state/pallas_call | solution.py:379
  15.4 0.0 collective-permute-done.2.first_ref
  15.4 2.5 %own_gram.1.total_ref = f32[392,128]{1,0:T(8,128)S(1)} custom-call(f32[32,128]{1,0:T(8,128)S(1)} %get-tuple-element.19.after_ref.mean_ref, bf16[32,64,128]{2,1,0:T(8,128)(2,1)S(1)} %get-tuple-element.20.rows_ref, f32[2,32,128]{2,1,0:T(8,128)S(1)} %get-tuple-element.18.after_ref.held_ref, f32[2,8,128]{2,1,0:T(8,128)S(1)} %broadcast_in_dim.40.inverse_ref, ...), custom_call_target="tpu_custom_call" | custom-call | tf_op jit(solution)/shard_map/own_gram/pallas_call | solution.py:387
  17.9 1.4 %collective-permute-done.4.second_ref = bf16[400,128]{1,0:T(8,128)(2,1)S(1)} collective-permute-done((bf16[400,128]{1,0:T(8,128)(2,1)S(1)}, bf16[400,128]{1,0:T(8,128)(2,1)S(1)}, u32[]{:S(2)}, u32[]{:S(2)}) %collective-permute-start.4) | collective-permute-done | bytes 102432 | tf_op jit(solution)/shard_map/ppermute | solution.py:378
  19.3 4.0 %finish.1 = bf16[1,64,32,128]{3,2,1,0:T(8,128)(2,1)} custom-call(f32[392,128]{1,0:T(8,128)S(1)} %own_gram.1.total_ref, bf16[400,128]{1,0:T(8,128)(2,1)S(1)} %collective-permute-done.4.second_ref, bf16[32,64,128]{2,1,0:T(8,128)(2,1)S(1)} %get-tuple-element.22.lag_ref, f32[32,128]{1,0:T(8,128)S(1)} %get-tuple-element.19.after_ref.mean_ref), custom_call_target="tpu_custom_call" | custom-call | tf_op jit(solution)/shard_map/finish/pallas_call | solution.py:388
  (2 shorter events, 0.0 us)
Async XLA Ops:
  0.0 3.6 %copy-start.4 = (s32[16]{0:T(128)S(1)}, s32[16]{0:T(128)}, u32[]{:S(2)}) copy-start(s32[16]{0:T(128)} %param.10) | copy-start | bytes 196
  0.0 9.6 %collective-permute-start = (bf16[32,32,128]{2,1,0:T(8,128)(2,1)}, bf16[32,32,128]{2,1,0:T(8,128)(2,1)S(1)}, u32[]{:S(2)}, u32[]{:S(2)}) collective-permute-start(bf16[32,32,128]{2,1,0:T(8,128)(2,1)} %refs_0_.1), channel_id=1, source_target_pairs={{1,0},{0,1},{3,2},{2,3},{5,4},{4,5},{7,6},{6,7},{9,8},{8,9},{11,10... | collective-permute-start | bytes 786440 | tf_op jit(solution)/shard_map/ppermute | solution.py:348
  3.6 0.9 %copy-start.3 = (s32[16,256]{1,0:T(8,128)S(1)}, s32[16,256]{1,0:T(8,128)}, u32[]{:S(2)}) copy-start(s32[16,256]{1,0:T(8,128)} %param.9) | copy-start | bytes 49156
  4.7 4.9 %collective-permute-start.1 = (f32[2,8,128]{2,1,0:T(8,128)S(1)}, f32[2,8,128]{2,1,0:T(8,128)S(1)}, u32[]{:S(2)}, u32[]{:S(2)}) collective-permute-start(f32[2,8,128]{2,1,0:T(8,128)S(1)} %broadcast_in_dim.40.inverse_ref), channel_id=1, source_target_pairs={{1,0},{3,1},{0,2},{5,3},{2,4},{7,5},{4,6},{9,7},{6,8},{11,9},{8,10... | collective-permute-start | bytes 24584 | tf_op jit(solution)/shard_map/ppermute | solution.py:359
  4.7 8.4 %collective-permute-start.3 = (f32[2,8,128]{2,1,0:T(8,128)S(1)}, f32[2,8,128]{2,1,0:T(8,128)S(1)}, u32[]{:S(2)}, u32[]{:S(2)}) collective-permute-start(f32[2,8,128]{2,1,0:T(8,128)S(1)} %broadcast_in_dim.40.inverse_ref), channel_id=1, source_target_pairs={{2,0},{0,1},{4,2},{1,3},{6,4},{3,5},{8,6},{5,7},{10,8},{7,9},{12,1... | collective-permute-start | bytes 24584 | tf_op jit(solution)/shard_map/ppermute | solution.py:359
  6.7 0.9 %copy-start = (bf16[32,32,128]{2,1,0:T(8,128)(2,1)S(1)}, bf16[32,32,128]{2,1,0:T(8,128)(2,1)}, u32[]{:S(2)}) copy-start(bf16[32,32,128]{2,1,0:T(8,128)(2,1)} %refs_0_.1) | copy-start | bytes 786436
  7.7 1.9 %copy-start.1 = (bf16[32,32,128]{2,1,0:T(8,128)(2,1)S(1)}, bf16[32,32,128]{2,1,0:T(8,128)(2,1)}, u32[]{:S(2)}) copy-start(bf16[32,32,128]{2,1,0:T(8,128)(2,1)} %refs_0_.1) | copy-start | bytes 786436
  9.6 5.1 %copy-start.2 = (bf16[1,64,32,128]{3,2,1,0:T(8,128)(2,1)S(1)}, bf16[1,64,32,128]{3,2,1,0:T(8,128)(2,1)}, u32[]{:S(2)}) copy-start(bf16[1,64,32,128]{3,2,1,0:T(8,128)(2,1)} %param.7) | copy-start | bytes 1572868
  11.4 4.0 %collective-permute-start.2 = (bf16[400,128]{1,0:T(8,128)(2,1)S(1)}, bf16[400,128]{1,0:T(8,128)(2,1)S(1)}, u32[]{:S(2)}, u32[]{:S(2)}) collective-permute-start(bf16[400,128]{1,0:T(8,128)(2,1)S(1)} %get-tuple-element.21), channel_id=1, source_target_pairs={{0,1},{1,3},{2,0},{3,5},{4,2},{5,7},{6,4},{7,9},{8,6},{9,11},{10,8... | collective-permute-start | bytes 307208 | tf_op jit(solution)/shard_map/ppermute | solution.py:376
  14.6 4.7 %collective-permute-start.4 = (bf16[400,128]{1,0:T(8,128)(2,1)S(1)}, bf16[400,128]{1,0:T(8,128)(2,1)S(1)}, u32[]{:S(2)}, u32[]{:S(2)}) collective-permute-start(bf16[400,128]{1,0:T(8,128)(2,1)S(1)} %second_gram.1), channel_id=1, source_target_pairs={{0,2},{1,0},{2,4},{3,1},{4,6},{5,3},{6,8},{7,5},{8,10},{9,7},{10,1... | collective-permute-start | bytes 307208 | tf_op jit(solution)/shard_map/ppermute | solution.py:378

commit v7 on v6

--- a/solution.py
+++ b/solution.py
@@ -69,8 +69,8 @@
         lag_ref[r] = flat_ref[pl.ds(r, members, stride=tile_rows), :].astype(bf16)
 
 
-def half_of_lags():
-    return lax.axis_index("lag") // (lax.axis_size("lag") // 2)
+def down_first():
+    return 1 - lax.axis_index("lag") // (lax.axis_size("lag") // 2)
 
 
 def ring(tiles, shares, turn):
@@ -78,7 +78,7 @@
     pairs = []
     for t in range(tiles):
         for l in range(shares):
-            target = t + (1 if (l // half) ^ turn else -1)
+            target = t + (-1 if (l // half) ^ turn else 1)
             if 0 <= target < tiles:
                 pairs.append((t * shares + l, target * shares + l))
             else:
@@ -170,14 +170,14 @@
 
 def arrived(ref, turn, side_count):
     tile = lax.axis_index("dom")
-    there = jnp.where(half_of_lags() ^ turn == 1, tile > 0, tile < lax.axis_size("dom") - 1)
+    there = jnp.where(down_first() ^ turn == 1, tile > 0, tile < lax.axis_size("dom") - 1)
     return jnp.where(there, read_message(ref, side_count), 0.0)
 
 
 def outward(turn, rows_ref, held_ref, inverse_ref, message_ref, total_ref):
     tile_rows, members, cols = rows_ref.shape
     patch_cols = cols // PATCH
-    down = half_of_lags() ^ turn
+    down = down_first() ^ turn
     near = pl.multiple_of(down * (tile_rows - NEAR), 8)
     middle = jnp.where(down == 0, MIDDLE - PATCH, MIDDLE + tile_rows)
     plans = [

time: 23.5 us -> 22.7 us (0.966)
  starting transfers between devices: 6.79 us -> 5.6 us
  waiting for transfers between devices: 2.82 us -> 3.23 us
    ppermute x1, starting transfers between devices: 0.06 us -> 2.06 us  [shards(): second = lax.ppermute(message, axes, rings[1])]
    ppermute x1, starting transfers between devices: 1.74 us -> 0.06 us  [shards(): first = lax.ppermute(message, axes, rings[0])]
    ppermute x2, starting transfers between devices: 2.02 us -> 0.51 us  [shards(): lax.ppermute(sent, axes, [(t, s) for s, t in pairs])]
    ppermute x1, waiting for transfers between devices: 1.41 us -> 0.01 us  [shards(): second = lax.ppermute(message, axes, rings[1])]
    ppermute x2, waiting for transfers between devices: 1.4 us -> 2.2 us  [shards(): lax.ppermute(sent, axes, [(t, s) for s, t in pairs])]
    ppermute x1, waiting for transfers between devices: 0.01 us -> 0.63 us  [shards(): lax.ppermute(forecast, 'lag', [((i + k) % shares, i) for i in range(share...]
    ppermute x1, waiting for transfers between devices: 0.01 us -> 0.4 us  [shards(): first = lax.ppermute(message, axes, rings[0])]
  transfers between devices with their start and end apart: 5 -> 5, of which waited for: 2 -> 3; matrix products, arithmetic and copies ran while one was open for 7% -> 8% of each run, Pallas kernels for 30% -> 31%
where the time goes in v7:
time: 22.7 us; the launch traced here: 22.5 us
  Pallas kernels  10.9 us (48%)
  starting transfers between devices  5.6 us (25%)
  waiting for transfers between devices  3.23 us (14%)
  other arithmetic  1.57 us (7%)
  local copies, waits for them, and re-layouts  1.12 us (5%)
    pallas_call x1, Pallas kernels, shards(): call(finish_kernel, 'finish', [vmem] * 4, shape((1, members, tile_rows, c...  3.95 us
    ppermute x1, starting transfers between devices, shards(): lax.ppermute(forecast, 'lag', [((i + k) % shares, i) for i in range(share...  2.97 us
    pallas_call x1, Pallas kernels, shards(): call(own_kernel, 'own_gram', [vmem] * 5, own_shape)  2.48 us
    ppermute x2, waiting for transfers between devices, shards(): lax.ppermute(sent, axes, [(t, s) for s, t in pairs])  2.2 us
    ppermute x1, starting transfers between devices, shards(): second = lax.ppermute(message, axes, rings[1])  2.06 us
    pallas_call x1, Pallas kernels, shards(): call(functools.partial(first_kernel, shares), 'first_gram', [vmem] * (sha...  1.82 us
    pallas_call x1, Pallas kernels, shards(): call(second_kernel, 'second_gram', [vmem] * 3, message_shape, [total_scra...  1.45 us
    unnamed x10, local copies, waits for them, and re-layouts  0.96 us
  transfers between devices with their start and end apart: 5, of which 3 were waited for; matrix products, arithmetic and copies ran while one was open for 8% of the time, Pallas kernels for 31%

profile of v7, /device:TPU:0, one launch (start us, length us, event | category | flops | bytes accessed | tf_op | source)
XLA Modules:
  0.0 22.5 jit_solution(887399048869179967)
XLA Ops:
  0.0 0.0 copy-start.4
  0.0 3.0 %collective-permute-start = (bf16[32,32,128]{2,1,0:T(8,128)(2,1)}, bf16[32,32,128]{2,1,0:T(8,128)(2,1)S(1)}, u32[]{:S(2)}, u32[]{:S(2)}) collective-permute-start(bf16[32,32,128]{2,1,0:T(8,128)(2,1)} %refs_0_.1), channel_id=1, source_target_pairs={{1,0},{0,1},{3,2},{2,3},{5,4},{4,5},{7,6},{6,7},{9,8},{8,9},{11,10... | collective-permute-start | bytes 786440 | tf_op jit(solution)/shard_map/ppermute | solution.py:348
  3.0 0.7 %multiply_divide_fusion = f32[16]{0:T(128)S(1)} fusion(s32[16]{0:T(128)} %param.13), kind=kLoop, calls=%fused_computation.5 | loop fusion | flops 48 | bytes 128 | tf_op jit(solution)/shard_map/div | solution.py:354
  3.6 0.0 copy-done.4
  3.6 0.0 copy-start.3
  3.6 0.8 %fusion.1 = (f32[16,256]{1,0:T(8,128)S(1)}, f32[16,256]{1,0:T(8,128)S(1)}) fusion(f32[16,256]{1,0:T(8,128)} %param.11, f32[16,256]{1,0:T(8,128)} %param.12, s32[16]{0:T(128)S(1)} %copy-done.4), kind=kLoop, calls=%fused_computation.6 | loop fusion | flops 12288 | bytes 65600 | tf_op jit(solution)/shard_map/mul | solution.py:352
  4.5 0.1 broadcast_in_dim.39
  4.5 0.0 copy-done.3
  4.6 0.1 select_select_fusion.table_ref
  4.6 0.1 broadcast_in_dim.40.inverse_ref
  4.7 0.0 collective-permute-start.1
  4.7 0.5 %collective-permute-start.3 = (f32[2,8,128]{2,1,0:T(8,128)S(1)}, f32[2,8,128]{2,1,0:T(8,128)S(1)}, u32[]{:S(2)}, u32[]{:S(2)}) collective-permute-start(f32[2,8,128]{2,1,0:T(8,128)S(1)} %broadcast_in_dim.40.inverse_ref), channel_id=1, source_target_pairs={{1,0},{3,1},{0,2},{5,3},{2,4},{7,5},{4,6},{9,7},{6,8},{11,9},{8,10... | collective-permute-start | bytes 24584 | tf_op jit(solution)/shard_map/ppermute | solution.py:359
  5.2 0.0 copy-start
  5.2 0.9 %copy-done = bf16[32,32,128]{2,1,0:T(8,128)(2,1)S(1)} copy-done((bf16[32,32,128]{2,1,0:T(8,128)(2,1)S(1)}, bf16[32,32,128]{2,1,0:T(8,128)(2,1)}, u32[]{:S(2)}) %copy-start) | copy-done | bytes 262168
  6.2 0.0 copy-start.1
  6.2 0.5 %fields.1 = (f32[2,32,128]{2,1,0:T(8,128)S(1)}, f32[32,128]{1,0:T(8,128)S(1)}) custom-call(f32[3,16,256]{2,1,0:T(8,128)S(1)} %select_select_fusion.table_ref, bf16[32,32,128]{2,1,0:T(8,128)(2,1)S(1)} %copy-done), custom_call_target="tpu_custom_call" | custom-call | tf_op jit(solution)/shard_map/fields/pallas_call | solution.py:360
  6.7 2.2 %collective-permute-done.1.refs_4_ = f32[2,8,128]{2,1,0:T(8,128)S(1)} collective-permute-done((f32[2,8,128]{2,1,0:T(8,128)S(1)}, f32[2,8,128]{2,1,0:T(8,128)S(1)}, u32[]{:S(2)}, u32[]{:S(2)}) %collective-permute-start.1) | collective-permute-done | bytes 8224 | tf_op jit(solution)/shard_map/ppermute | solution.py:359
  8.9 0.6 %collective-permute-done.refs_1_ = bf16[32,32,128]{2,1,0:T(8,128)(2,1)S(1)} collective-permute-done((bf16[32,32,128]{2,1,0:T(8,128)(2,1)}, bf16[32,32,128]{2,1,0:T(8,128)(2,1)S(1)}, u32[]{:S(2)}, u32[]{:S(2)}) %collective-permute-start) | collective-permute-done | bytes 262176 | tf_op jit(solution)/shard_map/ppermute | solution.py:348
  9.5 0.0 copy-done.1
  9.5 0.0 copy-start.2
  9.5 1.8 %first_gram.1 = (bf16[32,64,128]{2,1,0:T(8,128)(2,1)S(1)}, f32[2,32,128]{2,1,0:T(8,128)S(1)}, bf16[400,128]{1,0:T(8,128)(2,1)S(1)}) custom-call(bf16[32,32,128]{2,1,0:T(8,128)(2,1)S(1)} %copy-done.1, bf16[32,32,128]{2,1,0:T(8,128)(2,1)S(1)} %collective-permute-done.refs_1_, f32[32,128]{1,0:T(8,128)S(1)} %get-tuple-element.15.refs_2_, ...), custom_call_target="tpu_custom_call" | custom-call | tf_op jit(solution)/shard_map/first_gram/pallas_call | solution.py:369
  11.3 0.1 collective-permute-start.2
  11.4 0.0 collective-permute-done.3.inverse_ref
  11.4 1.4 %second_gram.1 = bf16[400,128]{1,0:T(8,128)(2,1)S(1)} custom-call(bf16[32,64,128]{2,1,0:T(8,128)(2,1)S(1)} %get-tuple-element.20.rows_ref, f32[2,32,128]{2,1,0:T(8,128)S(1)} %get-tuple-element.18.after_ref.held_ref, f32[2,8,128]{2,1,0:T(8,128)S(1)} %collective-permute-done.3.inverse_ref), custom_call_target="tpu_custom_call" | custom-call | tf_op jit(solution)/shard_map/second_gram/pallas_call | solution.py:377
  12.8 2.1 %collective-permute-start.4 = (bf16[400,128]{1,0:T(8,128)(2,1)S(1)}, bf16[400,128]{1,0:T(8,128)(2,1)S(1)}, u32[]{:S(2)}, u32[]{:S(2)}) collective-permute-start(bf16[400,128]{1,0:T(8,128)(2,1)S(1)} %second_gram.1), channel_id=1, source_target_pairs={{0,1},{1,3},{2,0},{3,5},{4,2},{5,7},{6,4},{7,9},{8,6},{9,11},{10,8... | collective-permute-start | bytes 307208 | tf_op jit(solution)/shard_map/ppermute | solution.py:378
  14.9 0.0 copy-done.2
  14.9 0.7 %state.1 = (bf16[32,64,128]{2,1,0:T(8,128)(2,1)S(1)}, f32[32,128]{1,0:T(8,128)S(1)}) custom-call(f32[2,32,128]{2,1,0:T(8,128)S(1)} %get-tuple-element.18.after_ref.held_ref, bf16[64,32,128]{2,1,0:T(8,128)(2,1)S(1)} %bitcast.1), custom_call_target="tpu_custom_call" | custom-call | tf_op jit(solution)/shard_map/state/pallas_call | solution.py:379
  15.6 0.4 %collective-permute-done.2.first_ref = bf16[400,128]{1,0:T(8,128)(2,1)S(1)} collective-permute-done((bf16[400,128]{1,0:T(8,128)(2,1)S(1)}, bf16[400,128]{1,0:T(8,128)(2,1)S(1)}, u32[]{:S(2)}, u32[]{:S(2)}) %collective-permute-start.2) | collective-permute-done | bytes 102432 | tf_op jit(solution)/shard_map/ppermute | solution.py:376
  16.0 2.5 %own_gram.1.total_ref = f32[392,128]{1,0:T(8,128)S(1)} custom-call(f32[32,128]{1,0:T(8,128)S(1)} %get-tuple-element.19.after_ref.mean_ref, bf16[32,64,128]{2,1,0:T(8,128)(2,1)S(1)} %get-tuple-element.20.rows_ref, f32[2,32,128]{2,1,0:T(8,128)S(1)} %get-tuple-element.18.after_ref.held_ref, f32[2,8,128]{2,1,0:T(8,128)S(1)} %broadcast_in_dim.40.inverse_ref, ...), custom_call_target="tpu_custom_call" | custom-call | tf_op jit(solution)/shard_map/own_gram/pallas_call | solution.py:387
  18.5 0.0 collective-permute-done.4.second_ref
  18.5 4.0 %finish.1 = bf16[1,64,32,128]{3,2,1,0:T(8,128)(2,1)} custom-call(f32[392,128]{1,0:T(8,128)S(1)} %own_gram.1.total_ref, bf16[400,128]{1,0:T(8,128)(2,1)S(1)} %collective-permute-done.4.second_ref, bf16[32,64,128]{2,1,0:T(8,128)(2,1)S(1)} %get-tuple-element.22.lag_ref, f32[32,128]{1,0:T(8,128)S(1)} %get-tuple-element.19.after_ref.mean_ref), custom_call_target="tpu_custom_call" | custom-call | tf_op jit(solution)/shard_map/finish/pallas_call | solution.py:388
  (2 shorter events, 0.0 us)
Async XLA Ops:
  0.0 3.6 %copy-start.4 = (s32[16]{0:T(128)S(1)}, s32[16]{0:T(128)}, u32[]{:S(2)}) copy-start(s32[16]{0:T(128)} %param.10) | copy-start | bytes 196
  0.0 9.5 %collective-permute-start = (bf16[32,32,128]{2,1,0:T(8,128)(2,1)}, bf16[32,32,128]{2,1,0:T(8,128)(2,1)S(1)}, u32[]{:S(2)}, u32[]{:S(2)}) collective-permute-start(bf16[32,32,128]{2,1,0:T(8,128)(2,1)} %refs_0_.1), channel_id=1, source_target_pairs={{1,0},{0,1},{3,2},{2,3},{5,4},{4,5},{7,6},{6,7},{9,8},{8,9},{11,10... | collective-permute-start | bytes 786440 | tf_op jit(solution)/shard_map/ppermute | solution.py:348
  3.6 0.9 %copy-start.3 = (s32[16,256]{1,0:T(8,128)S(1)}, s32[16,256]{1,0:T(8,128)}, u32[]{:S(2)}) copy-start(s32[16,256]{1,0:T(8,128)} %param.9) | copy-start | bytes 49156
  4.7 4.1 %collective-permute-start.1 = (f32[2,8,128]{2,1,0:T(8,128)S(1)}, f32[2,8,128]{2,1,0:T(8,128)S(1)}, u32[]{:S(2)}, u32[]{:S(2)}) collective-permute-start(f32[2,8,128]{2,1,0:T(8,128)S(1)} %broadcast_in_dim.40.inverse_ref), channel_id=1, source_target_pairs={{2,0},{0,1},{4,2},{1,3},{6,4},{3,5},{8,6},{5,7},{10,8},{7,9},{12,1... | collective-permute-start | bytes 24584 | tf_op jit(solution)/shard_map/ppermute | solution.py:359
  4.7 6.7 %collective-permute-start.3 = (f32[2,8,128]{2,1,0:T(8,128)S(1)}, f32[2,8,128]{2,1,0:T(8,128)S(1)}, u32[]{:S(2)}, u32[]{:S(2)}) collective-permute-start(f32[2,8,128]{2,1,0:T(8,128)S(1)} %broadcast_in_dim.40.inverse_ref), channel_id=1, source_target_pairs={{1,0},{3,1},{0,2},{5,3},{2,4},{7,5},{4,6},{9,7},{6,8},{11,9},{8,10... | collective-permute-start | bytes 24584 | tf_op jit(solution)/shard_map/ppermute | solution.py:359
  5.2 0.9 %copy-start = (bf16[32,32,128]{2,1,0:T(8,128)(2,1)S(1)}, bf16[32,32,128]{2,1,0:T(8,128)(2,1)}, u32[]{:S(2)}) copy-start(bf16[32,32,128]{2,1,0:T(8,128)(2,1)} %refs_0_.1) | copy-start | bytes 786436
  6.2 3.3 %copy-start.1 = (bf16[32,32,128]{2,1,0:T(8,128)(2,1)S(1)}, bf16[32,32,128]{2,1,0:T(8,128)(2,1)}, u32[]{:S(2)}) copy-start(bf16[32,32,128]{2,1,0:T(8,128)(2,1)} %refs_0_.1) | copy-start | bytes 786436
  9.5 5.4 %copy-start.2 = (bf16[1,64,32,128]{3,2,1,0:T(8,128)(2,1)S(1)}, bf16[1,64,32,128]{3,2,1,0:T(8,128)(2,1)}, u32[]{:S(2)}) copy-start(bf16[1,64,32,128]{3,2,1,0:T(8,128)(2,1)} %param.7) | copy-start | bytes 1572868
  11.3 4.7 %collective-permute-start.2 = (bf16[400,128]{1,0:T(8,128)(2,1)S(1)}, bf16[400,128]{1,0:T(8,128)(2,1)S(1)}, u32[]{:S(2)}, u32[]{:S(2)}) collective-permute-start(bf16[400,128]{1,0:T(8,128)(2,1)S(1)} %get-tuple-element.21), channel_id=1, source_target_pairs={{0,2},{1,0},{2,4},{3,1},{4,6},{5,3},{6,8},{7,5},{8,10},{9,7},{10,1... | collective-permute-start | bytes 307208 | tf_op jit(solution)/shard_map/ppermute | solution.py:376
  12.8 5.7 %collective-permute-start.4 = (bf16[400,128]{1,0:T(8,128)(2,1)S(1)}, bf16[400,128]{1,0:T(8,128)(2,1)S(1)}, u32[]{:S(2)}, u32[]{:S(2)}) collective-permute-start(bf16[400,128]{1,0:T(8,128)(2,1)S(1)} %second_gram.1), channel_id=1, source_target_pairs={{0,1},{1,3},{2,0},{3,5},{4,2},{5,7},{6,4},{7,9},{8,6},{9,11},{10,8... | collective-permute-start | bytes 307208 | tf_op jit(solution)/shard_map/ppermute | solution.py:378

commit v8 on v7

--- a/solution.py
+++ b/solution.py
@@ -113,7 +113,8 @@
     return total + mm(jnp.concatenate(lefts, 1), jnp.concatenate(anomalies, 1), NT)
 
 
-STEP = 8
+STEP = 16
+SMOOTH_STEP = 4
 
 
 def packed(totals, members, patch_cols):
@@ -310,12 +311,12 @@
         mixing = jnp.concatenate(
             [jnp.concatenate(mixings[2 * q : 2 * q + 2], 1) for q in range(a * quads, (a + 1) * quads)], 0
         )
-        for r in range(a * PATCH, (a + 1) * PATCH, 2):
+        for r in range(a * PATCH, (a + 1) * PATCH, SMOOTH_STEP):
             state = jnp.concatenate(
-                [jnp.concatenate([lag_ref[i] * mask for mask in masks], 0) for i in (r, r + 1)], 1
+                [jnp.concatenate([lag_ref[i] * mask for mask in masks], 0) for i in range(r, r + SMOOTH_STEP)], 1
             )
             spread_out = mm(mixing, state)
-            for i in (0, 1):
+            for i in range(SMOOTH_STEP):
                 part = spread_out[:, i * cols : (i + 1) * cols]
                 chosen = part[:members]
                 for q in range(1, quads):

time: 22.7 us -> 22.9 us (level)
  transfers between devices with their start and end apart: 5 -> 5, of which waited for: 3 -> 3; matrix products, arithmetic and copies ran while one was open for 8% -> 8% of each run, Pallas kernels for 31% -> 32%
where the time goes in v8:
time: 22.9 us; the launch traced here: 22.6 us
  Pallas kernels  11.1 us (48%)
  starting transfers between devices  5.61 us (24%)
  waiting for transfers between devices  3.22 us (14%)
  other arithmetic  1.57 us (7%)
  local copies, waits for them, and re-layouts  1.12 us (5%)
    pallas_call x1, Pallas kernels, shards(): call(finish_kernel, 'finish', [vmem] * 4, shape((1, members, tile_rows, c...  3.95 us
    ppermute x1, starting transfers between devices, shards(): lax.ppermute(forecast, 'lag', [((i + k) % shares, i) for i in range(share...  2.97 us
    pallas_call x1, Pallas kernels, shards(): call(own_kernel, 'own_gram', [vmem] * 5, own_shape)  2.48 us
    ppermute x2, waiting for transfers between devices, shards(): lax.ppermute(sent, axes, [(t, s) for s, t in pairs])  2.2 us
    ppermute x1, starting transfers between devices, shards(): second = lax.ppermute(message, axes, rings[1])  2.07 us
    pallas_call x1, Pallas kernels, shards(): call(functools.partial(first_kernel, shares), 'first_gram', [vmem] * (sha...  1.98 us
    pallas_call x1, Pallas kernels, shards(): call(second_kernel, 'second_gram', [vmem] * 3, message_shape, [total_scra...  1.45 us
    unnamed x10, local copies, waits for them, and re-layouts  0.96 us
  transfers between devices with their start and end apart: 5, of which 3 were waited for; matrix products, arithmetic and copies ran while one was open for 8% of the time, Pallas kernels for 32%

profile of v8, /device:TPU:0, one launch (start us, length us, event | category | flops | bytes accessed | tf_op | source)
XLA Modules:
  0.0 22.6 jit_solution(17177181745718334580)
XLA Ops:
  0.0 0.0 copy-start.4
  0.0 3.0 %collective-permute-start = (bf16[32,32,128]{2,1,0:T(8,128)(2,1)}, bf16[32,32,128]{2,1,0:T(8,128)(2,1)S(1)}, u32[]{:S(2)}, u32[]{:S(2)}) collective-permute-start(bf16[32,32,128]{2,1,0:T(8,128)(2,1)} %refs_0_.1), channel_id=1, source_target_pairs={{1,0},{0,1},{3,2},{2,3},{5,4},{4,5},{7,6},{6,7},{9,8},{8,9},{11,10... | collective-permute-start | bytes 786440 | tf_op jit(solution)/shard_map/ppermute | solution.py:349
  3.0 0.7 %multiply_divide_fusion = f32[16]{0:T(128)S(1)} fusion(s32[16]{0:T(128)} %param.13), kind=kLoop, calls=%fused_computation.5 | loop fusion | flops 48 | bytes 128 | tf_op jit(solution)/shard_map/div | solution.py:355
  3.6 0.0 copy-done.4
  3.6 0.0 copy-start.3
  3.6 0.8 %fusion.1 = (f32[16,256]{1,0:T(8,128)S(1)}, f32[16,256]{1,0:T(8,128)S(1)}) fusion(f32[16,256]{1,0:T(8,128)} %param.11, f32[16,256]{1,0:T(8,128)} %param.12, s32[16]{0:T(128)S(1)} %copy-done.4), kind=kLoop, calls=%fused_computation.6 | loop fusion | flops 12288 | bytes 65600 | tf_op jit(solution)/shard_map/mul | solution.py:353
  4.5 0.1 broadcast_in_dim.39
  4.5 0.0 copy-done.3
  4.6 0.1 select_select_fusion.table_ref
  4.6 0.1 broadcast_in_dim.40.inverse_ref
  4.7 0.0 collective-permute-start.1
  4.7 0.5 %collective-permute-start.3 = (f32[2,8,128]{2,1,0:T(8,128)S(1)}, f32[2,8,128]{2,1,0:T(8,128)S(1)}, u32[]{:S(2)}, u32[]{:S(2)}) collective-permute-start(f32[2,8,128]{2,1,0:T(8,128)S(1)} %broadcast_in_dim.40.inverse_ref), channel_id=1, source_target_pairs={{1,0},{3,1},{0,2},{5,3},{2,4},{7,5},{4,6},{9,7},{6,8},{11,9},{8,10... | collective-permute-start | bytes 24584 | tf_op jit(solution)/shard_map/ppermute | solution.py:360
  5.2 0.0 copy-start
  5.2 0.9 %copy-done = bf16[32,32,128]{2,1,0:T(8,128)(2,1)S(1)} copy-done((bf16[32,32,128]{2,1,0:T(8,128)(2,1)S(1)}, bf16[32,32,128]{2,1,0:T(8,128)(2,1)}, u32[]{:S(2)}) %copy-start) | copy-done | bytes 262168
  6.2 0.0 copy-start.1
  6.2 0.5 %fields.1 = (f32[2,32,128]{2,1,0:T(8,128)S(1)}, f32[32,128]{1,0:T(8,128)S(1)}) custom-call(f32[3,16,256]{2,1,0:T(8,128)S(1)} %select_select_fusion.table_ref, bf16[32,32,128]{2,1,0:T(8,128)(2,1)S(1)} %copy-done), custom_call_target="tpu_custom_call" | custom-call | tf_op jit(solution)/shard_map/fields/pallas_call | solution.py:361
  6.7 2.2 %collective-permute-done.1.refs_4_ = f32[2,8,128]{2,1,0:T(8,128)S(1)} collective-permute-done((f32[2,8,128]{2,1,0:T(8,128)S(1)}, f32[2,8,128]{2,1,0:T(8,128)S(1)}, u32[]{:S(2)}, u32[]{:S(2)}) %collective-permute-start.1) | collective-permute-done | bytes 8224 | tf_op jit(solution)/shard_map/ppermute | solution.py:360
  8.9 0.6 %collective-permute-done.refs_1_ = bf16[32,32,128]{2,1,0:T(8,128)(2,1)S(1)} collective-permute-done((bf16[32,32,128]{2,1,0:T(8,128)(2,1)}, bf16[32,32,128]{2,1,0:T(8,128)(2,1)S(1)}, u32[]{:S(2)}, u32[]{:S(2)}) %collective-permute-start) | collective-permute-done | bytes 262176 | tf_op jit(solution)/shard_map/ppermute | solution.py:349
  9.5 0.0 copy-done.1
  9.5 0.0 copy-start.2
  9.5 2.0 %first_gram.1 = (bf16[32,64,128]{2,1,0:T(8,128)(2,1)S(1)}, f32[2,32,128]{2,1,0:T(8,128)S(1)}, bf16[400,128]{1,0:T(8,128)(2,1)S(1)}) custom-call(bf16[32,32,128]{2,1,0:T(8,128)(2,1)S(1)} %copy-done.1, bf16[32,32,128]{2,1,0:T(8,128)(2,1)S(1)} %collective-permute-done.refs_1_, f32[32,128]{1,0:T(8,128)S(1)} %get-tuple-element.15.refs_2_, ...), custom_call_target="tpu_custom_call" | custom-call | tf_op jit(solution)/shard_map/first_gram/pallas_call | solution.py:370
  11.5 0.1 collective-permute-start.2
  11.5 0.0 collective-permute-done.3.inverse_ref
  11.6 1.5 %second_gram.1 = bf16[400,128]{1,0:T(8,128)(2,1)S(1)} custom-call(bf16[32,64,128]{2,1,0:T(8,128)(2,1)S(1)} %get-tuple-element.20.rows_ref, f32[2,32,128]{2,1,0:T(8,128)S(1)} %get-tuple-element.18.after_ref.held_ref, f32[2,8,128]{2,1,0:T(8,128)S(1)} %collective-permute-done.3.inverse_ref), custom_call_target="tpu_custom_call" | custom-call | tf_op jit(solution)/shard_map/second_gram/pallas_call | solution.py:378
  13.0 2.1 %collective-permute-start.4 = (bf16[400,128]{1,0:T(8,128)(2,1)S(1)}, bf16[400,128]{1,0:T(8,128)(2,1)S(1)}, u32[]{:S(2)}, u32[]{:S(2)}) collective-permute-start(bf16[400,128]{1,0:T(8,128)(2,1)S(1)} %second_gram.1), channel_id=1, source_target_pairs={{0,1},{1,3},{2,0},{3,5},{4,2},{5,7},{6,4},{7,9},{8,6},{9,11},{10,8... | collective-permute-start | bytes 307208 | tf_op jit(solution)/shard_map/ppermute | solution.py:379
  15.1 0.0 copy-done.2
  15.1 0.7 %state.1 = (bf16[32,64,128]{2,1,0:T(8,128)(2,1)S(1)}, f32[32,128]{1,0:T(8,128)S(1)}) custom-call(f32[2,32,128]{2,1,0:T(8,128)S(1)} %get-tuple-element.18.after_ref.held_ref, bf16[64,32,128]{2,1,0:T(8,128)(2,1)S(1)} %bitcast.1), custom_call_target="tpu_custom_call" | custom-call | tf_op jit(solution)/shard_map/state/pallas_call | solution.py:380
  15.8 0.4 %collective-permute-done.2.first_ref = bf16[400,128]{1,0:T(8,128)(2,1)S(1)} collective-permute-done((bf16[400,128]{1,0:T(8,128)(2,1)S(1)}, bf16[400,128]{1,0:T(8,128)(2,1)S(1)}, u32[]{:S(2)}, u32[]{:S(2)}) %collective-permute-start.2) | collective-permute-done | bytes 102432 | tf_op jit(solution)/shard_map/ppermute | solution.py:377
  16.2 2.5 %own_gram.1.total_ref = f32[392,128]{1,0:T(8,128)S(1)} custom-call(f32[32,128]{1,0:T(8,128)S(1)} %get-tuple-element.19.after_ref.mean_ref, bf16[32,64,128]{2,1,0:T(8,128)(2,1)S(1)} %get-tuple-element.20.rows_ref, f32[2,32,128]{2,1,0:T(8,128)S(1)} %get-tuple-element.18.after_ref.held_ref, f32[2,8,128]{2,1,0:T(8,128)S(1)} %broadcast_in_dim.40.inverse_ref, ...), custom_call_target="tpu_custom_call" | custom-call | tf_op jit(solution)/shard_map/own_gram/pallas_call | solution.py:388
  18.7 0.0 collective-permute-done.4.second_ref
  18.7 4.0 %finish.1 = bf16[1,64,32,128]{3,2,1,0:T(8,128)(2,1)} custom-call(f32[392,128]{1,0:T(8,128)S(1)} %own_gram.1.total_ref, bf16[400,128]{1,0:T(8,128)(2,1)S(1)} %collective-permute-done.4.second_ref, bf16[32,64,128]{2,1,0:T(8,128)(2,1)S(1)} %get-tuple-element.22.lag_ref, f32[32,128]{1,0:T(8,128)S(1)} %get-tuple-element.19.after_ref.mean_ref), custom_call_target="tpu_custom_call" | custom-call | tf_op jit(solution)/shard_map/finish/pallas_call | solution.py:389
  (2 shorter events, 0.0 us)
Async XLA Ops:
  0.0 3.6 %copy-start.4 = (s32[16]{0:T(128)S(1)}, s32[16]{0:T(128)}, u32[]{:S(2)}) copy-start(s32[16]{0:T(128)} %param.10) | copy-start | bytes 196
  0.0 9.5 %collective-permute-start = (bf16[32,32,128]{2,1,0:T(8,128)(2,1)}, bf16[32,32,128]{2,1,0:T(8,128)(2,1)S(1)}, u32[]{:S(2)}, u32[]{:S(2)}) collective-permute-start(bf16[32,32,128]{2,1,0:T(8,128)(2,1)} %refs_0_.1), channel_id=1, source_target_pairs={{1,0},{0,1},{3,2},{2,3},{5,4},{4,5},{7,6},{6,7},{9,8},{8,9},{11,10... | collective-permute-start | bytes 786440 | tf_op jit(solution)/shard_map/ppermute | solution.py:349
  3.6 0.9 %copy-start.3 = (s32[16,256]{1,0:T(8,128)S(1)}, s32[16,256]{1,0:T(8,128)}, u32[]{:S(2)}) copy-start(s32[16,256]{1,0:T(8,128)} %param.9) | copy-start | bytes 49156
  4.7 4.1 %collective-permute-start.1 = (f32[2,8,128]{2,1,0:T(8,128)S(1)}, f32[2,8,128]{2,1,0:T(8,128)S(1)}, u32[]{:S(2)}, u32[]{:S(2)}) collective-permute-start(f32[2,8,128]{2,1,0:T(8,128)S(1)} %broadcast_in_dim.40.inverse_ref), channel_id=1, source_target_pairs={{2,0},{0,1},{4,2},{1,3},{6,4},{3,5},{8,6},{5,7},{10,8},{7,9},{12,1... | collective-permute-start | bytes 24584 | tf_op jit(solution)/shard_map/ppermute | solution.py:360
  4.7 6.8 %collective-permute-start.3 = (f32[2,8,128]{2,1,0:T(8,128)S(1)}, f32[2,8,128]{2,1,0:T(8,128)S(1)}, u32[]{:S(2)}, u32[]{:S(2)}) collective-permute-start(f32[2,8,128]{2,1,0:T(8,128)S(1)} %broadcast_in_dim.40.inverse_ref), channel_id=1, source_target_pairs={{1,0},{3,1},{0,2},{5,3},{2,4},{7,5},{4,6},{9,7},{6,8},{11,9},{8,10... | collective-permute-start | bytes 24584 | tf_op jit(solution)/shard_map/ppermute | solution.py:360
  5.2 0.9 %copy-start = (bf16[32,32,128]{2,1,0:T(8,128)(2,1)S(1)}, bf16[32,32,128]{2,1,0:T(8,128)(2,1)}, u32[]{:S(2)}) copy-start(bf16[32,32,128]{2,1,0:T(8,128)(2,1)} %refs_0_.1) | copy-start | bytes 786436
  6.2 3.3 %copy-start.1 = (bf16[32,32,128]{2,1,0:T(8,128)(2,1)S(1)}, bf16[32,32,128]{2,1,0:T(8,128)(2,1)}, u32[]{:S(2)}) copy-start(bf16[32,32,128]{2,1,0:T(8,128)(2,1)} %refs_0_.1) | copy-start | bytes 786436
  9.5 5.6 %copy-start.2 = (bf16[1,64,32,128]{3,2,1,0:T(8,128)(2,1)S(1)}, bf16[1,64,32,128]{3,2,1,0:T(8,128)(2,1)}, u32[]{:S(2)}) copy-start(bf16[1,64,32,128]{3,2,1,0:T(8,128)(2,1)} %param.7) | copy-start | bytes 1572868
  11.5 4.7 %collective-permute-start.2 = (bf16[400,128]{1,0:T(8,128)(2,1)S(1)}, bf16[400,128]{1,0:T(8,128)(2,1)S(1)}, u32[]{:S(2)}, u32[]{:S(2)}) collective-permute-start(bf16[400,128]{1,0:T(8,128)(2,1)S(1)} %get-tuple-element.21), channel_id=1, source_target_pairs={{0,2},{1,0},{2,4},{3,1},{4,6},{5,3},{6,8},{7,5},{8,10},{9,7},{10,1... | collective-permute-start | bytes 307208 | tf_op jit(solution)/shard_map/ppermute | solution.py:377
  13.0 5.7 %collective-permute-start.4 = (bf16[400,128]{1,0:T(8,128)(2,1)S(1)}, bf16[400,128]{1,0:T(8,128)(2,1)S(1)}, u32[]{:S(2)}, u32[]{:S(2)}) collective-permute-start(bf16[400,128]{1,0:T(8,128)(2,1)S(1)} %second_gram.1), channel_id=1, source_target_pairs={{0,1},{1,3},{2,0},{3,5},{4,2},{5,7},{6,4},{7,9},{8,6},{9,11},{10,8... | collective-permute-start | bytes 307208 | tf_op jit(solution)/shard_map/ppermute | solution.py:379

commit v9 on v7

--- a/solution.py
+++ b/solution.py
@@ -59,7 +59,7 @@
         field_ref[1, rows, :] = total[2 * PATCH : 3 * PATCH] + total[3 * PATCH :]
 
 
-def state_kernel(after_ref, hist_ref, lag_ref, mean_ref, flat_ref):
+def state_kernel(hist_ref, lag_ref, mean_ref, flat_ref):
     members, tile_rows, cols = hist_ref.shape
     state = hist_ref[...].astype(f32)
     mean = jnp.sum(state, axis=0) / members
@@ -199,7 +199,7 @@
 
 def first_kernel(shares, *refs):
     parts, refs = refs[:shares], refs[shares:]
-    sum_ref, field_ref, inverse_ref, rows_ref, held_ref, message_ref, flat_ref, total_ref = refs
+    sum_ref, field_ref, inverse_ref, _, rows_ref, held_ref, message_ref, flat_ref, total_ref = refs
     share_members, tile_rows, cols = parts[0].shape
     members = share_members * shares
     lag = lax.axis_index("lag")
@@ -220,17 +220,26 @@
     outward(1, rows_ref, held_ref, inverse_ref, message_ref, total_ref)
 
 
-def own_kernel(after_ref, rows_ref, held_ref, inverse_ref, first_ref, out_ref):
-    tile_rows, members, cols = rows_ref.shape
-    patch_cols = cols // PATCH
-    plans = [taper_plan(MIDDLE + a * PATCH, inverse_ref[a]) for a in range(tile_rows // PATCH)]
+def own_sums(rows, rows_ref, held_ref, inverse_ref):
+    members, cols = rows_ref.shape[1:]
+    patch_rows, patch_cols = inverse_ref.shape[:2]
+    plans = [taper_plan(MIDDLE + a * PATCH, inverse_ref[a]) for a in range(patch_rows)]
     totals = [jnp.zeros((patch_cols * members + PATCH, members), f32) for _ in plans]
-    for start in range(0, tile_rows, STEP):
+    for start in range(rows.start, rows.stop, STEP):
         anomalies = [rows_ref[start + i] for i in range(STEP)]
         fields = [held_ref[k, start : start + STEP, :] for k in range(2)]
         totals = [accumulate(total, plan, anomalies, *fields, jnp.int32(start)) for total, plan in zip(totals, plans)]
-    sums = jnp.concatenate(packed(totals, members, patch_cols), 0)
-    out_ref[...] = sums + arrived(first_ref, 0, patch_cols)
+    return jnp.concatenate(packed(totals, members, patch_cols), 0)
+
+
+def upper_kernel(rows_ref, held_ref, inverse_ref, out_ref):
+    out_ref[...] = own_sums(slice(0, rows_ref.shape[0] // 2), rows_ref, held_ref, inverse_ref)
+
+
+def lower_kernel(upper_ref, rows_ref, held_ref, inverse_ref, first_ref, out_ref):
+    tile_rows = rows_ref.shape[0]
+    sums = own_sums(slice(tile_rows // 2, tile_rows), rows_ref, held_ref, inverse_ref)
+    out_ref[...] = upper_ref[...] + sums + arrived(first_ref, 0, inverse_ref.shape[1])
 
 
 def finish_kernel(total_ref, second_ref, lag_ref, mean_ref, out_ref, flat_ref):
@@ -366,25 +375,26 @@
     packed_rows = patch_cols * members * 3 // 4
     message_shape = shape((packed_rows + 2 * patch_cols, 2 * members), bf16)
     total_scratch = pltpu.VMEM((2, patch_cols * members + PATCH, members), f32)
+    lag_rows, lag_mean = call(
+        state_kernel,
+        "state",
+        [vmem],
+        [shape((tile_rows, members, cols), bf16), shape((tile_rows, cols), f32)],
+        [pltpu.VMEM((members * tile_rows, cols), f32)],
+    )(history[0])
     rows, held, message = call(
         functools.partial(first_kernel, shares),
         "first_gram",
-        [vmem] * (shares + 3),
+        [vmem] * (shares + 4),
         [shape((tile_rows, members, cols), bf16), shape((2, tile_rows, cols), f32), message_shape],
         [pltpu.VMEM((members * tile_rows, cols), f32), total_scratch],
-    )(*parts, own_sum, fields, next_inverses[0])
+    )(*parts, own_sum, fields, next_inverses[0], lag_mean)
     first = lax.ppermute(message, axes, rings[0])
     message = call(second_kernel, "second_gram", [vmem] * 3, message_shape, [total_scratch])(rows, held, next_inverses[1])
     second = lax.ppermute(message, axes, rings[1])
-    lag_rows, lag_mean = call(
-        state_kernel,
-        "state",
-        [vmem, vmem],
-        [shape((tile_rows, members, cols), bf16), shape((tile_rows, cols), f32)],
-        [pltpu.VMEM((members * tile_rows, cols), f32)],
-    )(held, history[0])
     own_shape = shape((packed_rows + patch_cols, 2 * members), f32)
-    own = call(own_kernel, "own_gram", [vmem] * 5, own_shape)(lag_mean, rows, held, inverse, first)
+    upper = call(upper_kernel, "upper_gram", [vmem] * 3, own_shape)(rows, held, inverse)
+    own = call(lower_kernel, "lower_gram", [vmem] * 5, own_shape)(upper, rows, held, inverse, first)
     return call(
         finish_kernel,
         "finish",

time: 22.7 us -> 22.7 us (level)
  the two profiles are of different devices: /device:TPU:0 before, /device:TPU:3 now
where the time goes in v9:
time: 22.7 us; the launch traced here: 22.4 us
  Pallas kernels  11.1 us (49%)
  starting transfers between devices  5.02 us (22%)
  local copies, waits for them, and re-layouts  2.37 us (10%)
  waiting for transfers between devices  2.24 us (10%)
  other arithmetic  1.57 us (7%)
    pallas_call x1, Pallas kernels, shards(): call(finish_kernel, 'finish', [vmem] * 4, shape((1, members, tile_rows, c...  3.95 us
    ppermute x2, starting transfers between devices, shards(): lax.ppermute(sent, axes, [(t, s) for s, t in pairs])  2.65 us
    ppermute x1, waiting for transfers between devices, shards(): second = lax.ppermute(message, axes, rings[1])  2.23 us
    unnamed x10, local copies, waits for them, and re-layouts  2.22 us
    pallas_call x1, Pallas kernels, shards(): call(functools.partial(first_kernel, shares), 'first_gram', [vmem] * (sha...  1.82 us
    pallas_call x1, Pallas kernels, shards(): call(second_kernel, 'second_gram', [vmem] * 3, message_shape, [total_scra...  1.45 us
    pallas_call x1, Pallas kernels, shards(): call(lower_kernel, 'lower_gram', [vmem] * 5, own_shape)  1.36 us
    pallas_call x1, Pallas kernels, shards(): call(upper_kernel, 'upper_gram', [vmem] * 3, own_shape)(rows, held, inverse)  1.36 us
  transfers between devices with their start and end apart: 5, of which 1 were waited for; matrix products, arithmetic and copies ran while one was open for 8% of the time, Pallas kernels for 32%

profile of v9, /device:TPU:3, one launch (start us, length us, event | category | flops | bytes accessed | tf_op | source)
XLA Modules:
  0.0 22.4 jit_solution(11530985853341773963)
XLA Ops:
  0.0 0.0 copy-start.4
  0.0 1.2 %collective-permute-start = (bf16[32,32,128]{2,1,0:T(8,128)(2,1)}, bf16[32,32,128]{2,1,0:T(8,128)(2,1)S(1)}, u32[]{:S(2)}, u32[]{:S(2)}) collective-permute-start(bf16[32,32,128]{2,1,0:T(8,128)(2,1)} %refs_0_.1), channel_id=1, source_target_pairs={{1,0},{0,1},{3,2},{2,3},{5,4},{4,5},{7,6},{6,7},{9,8},{8,9},{11,10... | collective-permute-start | bytes 786440 | tf_op jit(solution)/shard_map/ppermute | solution.py:357
  1.2 0.7 %multiply_divide_fusion = f32[16]{0:T(128)S(1)} fusion(s32[16]{0:T(128)} %param.13), kind=kLoop, calls=%fused_computation.5 | loop fusion | flops 48 | bytes 128 | tf_op jit(solution)/shard_map/div | solution.py:363
  1.9 0.0 copy-done.4
  1.9 0.0 copy-start.3
  1.9 0.8 %fusion.1 = (f32[16,256]{1,0:T(8,128)S(1)}, f32[16,256]{1,0:T(8,128)S(1)}) fusion(f32[16,256]{1,0:T(8,128)} %param.11, f32[16,256]{1,0:T(8,128)} %param.12, s32[16]{0:T(128)S(1)} %copy-done.4), kind=kLoop, calls=%fused_computation.6 | loop fusion | flops 12288 | bytes 65600 | tf_op jit(solution)/shard_map/mul | solution.py:361
  2.7 0.1 broadcast_in_dim.39
  2.8 0.0 copy-done.3
  2.8 0.1 select_select_fusion.table_ref
  2.9 0.1 broadcast_in_dim.40.inverse_ref
  3.0 1.0 %collective-permute-start.1 = (f32[2,8,128]{2,1,0:T(8,128)S(1)}, f32[2,8,128]{2,1,0:T(8,128)S(1)}, u32[]{:S(2)}, u32[]{:S(2)}) collective-permute-start(f32[2,8,128]{2,1,0:T(8,128)S(1)} %broadcast_in_dim.40.inverse_ref), channel_id=1, source_target_pairs={{2,0},{0,1},{4,2},{1,3},{6,4},{3,5},{8,6},{5,7},{10,8},{7,9},{12,1... | collective-permute-start | bytes 24584 | tf_op jit(solution)/shard_map/ppermute | solution.py:368
  3.9 1.7 %collective-permute-start.3 = (f32[2,8,128]{2,1,0:T(8,128)S(1)}, f32[2,8,128]{2,1,0:T(8,128)S(1)}, u32[]{:S(2)}, u32[]{:S(2)}) collective-permute-start(f32[2,8,128]{2,1,0:T(8,128)S(1)} %broadcast_in_dim.40.inverse_ref), channel_id=1, source_target_pairs={{1,0},{3,1},{0,2},{5,3},{2,4},{7,5},{4,6},{9,7},{6,8},{11,9},{8,10... | collective-permute-start | bytes 24584 | tf_op jit(solution)/shard_map/ppermute | solution.py:368
  5.6 0.0 copy-start
  5.6 0.9 %copy-done = bf16[32,32,128]{2,1,0:T(8,128)(2,1)S(1)} copy-done((bf16[32,32,128]{2,1,0:T(8,128)(2,1)S(1)}, bf16[32,32,128]{2,1,0:T(8,128)(2,1)}, u32[]{:S(2)}) %copy-start) | copy-done | bytes 262168
  6.6 0.5 %fields.1 = (f32[2,32,128]{2,1,0:T(8,128)S(1)}, f32[32,128]{1,0:T(8,128)S(1)}) custom-call(f32[3,16,256]{2,1,0:T(8,128)S(1)} %select_select_fusion.table_ref, bf16[32,32,128]{2,1,0:T(8,128)(2,1)S(1)} %copy-done), custom_call_target="tpu_custom_call" | custom-call | tf_op jit(solution)/shard_map/fields/pallas_call | solution.py:369
  7.1 0.0 copy-start.2
  7.1 1.1 %copy-done.2 = bf16[1,64,32,128]{3,2,1,0:T(8,128)(2,1)S(1)} copy-done((bf16[1,64,32,128]{3,2,1,0:T(8,128)(2,1)S(1)}, bf16[1,64,32,128]{3,2,1,0:T(8,128)(2,1)}, u32[]{:S(2)}) %copy-start.2) | copy-done | bytes 524312
  8.1 0.0 copy-start.1
  8.1 0.7 %state.1 = (bf16[32,64,128]{2,1,0:T(8,128)(2,1)S(1)}, f32[32,128]{1,0:T(8,128)S(1)}) custom-call(bf16[64,32,128]{2,1,0:T(8,128)(2,1)S(1)} %bitcast.1), custom_call_target="tpu_custom_call" | custom-call | tf_op jit(solution)/shard_map/state/pallas_call | solution.py:378
  8.9 0.0 collective-permute-done.1.refs_4_
  8.9 0.0 collective-permute-done.refs_1_
  8.9 0.2 copy-done.1
  9.1 1.8 %first_gram.1 = (bf16[32,64,128]{2,1,0:T(8,128)(2,1)S(1)}, f32[2,32,128]{2,1,0:T(8,128)S(1)}, bf16[400,128]{1,0:T(8,128)(2,1)S(1)}) custom-call(bf16[32,32,128]{2,1,0:T(8,128)(2,1)S(1)} %copy-done.1, bf16[32,32,128]{2,1,0:T(8,128)(2,1)S(1)} %collective-permute-done.refs_1_, f32[32,128]{1,0:T(8,128)S(1)} %get-tuple-element.15.refs_2_, ...), custom_call_target="tpu_custom_call" | custom-call | tf_op jit(solution)/shard_map/first_gram/pallas_call | solution.py:385
  10.9 1.1 %collective-permute-start.2 = (bf16[400,128]{1,0:T(8,128)(2,1)S(1)}, bf16[400,128]{1,0:T(8,128)(2,1)S(1)}, u32[]{:S(2)}, u32[]{:S(2)}) collective-permute-start(bf16[400,128]{1,0:T(8,128)(2,1)S(1)} %get-tuple-element.21), channel_id=1, source_target_pairs={{0,2},{1,0},{2,4},{3,1},{4,6},{5,3},{6,8},{7,5},{8,10},{9,7},{10,1... | collective-permute-start | bytes 307208 | tf_op jit(solution)/shard_map/ppermute | solution.py:392
  12.0 0.0 collective-permute-done.3.inverse_ref
  12.0 1.4 %second_gram.1 = bf16[400,128]{1,0:T(8,128)(2,1)S(1)} custom-call(bf16[32,64,128]{2,1,0:T(8,128)(2,1)S(1)} %get-tuple-element.19.rows_ref, f32[2,32,128]{2,1,0:T(8,128)S(1)} %get-tuple-element.20.held_ref, f32[2,8,128]{2,1,0:T(8,128)S(1)} %collective-permute-done.3.inverse_ref), custom_call_target="tpu_custom_call" | custom-call | tf_op jit(solution)/shard_map/second_gram/pallas_call | solution.py:393
  13.4 0.1 collective-permute-start.4
  13.5 1.4 %upper_gram.1.upper_ref = f32[392,128]{1,0:T(8,128)S(1)} custom-call(bf16[32,64,128]{2,1,0:T(8,128)(2,1)S(1)} %get-tuple-element.19.rows_ref, f32[2,32,128]{2,1,0:T(8,128)S(1)} %get-tuple-element.20.held_ref, f32[2,8,128]{2,1,0:T(8,128)S(1)} %broadcast_in_dim.40.inverse_ref), custom_call_target="tpu_custom_call" | custom-call | tf_op jit(solution)/shard_map/upper_gram/pallas_call | solution.py:396
  14.9 0.0 collective-permute-done.2.first_ref
  14.9 1.4 %lower_gram.1.total_ref = f32[392,128]{1,0:T(8,128)S(1)} custom-call(f32[392,128]{1,0:T(8,128)S(1)} %upper_gram.1.upper_ref, bf16[32,64,128]{2,1,0:T(8,128)(2,1)S(1)} %get-tuple-element.19.rows_ref, f32[2,32,128]{2,1,0:T(8,128)S(1)} %get-tuple-element.20.held_ref, f32[2,8,128]{2,1,0:T(8,128)S(1)} %broadcast_in_dim.40.inverse_ref, ...), custom_call_target="tpu_custom_call" | custom-call | tf_op jit(solution)/shard_map/lower_gram/pallas_call | solution.py:397
  16.2 2.2 %collective-permute-done.4.second_ref = bf16[400,128]{1,0:T(8,128)(2,1)S(1)} collective-permute-done((bf16[400,128]{1,0:T(8,128)(2,1)S(1)}, bf16[400,128]{1,0:T(8,128)(2,1)S(1)}, u32[]{:S(2)}, u32[]{:S(2)}) %collective-permute-start.4) | collective-permute-done | bytes 102432 | tf_op jit(solution)/shard_map/ppermute | solution.py:394
  18.5 4.0 %finish.1 = bf16[1,64,32,128]{3,2,1,0:T(8,128)(2,1)} custom-call(f32[392,128]{1,0:T(8,128)S(1)} %lower_gram.1.total_ref, bf16[400,128]{1,0:T(8,128)(2,1)S(1)} %collective-permute-done.4.second_ref, bf16[32,64,128]{2,1,0:T(8,128)(2,1)S(1)} %get-tuple-element.22.lag_ref, f32[32,128]{1,0:T(8,128)S(1)} %get-tuple-element.18.refs_5_.mean_ref), custom_call_target="tpu_custom_call" | custom-call | tf_op jit(solution)/shard_map/finish/pallas_call | solution.py:398
  (2 shorter events, 0.0 us)
Async XLA Ops:
  0.0 1.9 %copy-start.4 = (s32[16]{0:T(128)S(1)}, s32[16]{0:T(128)}, u32[]{:S(2)}) copy-start(s32[16]{0:T(128)} %param.10) | copy-start | bytes 196
  0.0 8.9 %collective-permute-start = (bf16[32,32,128]{2,1,0:T(8,128)(2,1)}, bf16[32,32,128]{2,1,0:T(8,128)(2,1)S(1)}, u32[]{:S(2)}, u32[]{:S(2)}) collective-permute-start(bf16[32,32,128]{2,1,0:T(8,128)(2,1)} %refs_0_.1), channel_id=1, source_target_pairs={{1,0},{0,1},{3,2},{2,3},{5,4},{4,5},{7,6},{6,7},{9,8},{8,9},{11,10... | collective-permute-start | bytes 786440 | tf_op jit(solution)/shard_map/ppermute | solution.py:357
  1.9 0.9 %copy-start.3 = (s32[16,256]{1,0:T(8,128)S(1)}, s32[16,256]{1,0:T(8,128)}, u32[]{:S(2)}) copy-start(s32[16,256]{1,0:T(8,128)} %param.9) | copy-start | bytes 49156
  3.0 5.9 %collective-permute-start.1 = (f32[2,8,128]{2,1,0:T(8,128)S(1)}, f32[2,8,128]{2,1,0:T(8,128)S(1)}, u32[]{:S(2)}, u32[]{:S(2)}) collective-permute-start(f32[2,8,128]{2,1,0:T(8,128)S(1)} %broadcast_in_dim.40.inverse_ref), channel_id=1, source_target_pairs={{2,0},{0,1},{4,2},{1,3},{6,4},{3,5},{8,6},{5,7},{10,8},{7,9},{12,1... | collective-permute-start | bytes 24584 | tf_op jit(solution)/shard_map/ppermute | solution.py:368
  3.9 8.0 %collective-permute-start.3 = (f32[2,8,128]{2,1,0:T(8,128)S(1)}, f32[2,8,128]{2,1,0:T(8,128)S(1)}, u32[]{:S(2)}, u32[]{:S(2)}) collective-permute-start(f32[2,8,128]{2,1,0:T(8,128)S(1)} %broadcast_in_dim.40.inverse_ref), channel_id=1, source_target_pairs={{1,0},{3,1},{0,2},{5,3},{2,4},{7,5},{4,6},{9,7},{6,8},{11,9},{8,10... | collective-permute-start | bytes 24584 | tf_op jit(solution)/shard_map/ppermute | solution.py:368
  5.6 0.9 %copy-start = (bf16[32,32,128]{2,1,0:T(8,128)(2,1)S(1)}, bf16[32,32,128]{2,1,0:T(8,128)(2,1)}, u32[]{:S(2)}) copy-start(bf16[32,32,128]{2,1,0:T(8,128)(2,1)} %refs_0_.1) | copy-start | bytes 786436
  7.1 1.1 %copy-start.2 = (bf16[1,64,32,128]{3,2,1,0:T(8,128)(2,1)S(1)}, bf16[1,64,32,128]{3,2,1,0:T(8,128)(2,1)}, u32[]{:S(2)}) copy-start(bf16[1,64,32,128]{3,2,1,0:T(8,128)(2,1)} %param.7) | copy-start | bytes 1572868
  8.1 0.9 %copy-start.1 = (bf16[32,32,128]{2,1,0:T(8,128)(2,1)S(1)}, bf16[32,32,128]{2,1,0:T(8,128)(2,1)}, u32[]{:S(2)}) copy-start(bf16[32,32,128]{2,1,0:T(8,128)(2,1)} %refs_0_.1) | copy-start | bytes 786436
  10.9 4.0 %collective-permute-start.2 = (bf16[400,128]{1,0:T(8,128)(2,1)S(1)}, bf16[400,128]{1,0:T(8,128)(2,1)S(1)}, u32[]{:S(2)}, u32[]{:S(2)}) collective-permute-start(bf16[400,128]{1,0:T(8,128)(2,1)S(1)} %get-tuple-element.21), channel_id=1, source_target_pairs={{0,2},{1,0},{2,4},{3,1},{4,6},{5,3},{6,8},{7,5},{8,10},{9,7},{10,1... | collective-permute-start | bytes 307208 | tf_op jit(solution)/shard_map/ppermute | solution.py:392
  13.4 5.0 %collective-permute-start.4 = (bf16[400,128]{1,0:T(8,128)(2,1)S(1)}, bf16[400,128]{1,0:T(8,128)(2,1)S(1)}, u32[]{:S(2)}, u32[]{:S(2)}) collective-permute-start(bf16[400,128]{1,0:T(8,128)(2,1)S(1)} %second_gram.1), channel_id=1, source_target_pairs={{0,1},{1,3},{2,0},{3,5},{4,2},{5,7},{6,4},{7,9},{8,6},{9,11},{10,8... | collective-permute-start | bytes 307208 | tf_op jit(solution)/shard_map/ppermute | solution.py:394

commit v10 on v9

--- a/solution.py
+++ b/solution.py
@@ -64,7 +64,7 @@
     state = hist_ref[...].astype(f32)
     mean = jnp.sum(state, axis=0) / members
     mean_ref[...] = mean
-    flat_ref[...] = (state - mean[None]).reshape(members * tile_rows, cols)
+    flat_ref[: members * tile_rows, :] = (state - mean[None]).reshape(members * tile_rows, cols)
     for r in range(tile_rows):
         lag_ref[r] = flat_ref[pl.ds(r, members, stride=tile_rows), :].astype(bf16)
 
@@ -330,7 +330,7 @@
                 for q in range(1, quads):
                     chosen = jnp.where(patch // 4 == q, part[q * members : (q + 1) * members], chosen)
                 flat_ref[pl.ds(r + i, members, stride=tile_rows), :] = chosen + mean_ref[r + i : r + i + 1, :]
-    out_ref[...] = flat_ref[...].reshape(1, members, tile_rows, cols).astype(bf16)
+    out_ref[...] = flat_ref[: members * tile_rows, :].reshape(1, members, tile_rows, cols).astype(bf16)
 
 
 def shards(history, forecast, spot, alive, levels, precision, radius):
@@ -380,14 +380,14 @@
         "state",
         [vmem],
         [shape((tile_rows, members, cols), bf16), shape((tile_rows, cols), f32)],
-        [pltpu.VMEM((members * tile_rows, cols), f32)],
+        [pltpu.VMEM(((members + 1) * tile_rows, cols), f32)],
     )(history[0])
     rows, held, message = call(
         functools.partial(first_kernel, shares),
         "first_gram",
         [vmem] * (shares + 4),
         [shape((tile_rows, members, cols), bf16), shape((2, tile_rows, cols), f32), message_shape],
-        [pltpu.VMEM((members * tile_rows, cols), f32), total_scratch],
+        [pltpu.VMEM(((members + 1) * tile_rows, cols), f32), total_scratch],
     )(*parts, own_sum, fields, next_inverses[0], lag_mean)
     first = lax.ppermute(message, axes, rings[0])
     message = call(second_kernel, "second_gram", [vmem] * 3, message_shape, [total_scratch])(rows, held, next_inverses[1])
@@ -400,7 +400,7 @@
         "finish",
         [vmem] * 4,
         shape((1, members, tile_rows, cols), bf16),
-        [pltpu.VMEM((members * tile_rows, cols), f32)],
+        [pltpu.VMEM(((members + 1) * tile_rows, cols), f32)],
     )(own, second, lag_rows, lag_mean)
 
 

time: 22.7 us -> 22.7 us (level)
  the two profiles are of different devices: /device:TPU:3 before, /device:TPU:11 now
where the time goes in v10:
time: 22.7 us; the launch traced here: 22.4 us
  Pallas kernels  11.1 us (49%)
  starting transfers between devices  5.02 us (22%)
  local copies, waits for them, and re-layouts  2.37 us (10%)
  waiting for transfers between devices  2.24 us (10%)
  other arithmetic  1.57 us (7%)
    pallas_call x1, Pallas kernels, shards(): call(finish_kernel, 'finish', [vmem] * 4, shape((1, members, tile_rows, c...  3.95 us
    ppermute x2, starting transfers between devices, shards(): lax.ppermute(sent, axes, [(t, s) for s, t in pairs])  2.65 us
    ppermute x1, waiting for transfers between devices, shards(): second = lax.ppermute(message, axes, rings[1])  2.23 us
    unnamed x10, local copies, waits for them, and re-layouts  2.22 us
    pallas_call x1, Pallas kernels, shards(): call(functools.partial(first_kernel, shares), 'first_gram', [vmem] * (sha...  1.82 us
    pallas_call x1, Pallas kernels, shards(): call(second_kernel, 'second_gram', [vmem] * 3, message_shape, [total_scra...  1.44 us
    pallas_call x1, Pallas kernels, shards(): call(lower_kernel, 'lower_gram', [vmem] * 5, own_shape)  1.36 us
    pallas_call x1, Pallas kernels, shards(): call(upper_kernel, 'upper_gram', [vmem] * 3, own_shape)(rows, held, inverse)  1.36 us
  transfers between devices with their start and end apart: 5, of which 1 were waited for; matrix products, arithmetic and copies ran while one was open for 8% of the time, Pallas kernels for 32%

profile of v10, /device:TPU:11, one launch (start us, length us, event | category | flops | bytes accessed | tf_op | source)
XLA Modules:
  0.0 22.4 jit_solution(9410730481999578518)
XLA Ops:
  0.0 0.0 copy-start.4
  0.0 1.2 %collective-permute-start = (bf16[32,32,128]{2,1,0:T(8,128)(2,1)}, bf16[32,32,128]{2,1,0:T(8,128)(2,1)S(1)}, u32[]{:S(2)}, u32[]{:S(2)}) collective-permute-start(bf16[32,32,128]{2,1,0:T(8,128)(2,1)} %refs_0_.1), channel_id=1, source_target_pairs={{1,0},{0,1},{3,2},{2,3},{5,4},{4,5},{7,6},{6,7},{9,8},{8,9},{11,10... | collective-permute-start | bytes 786440 | tf_op jit(solution)/shard_map/ppermute | solution.py:357
  1.2 0.7 %multiply_divide_fusion = f32[16]{0:T(128)S(1)} fusion(s32[16]{0:T(128)} %param.13), kind=kLoop, calls=%fused_computation.5 | loop fusion | flops 48 | bytes 128 | tf_op jit(solution)/shard_map/div | solution.py:363
  1.9 0.0 copy-done.4
  1.9 0.0 copy-start.3
  1.9 0.8 %fusion.1 = (f32[16,256]{1,0:T(8,128)S(1)}, f32[16,256]{1,0:T(8,128)S(1)}) fusion(f32[16,256]{1,0:T(8,128)} %param.11, f32[16,256]{1,0:T(8,128)} %param.12, s32[16]{0:T(128)S(1)} %copy-done.4), kind=kLoop, calls=%fused_computation.6 | loop fusion | flops 12288 | bytes 65600 | tf_op jit(solution)/shard_map/mul | solution.py:361
  2.7 0.1 broadcast_in_dim.39
  2.8 0.0 copy-done.3
  2.8 0.1 select_select_fusion.table_ref
  2.9 0.1 broadcast_in_dim.40.inverse_ref
  3.0 1.0 %collective-permute-start.1 = (f32[2,8,128]{2,1,0:T(8,128)S(1)}, f32[2,8,128]{2,1,0:T(8,128)S(1)}, u32[]{:S(2)}, u32[]{:S(2)}) collective-permute-start(f32[2,8,128]{2,1,0:T(8,128)S(1)} %broadcast_in_dim.40.inverse_ref), channel_id=1, source_target_pairs={{2,0},{0,1},{4,2},{1,3},{6,4},{3,5},{8,6},{5,7},{10,8},{7,9},{12,1... | collective-permute-start | bytes 24584 | tf_op jit(solution)/shard_map/ppermute | solution.py:368
  3.9 1.7 %collective-permute-start.3 = (f32[2,8,128]{2,1,0:T(8,128)S(1)}, f32[2,8,128]{2,1,0:T(8,128)S(1)}, u32[]{:S(2)}, u32[]{:S(2)}) collective-permute-start(f32[2,8,128]{2,1,0:T(8,128)S(1)} %broadcast_in_dim.40.inverse_ref), channel_id=1, source_target_pairs={{1,0},{3,1},{0,2},{5,3},{2,4},{7,5},{4,6},{9,7},{6,8},{11,9},{8,10... | collective-permute-start | bytes 24584 | tf_op jit(solution)/shard_map/ppermute | solution.py:368
  5.6 0.0 copy-start
  5.6 0.9 %copy-done = bf16[32,32,128]{2,1,0:T(8,128)(2,1)S(1)} copy-done((bf16[32,32,128]{2,1,0:T(8,128)(2,1)S(1)}, bf16[32,32,128]{2,1,0:T(8,128)(2,1)}, u32[]{:S(2)}) %copy-start) | copy-done | bytes 262168
  6.6 0.5 %fields.1 = (f32[2,32,128]{2,1,0:T(8,128)S(1)}, f32[32,128]{1,0:T(8,128)S(1)}) custom-call(f32[3,16,256]{2,1,0:T(8,128)S(1)} %select_select_fusion.table_ref, bf16[32,32,128]{2,1,0:T(8,128)(2,1)S(1)} %copy-done), custom_call_target="tpu_custom_call" | custom-call | tf_op jit(solution)/shard_map/fields/pallas_call | solution.py:369
  7.1 0.0 copy-start.2
  7.1 1.1 %copy-done.2 = bf16[1,64,32,128]{3,2,1,0:T(8,128)(2,1)S(1)} copy-done((bf16[1,64,32,128]{3,2,1,0:T(8,128)(2,1)S(1)}, bf16[1,64,32,128]{3,2,1,0:T(8,128)(2,1)}, u32[]{:S(2)}) %copy-start.2) | copy-done | bytes 524312
  8.1 0.0 copy-start.1
  8.1 0.7 %state.1 = (bf16[32,64,128]{2,1,0:T(8,128)(2,1)S(1)}, f32[32,128]{1,0:T(8,128)S(1)}) custom-call(bf16[64,32,128]{2,1,0:T(8,128)(2,1)S(1)} %bitcast.1), custom_call_target="tpu_custom_call" | custom-call | tf_op jit(solution)/shard_map/state/pallas_call | solution.py:378
  8.9 0.0 collective-permute-done.1.refs_4_
  8.9 0.0 collective-permute-done.refs_1_
  8.9 0.2 copy-done.1
  9.1 1.8 %first_gram.1 = (bf16[32,64,128]{2,1,0:T(8,128)(2,1)S(1)}, f32[2,32,128]{2,1,0:T(8,128)S(1)}, bf16[400,128]{1,0:T(8,128)(2,1)S(1)}) custom-call(bf16[32,32,128]{2,1,0:T(8,128)(2,1)S(1)} %copy-done.1, bf16[32,32,128]{2,1,0:T(8,128)(2,1)S(1)} %collective-permute-done.refs_1_, f32[32,128]{1,0:T(8,128)S(1)} %get-tuple-element.15.refs_2_, ...), custom_call_target="tpu_custom_call" | custom-call | tf_op jit(solution)/shard_map/first_gram/pallas_call | solution.py:385
  10.9 1.1 %collective-permute-start.2 = (bf16[400,128]{1,0:T(8,128)(2,1)S(1)}, bf16[400,128]{1,0:T(8,128)(2,1)S(1)}, u32[]{:S(2)}, u32[]{:S(2)}) collective-permute-start(bf16[400,128]{1,0:T(8,128)(2,1)S(1)} %get-tuple-element.21), channel_id=1, source_target_pairs={{0,2},{1,0},{2,4},{3,1},{4,6},{5,3},{6,8},{7,5},{8,10},{9,7},{10,1... | collective-permute-start | bytes 307208 | tf_op jit(solution)/shard_map/ppermute | solution.py:392
  12.0 0.0 collective-permute-done.3.inverse_ref
  12.0 1.4 %second_gram.1 = bf16[400,128]{1,0:T(8,128)(2,1)S(1)} custom-call(bf16[32,64,128]{2,1,0:T(8,128)(2,1)S(1)} %get-tuple-element.19.rows_ref, f32[2,32,128]{2,1,0:T(8,128)S(1)} %get-tuple-element.20.held_ref, f32[2,8,128]{2,1,0:T(8,128)S(1)} %collective-permute-done.3.inverse_ref), custom_call_target="tpu_custom_call" | custom-call | tf_op jit(solution)/shard_map/second_gram/pallas_call | solution.py:393
  13.4 0.1 collective-permute-start.4
  13.5 1.4 %upper_gram.1.upper_ref = f32[392,128]{1,0:T(8,128)S(1)} custom-call(bf16[32,64,128]{2,1,0:T(8,128)(2,1)S(1)} %get-tuple-element.19.rows_ref, f32[2,32,128]{2,1,0:T(8,128)S(1)} %get-tuple-element.20.held_ref, f32[2,8,128]{2,1,0:T(8,128)S(1)} %broadcast_in_dim.40.inverse_ref), custom_call_target="tpu_custom_call" | custom-call | tf_op jit(solution)/shard_map/upper_gram/pallas_call | solution.py:396
  14.9 0.0 collective-permute-done.2.first_ref
  14.9 1.4 %lower_gram.1.total_ref = f32[392,128]{1,0:T(8,128)S(1)} custom-call(f32[392,128]{1,0:T(8,128)S(1)} %upper_gram.1.upper_ref, bf16[32,64,128]{2,1,0:T(8,128)(2,1)S(1)} %get-tuple-element.19.rows_ref, f32[2,32,128]{2,1,0:T(8,128)S(1)} %get-tuple-element.20.held_ref, f32[2,8,128]{2,1,0:T(8,128)S(1)} %broadcast_in_dim.40.inverse_ref, ...), custom_call_target="tpu_custom_call" | custom-call | tf_op jit(solution)/shard_map/lower_gram/pallas_call | solution.py:397
  16.2 2.2 %collective-permute-done.4.second_ref = bf16[400,128]{1,0:T(8,128)(2,1)S(1)} collective-permute-done((bf16[400,128]{1,0:T(8,128)(2,1)S(1)}, bf16[400,128]{1,0:T(8,128)(2,1)S(1)}, u32[]{:S(2)}, u32[]{:S(2)}) %collective-permute-start.4) | collective-permute-done | bytes 102432 | tf_op jit(solution)/shard_map/ppermute | solution.py:394
  18.5 4.0 %finish.1 = bf16[1,64,32,128]{3,2,1,0:T(8,128)(2,1)} custom-call(f32[392,128]{1,0:T(8,128)S(1)} %lower_gram.1.total_ref, bf16[400,128]{1,0:T(8,128)(2,1)S(1)} %collective-permute-done.4.second_ref, bf16[32,64,128]{2,1,0:T(8,128)(2,1)S(1)} %get-tuple-element.22.lag_ref, f32[32,128]{1,0:T(8,128)S(1)} %get-tuple-element.18.refs_5_.mean_ref), custom_call_target="tpu_custom_call" | custom-call | tf_op jit(solution)/shard_map/finish/pallas_call | solution.py:398
  (2 shorter events, 0.0 us)
Async XLA Ops:
  0.0 1.9 %copy-start.4 = (s32[16]{0:T(128)S(1)}, s32[16]{0:T(128)}, u32[]{:S(2)}) copy-start(s32[16]{0:T(128)} %param.10) | copy-start | bytes 196
  0.0 8.9 %collective-permute-start = (bf16[32,32,128]{2,1,0:T(8,128)(2,1)}, bf16[32,32,128]{2,1,0:T(8,128)(2,1)S(1)}, u32[]{:S(2)}, u32[]{:S(2)}) collective-permute-start(bf16[32,32,128]{2,1,0:T(8,128)(2,1)} %refs_0_.1), channel_id=1, source_target_pairs={{1,0},{0,1},{3,2},{2,3},{5,4},{4,5},{7,6},{6,7},{9,8},{8,9},{11,10... | collective-permute-start | bytes 786440 | tf_op jit(solution)/shard_map/ppermute | solution.py:357
  1.9 0.9 %copy-start.3 = (s32[16,256]{1,0:T(8,128)S(1)}, s32[16,256]{1,0:T(8,128)}, u32[]{:S(2)}) copy-start(s32[16,256]{1,0:T(8,128)} %param.9) | copy-start | bytes 49156
  3.0 5.9 %collective-permute-start.1 = (f32[2,8,128]{2,1,0:T(8,128)S(1)}, f32[2,8,128]{2,1,0:T(8,128)S(1)}, u32[]{:S(2)}, u32[]{:S(2)}) collective-permute-start(f32[2,8,128]{2,1,0:T(8,128)S(1)} %broadcast_in_dim.40.inverse_ref), channel_id=1, source_target_pairs={{2,0},{0,1},{4,2},{1,3},{6,4},{3,5},{8,6},{5,7},{10,8},{7,9},{12,1... | collective-permute-start | bytes 24584 | tf_op jit(solution)/shard_map/ppermute | solution.py:368
  3.9 8.0 %collective-permute-start.3 = (f32[2,8,128]{2,1,0:T(8,128)S(1)}, f32[2,8,128]{2,1,0:T(8,128)S(1)}, u32[]{:S(2)}, u32[]{:S(2)}) collective-permute-start(f32[2,8,128]{2,1,0:T(8,128)S(1)} %broadcast_in_dim.40.inverse_ref), channel_id=1, source_target_pairs={{1,0},{3,1},{0,2},{5,3},{2,4},{7,5},{4,6},{9,7},{6,8},{11,9},{8,10... | collective-permute-start | bytes 24584 | tf_op jit(solution)/shard_map/ppermute | solution.py:368
  5.6 0.9 %copy-start = (bf16[32,32,128]{2,1,0:T(8,128)(2,1)S(1)}, bf16[32,32,128]{2,1,0:T(8,128)(2,1)}, u32[]{:S(2)}) copy-start(bf16[32,32,128]{2,1,0:T(8,128)(2,1)} %refs_0_.1) | copy-start | bytes 786436
  7.1 1.1 %copy-start.2 = (bf16[1,64,32,128]{3,2,1,0:T(8,128)(2,1)S(1)}, bf16[1,64,32,128]{3,2,1,0:T(8,128)(2,1)}, u32[]{:S(2)}) copy-start(bf16[1,64,32,128]{3,2,1,0:T(8,128)(2,1)} %param.7) | copy-start | bytes 1572868
  8.1 0.9 %copy-start.1 = (bf16[32,32,128]{2,1,0:T(8,128)(2,1)S(1)}, bf16[32,32,128]{2,1,0:T(8,128)(2,1)}, u32[]{:S(2)}) copy-start(bf16[32,32,128]{2,1,0:T(8,128)(2,1)} %refs_0_.1) | copy-start | bytes 786436
  10.9 4.0 %collective-permute-start.2 = (bf16[400,128]{1,0:T(8,128)(2,1)S(1)}, bf16[400,128]{1,0:T(8,128)(2,1)S(1)}, u32[]{:S(2)}, u32[]{:S(2)}) collective-permute-start(bf16[400,128]{1,0:T(8,128)(2,1)S(1)} %get-tuple-element.21), channel_id=1, source_target_pairs={{0,2},{1,0},{2,4},{3,1},{4,6},{5,3},{6,8},{7,5},{8,10},{9,7},{10,1... | collective-permute-start | bytes 307208 | tf_op jit(solution)/shard_map/ppermute | solution.py:392
  13.4 5.0 %collective-permute-start.4 = (bf16[400,128]{1,0:T(8,128)(2,1)S(1)}, bf16[400,128]{1,0:T(8,128)(2,1)S(1)}, u32[]{:S(2)}, u32[]{:S(2)}) collective-permute-start(bf16[400,128]{1,0:T(8,128)(2,1)S(1)} %second_gram.1), channel_id=1, source_target_pairs={{0,1},{1,3},{2,0},{3,5},{4,2},{5,7},{6,4},{7,9},{8,6},{9,11},{10,8... | collective-permute-start | bytes 307208 | tf_op jit(solution)/shard_map/ppermute | solution.py:394

commit v11 on v10

--- a/solution.py
+++ b/solution.py
@@ -267,7 +267,16 @@
         ]
 
     def products(lefts, factors):
-        stacks = [jnp.concatenate([half for halves in left for half in halves], 0) for left in lefts]
+        stacks = [
+            jnp.concatenate(
+                [jnp.concatenate([half.astype(f32) for half in left[0]], 0).astype(bf16)]
+                + [half for halves in left[1:] for half in halves]
+                if left[0][0].shape[0] < PATCH
+                else [half for halves in left for half in halves],
+                0,
+            )
+            for left in lefts
+        ]
         boths = [mm(stack, factor) for stack, factor in zip(stacks, factors)]
         results = []
         for left, both in zip(lefts, boths):
@@ -290,7 +299,7 @@
     bounds = degree + jnp.sqrt(jnp.where(at_left, norm_left, norm_right))
     inverses = 1.0 / bounds
     spreads = jnp.sqrt(degree * inverses)
-    sides = [jnp.broadcast_to(total[grams_end + p : grams_end + p + 1], (PATCH, cols)) for p in pairs]
+    sides = [jnp.broadcast_to(total[grams_end + p : grams_end + p + 1], (PATCH // 2, cols)) for p in pairs]
     iterates = [(grams[p] + degree * identity) * inverses[p : p + 1] for p in pairs]
     roots = [None for _ in pairs]
     for step in range(NS_STEPS):

time: 22.7 us -> 22.6 us (level)
  the two profiles are of different devices: /device:TPU:11 before, /device:TPU:3 now
where the time goes in v11:
time: 22.6 us; the launch traced here: 22.4 us
  Pallas kernels  11.1 us (49%)
  starting transfers between devices  5.02 us (22%)
  local copies, waits for them, and re-layouts  2.37 us (10%)
  waiting for transfers between devices  2.24 us (10%)
  other arithmetic  1.57 us (7%)
    pallas_call x1, Pallas kernels, shards(): call(finish_kernel, 'finish', [vmem] * 4, shape((1, members, tile_rows, c...  3.88 us
    ppermute x2, starting transfers between devices, shards(): lax.ppermute(sent, axes, [(t, s) for s, t in pairs])  2.65 us
    ppermute x1, waiting for transfers between devices, shards(): second = lax.ppermute(message, axes, rings[1])  2.23 us
    unnamed x10, local copies, waits for them, and re-layouts  2.22 us
    pallas_call x1, Pallas kernels, shards(): call(functools.partial(first_kernel, shares), 'first_gram', [vmem] * (sha...  1.82 us
    pallas_call x1, Pallas kernels, shards(): call(second_kernel, 'second_gram', [vmem] * 3, message_shape, [total_scra...  1.45 us
    pallas_call x1, Pallas kernels, shards(): call(lower_kernel, 'lower_gram', [vmem] * 5, own_shape)  1.36 us
    pallas_call x1, Pallas kernels, shards(): call(upper_kernel, 'upper_gram', [vmem] * 3, own_shape)(rows, held, inverse)  1.36 us
  transfers between devices with their start and end apart: 5, of which 1 were waited for; matrix products, arithmetic and copies ran while one was open for 8% of the time, Pallas kernels for 32%

profile of v11, /device:TPU:3, one launch (start us, length us, event | category | flops | bytes accessed | tf_op | source)
XLA Modules:
  0.0 22.4 jit_solution(8243293918655383509)
XLA Ops:
  0.0 0.0 copy-start.4
  0.0 1.2 %collective-permute-start = (bf16[32,32,128]{2,1,0:T(8,128)(2,1)}, bf16[32,32,128]{2,1,0:T(8,128)(2,1)S(1)}, u32[]{:S(2)}, u32[]{:S(2)}) collective-permute-start(bf16[32,32,128]{2,1,0:T(8,128)(2,1)} %refs_0_.1), channel_id=1, source_target_pairs={{1,0},{0,1},{3,2},{2,3},{5,4},{4,5},{7,6},{6,7},{9,8},{8,9},{11,10... | collective-permute-start | bytes 786440 | tf_op jit(solution)/shard_map/ppermute | solution.py:366
  1.2 0.7 %multiply_divide_fusion = f32[16]{0:T(128)S(1)} fusion(s32[16]{0:T(128)} %param.13), kind=kLoop, calls=%fused_computation.5 | loop fusion | flops 48 | bytes 128 | tf_op jit(solution)/shard_map/div | solution.py:372
  1.9 0.0 copy-done.4
  1.9 0.0 copy-start.3
  1.9 0.8 %fusion.1 = (f32[16,256]{1,0:T(8,128)S(1)}, f32[16,256]{1,0:T(8,128)S(1)}) fusion(f32[16,256]{1,0:T(8,128)} %param.11, f32[16,256]{1,0:T(8,128)} %param.12, s32[16]{0:T(128)S(1)} %copy-done.4), kind=kLoop, calls=%fused_computation.6 | loop fusion | flops 12288 | bytes 65600 | tf_op jit(solution)/shard_map/mul | solution.py:370
  2.7 0.1 broadcast_in_dim.39
  2.8 0.0 copy-done.3
  2.8 0.1 select_select_fusion.table_ref
  2.9 0.1 broadcast_in_dim.40.inverse_ref
  3.0 1.0 %collective-permute-start.1 = (f32[2,8,128]{2,1,0:T(8,128)S(1)}, f32[2,8,128]{2,1,0:T(8,128)S(1)}, u32[]{:S(2)}, u32[]{:S(2)}) collective-permute-start(f32[2,8,128]{2,1,0:T(8,128)S(1)} %broadcast_in_dim.40.inverse_ref), channel_id=1, source_target_pairs={{2,0},{0,1},{4,2},{1,3},{6,4},{3,5},{8,6},{5,7},{10,8},{7,9},{12,1... | collective-permute-start | bytes 24584 | tf_op jit(solution)/shard_map/ppermute | solution.py:377
  3.9 1.7 %collective-permute-start.3 = (f32[2,8,128]{2,1,0:T(8,128)S(1)}, f32[2,8,128]{2,1,0:T(8,128)S(1)}, u32[]{:S(2)}, u32[]{:S(2)}) collective-permute-start(f32[2,8,128]{2,1,0:T(8,128)S(1)} %broadcast_in_dim.40.inverse_ref), channel_id=1, source_target_pairs={{1,0},{3,1},{0,2},{5,3},{2,4},{7,5},{4,6},{9,7},{6,8},{11,9},{8,10... | collective-permute-start | bytes 24584 | tf_op jit(solution)/shard_map/ppermute | solution.py:377
  5.6 0.0 copy-start
  5.6 0.9 %copy-done = bf16[32,32,128]{2,1,0:T(8,128)(2,1)S(1)} copy-done((bf16[32,32,128]{2,1,0:T(8,128)(2,1)S(1)}, bf16[32,32,128]{2,1,0:T(8,128)(2,1)}, u32[]{:S(2)}) %copy-start) | copy-done | bytes 262168
  6.6 0.5 %fields.1 = (f32[2,32,128]{2,1,0:T(8,128)S(1)}, f32[32,128]{1,0:T(8,128)S(1)}) custom-call(f32[3,16,256]{2,1,0:T(8,128)S(1)} %select_select_fusion.table_ref, bf16[32,32,128]{2,1,0:T(8,128)(2,1)S(1)} %copy-done), custom_call_target="tpu_custom_call" | custom-call | tf_op jit(solution)/shard_map/fields/pallas_call | solution.py:378
  7.1 0.0 copy-start.2
  7.1 1.1 %copy-done.2 = bf16[1,64,32,128]{3,2,1,0:T(8,128)(2,1)S(1)} copy-done((bf16[1,64,32,128]{3,2,1,0:T(8,128)(2,1)S(1)}, bf16[1,64,32,128]{3,2,1,0:T(8,128)(2,1)}, u32[]{:S(2)}) %copy-start.2) | copy-done | bytes 524312
  8.1 0.0 copy-start.1
  8.1 0.7 %state.1 = (bf16[32,64,128]{2,1,0:T(8,128)(2,1)S(1)}, f32[32,128]{1,0:T(8,128)S(1)}) custom-call(bf16[64,32,128]{2,1,0:T(8,128)(2,1)S(1)} %bitcast.1), custom_call_target="tpu_custom_call" | custom-call | tf_op jit(solution)/shard_map/state/pallas_call | solution.py:387
  8.9 0.0 collective-permute-done.1.refs_4_
  8.9 0.0 collective-permute-done.refs_1_
  8.9 0.2 copy-done.1
  9.1 1.8 %first_gram.1 = (bf16[32,64,128]{2,1,0:T(8,128)(2,1)S(1)}, f32[2,32,128]{2,1,0:T(8,128)S(1)}, bf16[400,128]{1,0:T(8,128)(2,1)S(1)}) custom-call(bf16[32,32,128]{2,1,0:T(8,128)(2,1)S(1)} %copy-done.1, bf16[32,32,128]{2,1,0:T(8,128)(2,1)S(1)} %collective-permute-done.refs_1_, f32[32,128]{1,0:T(8,128)S(1)} %get-tuple-element.15.refs_2_, ...), custom_call_target="tpu_custom_call" | custom-call | tf_op jit(solution)/shard_map/first_gram/pallas_call | solution.py:394
  10.9 1.1 %collective-permute-start.2 = (bf16[400,128]{1,0:T(8,128)(2,1)S(1)}, bf16[400,128]{1,0:T(8,128)(2,1)S(1)}, u32[]{:S(2)}, u32[]{:S(2)}) collective-permute-start(bf16[400,128]{1,0:T(8,128)(2,1)S(1)} %get-tuple-element.21), channel_id=1, source_target_pairs={{0,2},{1,0},{2,4},{3,1},{4,6},{5,3},{6,8},{7,5},{8,10},{9,7},{10,1... | collective-permute-start | bytes 307208 | tf_op jit(solution)/shard_map/ppermute | solution.py:401
  12.0 0.0 collective-permute-done.3.inverse_ref
  12.0 1.4 %second_gram.1 = bf16[400,128]{1,0:T(8,128)(2,1)S(1)} custom-call(bf16[32,64,128]{2,1,0:T(8,128)(2,1)S(1)} %get-tuple-element.19.rows_ref, f32[2,32,128]{2,1,0:T(8,128)S(1)} %get-tuple-element.20.held_ref, f32[2,8,128]{2,1,0:T(8,128)S(1)} %collective-permute-done.3.inverse_ref), custom_call_target="tpu_custom_call" | custom-call | tf_op jit(solution)/shard_map/second_gram/pallas_call | solution.py:402
  13.4 0.1 collective-permute-start.4
  13.5 1.4 %upper_gram.1.upper_ref = f32[392,128]{1,0:T(8,128)S(1)} custom-call(bf16[32,64,128]{2,1,0:T(8,128)(2,1)S(1)} %get-tuple-element.19.rows_ref, f32[2,32,128]{2,1,0:T(8,128)S(1)} %get-tuple-element.20.held_ref, f32[2,8,128]{2,1,0:T(8,128)S(1)} %broadcast_in_dim.40.inverse_ref), custom_call_target="tpu_custom_call" | custom-call | tf_op jit(solution)/shard_map/upper_gram/pallas_call | solution.py:405
  14.9 0.0 collective-permute-done.2.first_ref
  14.9 1.4 %lower_gram.1.total_ref = f32[392,128]{1,0:T(8,128)S(1)} custom-call(f32[392,128]{1,0:T(8,128)S(1)} %upper_gram.1.upper_ref, bf16[32,64,128]{2,1,0:T(8,128)(2,1)S(1)} %get-tuple-element.19.rows_ref, f32[2,32,128]{2,1,0:T(8,128)S(1)} %get-tuple-element.20.held_ref, f32[2,8,128]{2,1,0:T(8,128)S(1)} %broadcast_in_dim.40.inverse_ref, ...), custom_call_target="tpu_custom_call" | custom-call | tf_op jit(solution)/shard_map/lower_gram/pallas_call | solution.py:406
  16.2 2.2 %collective-permute-done.4.second_ref = bf16[400,128]{1,0:T(8,128)(2,1)S(1)} collective-permute-done((bf16[400,128]{1,0:T(8,128)(2,1)S(1)}, bf16[400,128]{1,0:T(8,128)(2,1)S(1)}, u32[]{:S(2)}, u32[]{:S(2)}) %collective-permute-start.4) | collective-permute-done | bytes 102432 | tf_op jit(solution)/shard_map/ppermute | solution.py:403
  18.5 3.9 %finish.1 = bf16[1,64,32,128]{3,2,1,0:T(8,128)(2,1)} custom-call(f32[392,128]{1,0:T(8,128)S(1)} %lower_gram.1.total_ref, bf16[400,128]{1,0:T(8,128)(2,1)S(1)} %collective-permute-done.4.second_ref, bf16[32,64,128]{2,1,0:T(8,128)(2,1)S(1)} %get-tuple-element.22.lag_ref, f32[32,128]{1,0:T(8,128)S(1)} %get-tuple-element.18.refs_5_.mean_ref), custom_call_target="tpu_custom_call" | custom-call | tf_op jit(solution)/shard_map/finish/pallas_call | solution.py:407
  (2 shorter events, 0.0 us)
Async XLA Ops:
  0.0 1.9 %copy-start.4 = (s32[16]{0:T(128)S(1)}, s32[16]{0:T(128)}, u32[]{:S(2)}) copy-start(s32[16]{0:T(128)} %param.10) | copy-start | bytes 196
  0.0 8.9 %collective-permute-start = (bf16[32,32,128]{2,1,0:T(8,128)(2,1)}, bf16[32,32,128]{2,1,0:T(8,128)(2,1)S(1)}, u32[]{:S(2)}, u32[]{:S(2)}) collective-permute-start(bf16[32,32,128]{2,1,0:T(8,128)(2,1)} %refs_0_.1), channel_id=1, source_target_pairs={{1,0},{0,1},{3,2},{2,3},{5,4},{4,5},{7,6},{6,7},{9,8},{8,9},{11,10... | collective-permute-start | bytes 786440 | tf_op jit(solution)/shard_map/ppermute | solution.py:366
  1.9 0.9 %copy-start.3 = (s32[16,256]{1,0:T(8,128)S(1)}, s32[16,256]{1,0:T(8,128)}, u32[]{:S(2)}) copy-start(s32[16,256]{1,0:T(8,128)} %param.9) | copy-start | bytes 49156
  3.0 5.9 %collective-permute-start.1 = (f32[2,8,128]{2,1,0:T(8,128)S(1)}, f32[2,8,128]{2,1,0:T(8,128)S(1)}, u32[]{:S(2)}, u32[]{:S(2)}) collective-permute-start(f32[2,8,128]{2,1,0:T(8,128)S(1)} %broadcast_in_dim.40.inverse_ref), channel_id=1, source_target_pairs={{2,0},{0,1},{4,2},{1,3},{6,4},{3,5},{8,6},{5,7},{10,8},{7,9},{12,1... | collective-permute-start | bytes 24584 | tf_op jit(solution)/shard_map/ppermute | solution.py:377
  3.9 8.0 %collective-permute-start.3 = (f32[2,8,128]{2,1,0:T(8,128)S(1)}, f32[2,8,128]{2,1,0:T(8,128)S(1)}, u32[]{:S(2)}, u32[]{:S(2)}) collective-permute-start(f32[2,8,128]{2,1,0:T(8,128)S(1)} %broadcast_in_dim.40.inverse_ref), channel_id=1, source_target_pairs={{1,0},{3,1},{0,2},{5,3},{2,4},{7,5},{4,6},{9,7},{6,8},{11,9},{8,10... | collective-permute-start | bytes 24584 | tf_op jit(solution)/shard_map/ppermute | solution.py:377
  5.6 0.9 %copy-start = (bf16[32,32,128]{2,1,0:T(8,128)(2,1)S(1)}, bf16[32,32,128]{2,1,0:T(8,128)(2,1)}, u32[]{:S(2)}) copy-start(bf16[32,32,128]{2,1,0:T(8,128)(2,1)} %refs_0_.1) | copy-start | bytes 786436
  7.1 1.1 %copy-start.2 = (bf16[1,64,32,128]{3,2,1,0:T(8,128)(2,1)S(1)}, bf16[1,64,32,128]{3,2,1,0:T(8,128)(2,1)}, u32[]{:S(2)}) copy-start(bf16[1,64,32,128]{3,2,1,0:T(8,128)(2,1)} %param.7) | copy-start | bytes 1572868
  8.1 0.9 %copy-start.1 = (bf16[32,32,128]{2,1,0:T(8,128)(2,1)S(1)}, bf16[32,32,128]{2,1,0:T(8,128)(2,1)}, u32[]{:S(2)}) copy-start(bf16[32,32,128]{2,1,0:T(8,128)(2,1)} %refs_0_.1) | copy-start | bytes 786436
  10.9 4.0 %collective-permute-start.2 = (bf16[400,128]{1,0:T(8,128)(2,1)S(1)}, bf16[400,128]{1,0:T(8,128)(2,1)S(1)}, u32[]{:S(2)}, u32[]{:S(2)}) collective-permute-start(bf16[400,128]{1,0:T(8,128)(2,1)S(1)} %get-tuple-element.21), channel_id=1, source_target_pairs={{0,2},{1,0},{2,4},{3,1},{4,6},{5,3},{6,8},{7,5},{8,10},{9,7},{10,1... | collective-permute-start | bytes 307208 | tf_op jit(solution)/shard_map/ppermute | solution.py:401
  13.4 5.0 %collective-permute-start.4 = (bf16[400,128]{1,0:T(8,128)(2,1)S(1)}, bf16[400,128]{1,0:T(8,128)(2,1)S(1)}, u32[]{:S(2)}, u32[]{:S(2)}) collective-permute-start(bf16[400,128]{1,0:T(8,128)(2,1)S(1)} %second_gram.1), channel_id=1, source_target_pairs={{0,1},{1,3},{2,0},{3,5},{4,2},{5,7},{6,4},{7,9},{8,6},{9,11},{10,8... | collective-permute-start | bytes 307208 | tf_op jit(solution)/shard_map/ppermute | solution.py:403
